TPU v7x, 32 devices: a whole 2x2x4 slice. The times are simulated.
32 devices in a mesh: groups: 2 (over x), depth: 16 (over z, y, core).
Axes of the slice: x: 2, y: 2, z: 4, core: 2. Of those that a mesh axis runs over, the one named last changes fastest.
Arguments:
- fields: float32 [32, 2, 2, 512, 256], P(('groups', 'depth')), parts along dimension 0, may hold values from -6 to 6
- vel_tiles: float32 [64, 128, 128], P(('groups', 'depth')), parts along dimension 0, may hold values from 0.5 to 2
- tile_ids: int32 [32, 2, 4, 2], P(('groups', 'depth')), parts along dimension 0, may hold values from 0 to 31
- orders: int32 [32, 2], P(('groups', 'depth')), parts along dimension 0, may hold values from 1 to 3
- term_weights: float32 [3], replicated, may hold values from 0.05 to 0.12
- phase_rates: float32 [4], replicated, may hold values from 1 to 4
- owners: int32 [32, 16], P(('groups', 'depth')), parts along dimension 0, may hold values from 0 to 15, as said below
- image_slots: int32 [32, 16], P(('groups', 'depth')), parts along dimension 0, may hold values from 0 to 7
Outputs:
- image_volume: float32 [256, 128, 128], P(('groups', 'depth')), parts along dimension 0
- wavefields_out: float32 [32, 2, 2, 512, 256], P(('groups', 'depth')), parts along dimension 0
There are 2 independent parts, one for each index of `groups`. A program takes and returns all parts, laid end to end along the dimension named above; an argument that names none is the same for every part. Nothing has to cross between parts.
Inputs may be any that keep to these rules, and one draw needn't show every extreme that they name: `owners`: of the 16 tiles of one slab, at most 2 have the same owner, and some owner gets exactly 2 of them.
All inputs are finite; a program needn't handle non-finite values.
Results may differ from a plain program's by a relative error of at most 0.0003.
Values sent between devices are 32-bit elements; how exact they have to be, the bound alone decides.
No kernel may reach another device: no remote copies, remote signals or barrier semaphores. Data moves between devices by JAX's collectives and lax.ppermute only.
A program may use at most 64 MiB of HBM per device.

v0:
```python
from functools import partial

import jax
import jax.numpy as jnp
from jax import lax
from jax.sharding import PartitionSpec as P

TICKS = 2
CAP = 2
IMG_SLOTS = 8


def from_behind(shard, axis, by):
    peers = lax.axis_size(axis)
    pairs = [(i, i + by) for i in range(peers) if 0 <= i + by < peers]
    return lax.ppermute(shard, axis, pairs)


def mcclellan(fields_in):
    padded = jnp.pad(fields_in, ((0, 0), (1, 1), (1, 1)))
    beside = padded[:, 2:, 1:-1] + padded[:, :-2, 1:-1] + padded[:, 1:-1, 2:] + padded[:, 1:-1, :-2]
    corner = padded[:, 2:, 2:] + padded[:, :-2, :-2] + padded[:, 2:, :-2] + padded[:, :-2, 2:]
    return -0.5 * fields_in + 0.25 * beside + 0.125 * corner


def rotate_add(result, series_term, real_part, imag_part, pair_signs):
    pieces_out = []
    for pair_index, pair_sign in enumerate(pair_signs):
        real_in = series_term[2 * pair_index]
        imag_in = series_term[2 * pair_index + 1]
        pieces_out.append(
            result[2 * pair_index] + real_part * real_in - pair_sign * imag_part * imag_in
        )
        pieces_out.append(
            result[2 * pair_index + 1] + real_part * imag_in + pair_sign * imag_part * real_in
        )
    return jnp.stack(pieces_out)


def advance(wave_state, slowness_now, highest, weights, phase_rates, pair_signs):
    result = jnp.zeros_like(wave_state)
    previous = wave_state
    current = wave_state
    for degree in range(highest + 1):
        if degree == 0:
            series_term = wave_state
        elif degree == 1:
            series_term = mcclellan(wave_state)
        else:
            series_term = 2.0 * mcclellan(current) - previous
        if degree >= 1:
            previous, current = (current, series_term)
        angle_now = phase_rates[degree] * slowness_now
        real_part = weights[degree] * jnp.cos(angle_now)
        imag_part = weights[degree] * jnp.sin(angle_now)
        result = rotate_add(result, series_term, real_part, imag_part, pair_signs)
    return result


def stepped(wave_state, slowness_now, order_now, weights, phase_rates, pair_signs):
    branches = [
        partial(
            advance,
            highest=level_top,
            weights=weights,
            phase_rates=phase_rates,
            pair_signs=pair_signs,
        )
        for level_top in range(1, phase_rates.shape[0])
    ]
    return lax.switch(order_now - 1, branches, wave_state, slowness_now)


def local(fields, vel_tiles, tile_ids, orders, term_weights, phase_rates, owners, image_slots):
    cells_x = fields.shape[3]
    cells_y = fields.shape[4]
    tile_size = vel_tiles.shape[1]
    depth_steps = tile_ids.shape[1]
    tiles_x = tile_ids.shape[2]
    tiles_y = tile_ids.shape[3]
    library = lax.all_gather(vel_tiles, "depth", axis=0, tiled=True)
    picked = library[tile_ids[0]]
    slowness = picked.transpose(0, 1, 3, 2, 4).reshape(depth_steps, cells_x, cells_y)
    weights = jnp.concatenate([(1.0 - jnp.sum(term_weights))[None], term_weights])
    wave_state = fields[0].reshape(4, cells_x, cells_y)
    image_sum = [jnp.zeros((cells_x, cells_y), jnp.float32) for step_index in range(depth_steps)]
    source = wave_state[:2]
    receiver = wave_state[2:]
    for tick_index in range(TICKS):
        source_steps = []
        for step_index in range(depth_steps):
            source = stepped(
                source, slowness[step_index], orders[0, step_index], weights, phase_rates, (1.0,)
            )
            source_steps.append(source)
        if tick_index + 1 < TICKS:
            source_moved = from_behind(source, "depth", 1)
        for step_index in range(depth_steps):
            receiver = stepped(
                receiver, slowness[step_index], orders[0, step_index], weights, phase_rates, (-1.0,)
            )
            product = (
                source_steps[step_index][0] * receiver[0]
                + source_steps[step_index][1] * receiver[1]
            )
            image_sum[step_index] = image_sum[step_index] + product
        if tick_index + 1 < TICKS:
            receiver = from_behind(receiver, "depth", 1)
            source = source_moved
    wave_state = jnp.concatenate([source, receiver], 0)
    stacked = jnp.stack(image_sum)
    tile_rows = stacked.reshape(depth_steps, tiles_x, tile_size, tiles_y, tile_size).transpose(
        0, 1, 3, 2, 4
    )
    tile_rows = tile_rows.reshape(-1, tile_size * tile_size)
    pieces_total = tile_rows.shape[0]
    owner_now = owners[0]
    slot_now = image_slots[0]
    sections = lax.axis_size("depth")
    order_ids = jnp.arange(pieces_total)
    same_owner = (owner_now[:, None] == owner_now[None, :]) & (
        order_ids[:, None] > order_ids[None, :]
    )
    rank_within = jnp.sum(same_owner.astype(jnp.int32), axis=1)
    position = owner_now * CAP + rank_within
    seat_ids = jnp.arange(sections * CAP)
    onehot = seat_ids[:, None] == position[None, :]
    buffer = jnp.dot(onehot.astype(jnp.float32), tile_rows, precision=lax.Precision.HIGHEST)
    buffer = buffer.reshape(sections, CAP, tile_size, tile_size)
    sent_slots = jnp.sum(jnp.where(onehot, slot_now[None, :] + 1, 0), axis=1) - 1
    sent_slots = sent_slots.reshape(sections, CAP)
    received, received_slots = (
        lax.all_to_all(buffer, "depth", split_axis=0, concat_axis=0, tiled=True),
        lax.all_to_all(sent_slots, "depth", split_axis=0, concat_axis=0, tiled=True),
    )
    select = jnp.arange(IMG_SLOTS)[:, None] == received_slots.reshape(1, -1)
    volume = jnp.dot(
        select.astype(jnp.float32),
        received.reshape(sections * CAP, tile_size * tile_size),
        precision=lax.Precision.HIGHEST,
    )
    image_volume = volume.reshape(IMG_SLOTS, tile_size, tile_size)
    return (image_volume, wave_state.reshape(1, 2, 2, cells_x, cells_y))


def solution(mesh):
    placed = (
        P(("groups", "depth"), None, None, None, None),
        P(("groups", "depth"), None, None),
        P(("groups", "depth"), None, None, None),
        P(("groups", "depth"), None),
        P(),
        P(),
        P(("groups", "depth"), None),
        P(("groups", "depth"), None),
    )
    return jax.shard_map(
        local,
        mesh=mesh,
        in_specs=placed,
        out_specs=(
            P(("groups", "depth"), None, None),
            P(("groups", "depth"), None, None, None, None),
        ),
        check_vma=False,
    )
```

profile of v0, /device:TPU:15, one launch (start us, length us, event | category | flops | bytes accessed | tf_op | source)
XLA Modules:
  0.0 473.0 jit_solution(14045230223784665825)
XLA Ops:
  8.8 1.3 fusion.877
  11.4 1.3 reduce_sum.32
  13.3 37.9 %all-gather.2.cloned.1.call-done = f32[32,128,128]{2,1,0:T(8,128)} async-done(((f32[2,128,128]{2,1,0:T(8,128)}), f32[32,128,128]{2,1,0:T(8,128)}) %all-gather.2.cloned.1.call-update) | async-done | bytes 2097168 | tf_op jit(solution)/shard_map/all_gather | solution.py:81
  51.2 2.2 gather_fusion
  55.5 34.1 %conditional.8 = (f32[2,512,256]{2,1,0:T(8,128)}) conditional(s32[]{:T(128)} %bitcast.326, (f32[]{:T(128)}, f32[4]{0:T(128)S(1)}, f32[512,256]{1,0:T(8,128)S(1)}, f32[1,2,2,512,256]{4,3,2,1,0:T(8,128)S(1)}, f32[3]{0:T(128)S(1)}) %tuple.310, (f32[]{:T(128)}, f32[4]{0:T(128)S(1)}, f32[512,256]{1,0:T(8,128)S(1)}, ...), branch_computations={%region_3.4_spmd, %region_4.5_spmd, %region_5.6_spmd} | conditional | flops 19922944 | bytes 23068800 | solution.py:71
  56.1 1.7 fusion.57
  57.8 1.7 fusion.69
  59.6 3.6 fusion.81
  63.9 12.3 %fusion.93 = f32[1,512,256]{2,1,0:T(8,128)S(1)} fusion(f32[2,512,256]{2,1,0:T(8,128)S(1)} %fusion.57, f32[2,512,256]{2,1,0:T(8,128)S(1)} %fusion.69, f32[2,512,256]{2,1,0:T(8,128)S(1)} %fusion.81, f32[1,2,2,512,256]{4,3,2,1,0:T(8,128)S(1)} %get-tuple-element.399, f32[512,256]{1,0:T(8,128)S(1)} %get-tuple-element.278, f32[]{:T(128)} %bitcast.37, ...), kind=kLoop, calls=%fused_computation.180 | loop fusion | flops 3538944 | bytes 5242912 | tf_op jit(solution)/shard_map/cond/branch_2_fun/stack | solution.py:37
  76.1 12.3 %fusion.101 = f32[1,512,256]{2,1,0:T(8,128)S(1)} fusion(f32[2,512,256]{2,1,0:T(8,128)S(1)} %fusion.57, f32[2,512,256]{2,1,0:T(8,128)S(1)} %fusion.69, f32[2,512,256]{2,1,0:T(8,128)S(1)} %fusion.81, f32[1,2,2,512,256]{4,3,2,1,0:T(8,128)S(1)} %get-tuple-element.399, f32[512,256]{1,0:T(8,128)S(1)} %get-tuple-element.278, f32[]{:T(128)} %bitcast.37, ...), kind=kLoop, calls=%fused_computation.188 | loop fusion | flops 3538944 | bytes 5242912 | tf_op jit(solution)/shard_map/cond/branch_2_fun/stack | solution.py:37
  89.6 44.3 %conditional.10 = (f32[2,512,256]{2,1,0:T(8,128)}) conditional(s32[]{:T(128)} %bitcast.330, (f32[]{:T(128)}, f32[4]{0:T(128)S(1)}, f32[512,256]{1,0:T(8,128)S(1)}, f32[2,512,256]{2,1,0:T(8,128)}, f32[3]{0:T(128)S(1)}) %tuple.313, (f32[]{:T(128)}, f32[4]{0:T(128)S(1)}, f32[512,256]{1,0:T(8,128)S(1)}, f32[2,512,256]{2,1,0:T(8,128)}, ...), branch_computations={%region_9.10_spmd, %region_10.11_spmd, %region_11.12_spmd} | conditional | flops 19922944 | bytes 25165980 | solution.py:71
  95.4 6.7 %fusion.261 = f32[2,512,256]{2,1,0:T(8,128)S(1)} fusion(f32[2,512,256]{2,1,0:T(8,128)} %get-tuple-element.315), kind=kLoop, calls=%fused_computation.528 | loop fusion | flops 2883584 | bytes 2097152 | tf_op jit(solution)/shard_map/cond/branch_2_fun/add | solution.py:23
  102.1 1.7 fusion.273
  103.8 3.6 fusion.285
  108.1 12.3 %fusion.297 = f32[1,512,256]{2,1,0:T(8,128)S(1)} fusion(f32[2,512,256]{2,1,0:T(8,128)S(1)} %fusion.261, f32[2,512,256]{2,1,0:T(8,128)S(1)} %fusion.273, f32[2,512,256]{2,1,0:T(8,128)S(1)} %fusion.285, f32[2,512,256]{2,1,0:T(8,128)S(1)} %copy-done.4, f32[512,256]{1,0:T(8,128)S(1)} %get-tuple-element.314, f32[]{:T(128)} %bitcast.118, f32[]{:T(128)} %bitcast.117, ...), kind=kLoop, calls=%fused_computation.573 | loop fusion | flops 3538944 | bytes 5242912 | tf_op jit(solution)/shard_map/cond/branch_2_fun/stack | solution.py:37
  120.4 12.3 %fusion.305 = f32[1,512,256]{2,1,0:T(8,128)S(1)} fusion(f32[2,512,256]{2,1,0:T(8,128)S(1)} %fusion.261, f32[2,512,256]{2,1,0:T(8,128)S(1)} %fusion.273, f32[2,512,256]{2,1,0:T(8,128)S(1)} %fusion.285, f32[2,512,256]{2,1,0:T(8,128)S(1)} %copy-done.4, f32[512,256]{1,0:T(8,128)S(1)} %get-tuple-element.314, f32[]{:T(128)} %bitcast.118, f32[]{:T(128)} %bitcast.117, ...), kind=kLoop, calls=%fused_computation.581 | loop fusion | flops 3538944 | bytes 5242912 | tf_op jit(solution)/shard_map/cond/branch_2_fun/stack | solution.py:37
  134.0 1.9 collective-permute-start
  135.9 37.7 %conditional.9 = (f32[2,512,256]{2,1,0:T(8,128)}) conditional(s32[]{:T(128)} %bitcast.326, (f32[]{:T(128)}, f32[4]{0:T(128)S(1)}, f32[512,256]{1,0:T(8,128)S(1)}, f32[1,2,2,512,256]{4,3,2,1,0:T(8,128)S(1)}, f32[3]{0:T(128)S(1)}) %tuple.316, (f32[]{:T(128)}, f32[4]{0:T(128)S(1)}, f32[512,256]{1,0:T(8,128)S(1)}, ...), branch_computations={%region_6.7_spmd, %region_7.8_spmd, %region_8.9_spmd} | conditional | flops 20971520 | bytes 23068800 | solution.py:71
  140.0 1.7 fusion.159
  141.8 1.7 fusion.171
  143.5 3.6 fusion.183
  147.8 12.3 %fusion.195 = f32[1,512,256]{2,1,0:T(8,128)S(1)} fusion(f32[2,512,256]{2,1,0:T(8,128)S(1)} %fusion.159, f32[2,512,256]{2,1,0:T(8,128)S(1)} %fusion.171, f32[2,512,256]{2,1,0:T(8,128)S(1)} %fusion.183, f32[1,2,2,512,256]{4,3,2,1,0:T(8,128)S(1)} %get-tuple-element.405, f32[512,256]{1,0:T(8,128)S(1)} %get-tuple-element.299, f32[]{:T(128)} %bitcast.79, ...), kind=kLoop, calls=%fused_computation.378 | loop fusion | flops 4063232 | bytes 5242912 | tf_op jit(solution)/shard_map/cond/branch_2_fun/stack | solution.py:37
  160.1 12.3 %fusion.203 = f32[1,512,256]{2,1,0:T(8,128)S(1)} fusion(f32[2,512,256]{2,1,0:T(8,128)S(1)} %fusion.159, f32[2,512,256]{2,1,0:T(8,128)S(1)} %fusion.171, f32[2,512,256]{2,1,0:T(8,128)S(1)} %fusion.183, f32[1,2,2,512,256]{4,3,2,1,0:T(8,128)S(1)} %get-tuple-element.405, f32[512,256]{1,0:T(8,128)S(1)} %get-tuple-element.299, f32[]{:T(128)} %bitcast.79, ...), kind=kLoop, calls=%fused_computation.386 | loop fusion | flops 4063232 | bytes 5242912 | tf_op jit(solution)/shard_map/cond/branch_2_fun/stack | solution.py:37
  173.7 52.3 %conditional.12 = (f32[2,512,256]{2,1,0:T(8,128)}) conditional(s32[]{:T(128)} %bitcast.330, (f32[]{:T(128)}, f32[4]{0:T(128)S(1)}, f32[512,256]{1,0:T(8,128)S(1)}, f32[2,512,256]{2,1,0:T(8,128)}, f32[3]{0:T(128)S(1)}) %tuple.321, (f32[]{:T(128)}, f32[4]{0:T(128)S(1)}, f32[512,256]{1,0:T(8,128)S(1)}, f32[2,512,256]{2,1,0:T(8,128)}, ...), branch_computations={%region_15.16_spmd, %region_16.17_spmd, %region_17.18_spmd} | conditional | flops 20971520 | bytes 20971648 | solution.py:71
  179.4 7.0 %fusion.465 = f32[2,512,256]{2,1,0:T(8,128)S(1)} fusion(f32[2,512,256]{2,1,0:T(8,128)} %get-tuple-element.345), kind=kLoop, calls=%fused_computation.918 | loop fusion | flops 2883584 | bytes 2097152 | tf_op jit(solution)/shard_map/cond/branch_2_fun/add | solution.py:23
  186.5 2.9 fusion.477
  189.4 8.1 %fusion.489 = f32[2,512,256]{2,1,0:T(8,128)S(1)} fusion(f32[2,512,256]{2,1,0:T(8,128)S(1)} %fusion.477, f32[2,512,256]{2,1,0:T(8,128)} %get-tuple-element.345), kind=kLoop, calls=%fused_computation.942 | loop fusion | flops 6291456 | bytes 3145728 | tf_op jit(solution)/shard_map/cond/branch_2_fun/sub | solution.py:50
  198.2 13.2 %fusion.501 = f32[1,512,256]{2,1,0:T(8,128)S(1)} fusion(f32[2,512,256]{2,1,0:T(8,128)S(1)} %fusion.465, f32[2,512,256]{2,1,0:T(8,128)S(1)} %fusion.477, f32[2,512,256]{2,1,0:T(8,128)S(1)} %fusion.489, f32[2,512,256]{2,1,0:T(8,128)} %get-tuple-element.345, f32[512,256]{1,0:T(8,128)S(1)} %get-tuple-element.344, f32[]{:T(128)} %bitcast.196, f32[]{:T(128)} %bitcast.195, ...), kind=kLoop, calls=%fused_computation.963 | loop fusion | flops 4063232 | bytes 5242912 | tf_op jit(solution)/shard_map/cond/branch_2_fun/stack | solution.py:37
  211.5 13.2 %fusion.509 = f32[1,512,256]{2,1,0:T(8,128)S(1)} fusion(f32[2,512,256]{2,1,0:T(8,128)S(1)} %fusion.465, f32[2,512,256]{2,1,0:T(8,128)S(1)} %fusion.477, f32[2,512,256]{2,1,0:T(8,128)S(1)} %fusion.489, f32[2,512,256]{2,1,0:T(8,128)} %get-tuple-element.345, f32[512,256]{1,0:T(8,128)S(1)} %get-tuple-element.344, f32[]{:T(128)} %bitcast.196, f32[]{:T(128)} %bitcast.195, ...), kind=kLoop, calls=%fused_computation.971 | loop fusion | flops 4063232 | bytes 5242912 | tf_op jit(solution)/shard_map/cond/branch_2_fun/stack | solution.py:37
  226.0 1.9 collective-permute-start.1
  228.9 5.3 %all-to-all-start = ((s32[16,1,2]{2,1,0:T(1,128)}), s32[16,1,2]{2,1,0:T(1,128)S(1)}, u32[]{:S(2)}, u32[]{:S(2)}) async-start(s32[16,1,2]{2,1,0:T(1,128)} %bitcast.322), calls=%async_computation | async-start | bytes 16384 | tf_op jit(solution)/shard_map/all_to_all | solution.py:134
  234.2 45.5 %conditional.11 = (f32[2,512,256]{2,1,0:T(8,128)S(1)}) conditional(s32[]{:T(128)} %bitcast.326, (f32[]{:T(128)}, f32[4]{0:T(128)S(1)}, f32[512,256]{1,0:T(8,128)S(1)}, f32[2,512,256]{2,1,0:T(8,128)}, f32[3]{0:T(128)S(1)}) %tuple.322, (f32[]{:T(128)}, f32[4]{0:T(128)S(1)}, f32[512,256]{1,0:T(8,128)S(1)}, ...), branch_computations={%region_12.13_spmd, %region_13.14_spmd, %region_14.15_spmd} | conditional | flops 19922944 | bytes 20971648 | solution.py:71
  234.7 6.7 %fusion.363 = f32[2,512,256]{2,1,0:T(8,128)S(1)} fusion(f32[2,512,256]{2,1,0:T(8,128)} %get-tuple-element.330), kind=kLoop, calls=%fused_computation.723 | loop fusion | flops 2883584 | bytes 2097152 | tf_op jit(solution)/shard_map/cond/branch_2_fun/add | solution.py:23
  241.4 2.9 fusion.375
  244.3 8.1 %fusion.387 = f32[2,512,256]{2,1,0:T(8,128)S(1)} fusion(f32[2,512,256]{2,1,0:T(8,128)S(1)} %fusion.375, f32[2,512,256]{2,1,0:T(8,128)} %get-tuple-element.330), kind=kLoop, calls=%fused_computation.747 | loop fusion | flops 6291456 | bytes 3145728 | tf_op jit(solution)/shard_map/cond/branch_2_fun/sub | solution.py:50
  253.2 13.1 %fusion.399 = f32[1,512,256]{2,1,0:T(8,128)S(1)} fusion(f32[2,512,256]{2,1,0:T(8,128)S(1)} %fusion.363, f32[2,512,256]{2,1,0:T(8,128)S(1)} %fusion.375, f32[2,512,256]{2,1,0:T(8,128)S(1)} %fusion.387, f32[2,512,256]{2,1,0:T(8,128)} %get-tuple-element.330, f32[512,256]{1,0:T(8,128)S(1)} %get-tuple-element.329, f32[]{:T(128)} %bitcast.157, f32[]{:T(128)} %bitcast.156, ...), kind=kLoop, calls=%fused_computation.768 | loop fusion | flops 3538944 | bytes 5242912 | tf_op jit(solution)/shard_map/cond/branch_2_fun/stack | solution.py:37
  266.3 13.1 %fusion.407 = f32[1,512,256]{2,1,0:T(8,128)S(1)} fusion(f32[2,512,256]{2,1,0:T(8,128)S(1)} %fusion.363, f32[2,512,256]{2,1,0:T(8,128)S(1)} %fusion.375, f32[2,512,256]{2,1,0:T(8,128)S(1)} %fusion.387, f32[2,512,256]{2,1,0:T(8,128)} %get-tuple-element.330, f32[512,256]{1,0:T(8,128)S(1)} %get-tuple-element.329, f32[]{:T(128)} %bitcast.157, f32[]{:T(128)} %bitcast.156, ...), kind=kLoop, calls=%fused_computation.776 | loop fusion | flops 3538944 | bytes 5242912 | tf_op jit(solution)/shard_map/cond/branch_2_fun/stack | solution.py:37
  280.6 43.4 %conditional.13 = (f32[2,512,256]{2,1,0:T(8,128)}) conditional(s32[]{:T(128)} %bitcast.326, (f32[]{:T(128)}, f32[4]{0:T(128)S(1)}, f32[512,256]{1,0:T(8,128)S(1)}, f32[2,512,256]{2,1,0:T(8,128)}, f32[3]{0:T(128)S(1)}) %tuple.325, (f32[]{:T(128)}, f32[4]{0:T(128)S(1)}, f32[512,256]{1,0:T(8,128)S(1)}, f32[2,512,256]{2,1,0:T(8,128)}, ...), branch_computations={%region_18.19_spmd, %region_19.20_spmd, %region_20.21_spmd} | conditional | flops 20971520 | bytes 25165980 | solution.py:71
  285.4 6.8 %fusion.567 = f32[2,512,256]{2,1,0:T(8,128)S(1)} fusion(f32[2,512,256]{2,1,0:T(8,128)} %get-tuple-element.360), kind=kLoop, calls=%fused_computation.1113 | loop fusion | flops 2883584 | bytes 2097152 | tf_op jit(solution)/shard_map/cond/branch_2_fun/add | solution.py:23
  292.2 1.7 fusion.579
  294.0 3.6 fusion.591
  298.3 12.2 %fusion.603 = f32[1,512,256]{2,1,0:T(8,128)S(1)} fusion(f32[2,512,256]{2,1,0:T(8,128)S(1)} %fusion.567, f32[2,512,256]{2,1,0:T(8,128)S(1)} %fusion.579, f32[2,512,256]{2,1,0:T(8,128)S(1)} %fusion.591, f32[2,512,256]{2,1,0:T(8,128)S(1)} %copy-done.9, f32[512,256]{1,0:T(8,128)S(1)} %get-tuple-element.359, f32[]{:T(128)} %bitcast.235, f32[]{:T(128)} %bitcast.234, ...), kind=kLoop, calls=%fused_computation.1158 | loop fusion | flops 4063232 | bytes 5242912 | tf_op jit(solution)/shard_map/cond/branch_2_fun/stack | solution.py:37
  310.5 12.2 %fusion.611 = f32[1,512,256]{2,1,0:T(8,128)S(1)} fusion(f32[2,512,256]{2,1,0:T(8,128)S(1)} %fusion.567, f32[2,512,256]{2,1,0:T(8,128)S(1)} %fusion.579, f32[2,512,256]{2,1,0:T(8,128)S(1)} %fusion.591, f32[2,512,256]{2,1,0:T(8,128)S(1)} %copy-done.9, f32[512,256]{1,0:T(8,128)S(1)} %get-tuple-element.359, f32[]{:T(128)} %bitcast.235, f32[]{:T(128)} %bitcast.234, ...), kind=kLoop, calls=%fused_computation.1166 | loop fusion | flops 4063232 | bytes 5242912 | tf_op jit(solution)/shard_map/cond/branch_2_fun/stack | solution.py:37
  324.1 2.6 fusion.825
  326.7 35.8 %conditional.14 = (f32[2,512,256]{2,1,0:T(8,128)S(1)}) conditional(s32[]{:T(128)} %bitcast.330, (f32[]{:T(128)}, f32[4]{0:T(128)S(1)}, f32[512,256]{1,0:T(8,128)S(1)}, f32[2,512,256]{2,1,0:T(8,128)S(1)}, f32[3]{0:T(128)S(1)}) %tuple.328, (f32[]{:T(128)}, f32[4]{0:T(128)S(1)}, f32[512,256]{1,0:T(8,128)S(1)}, ...), branch_computations={%region_21.22_spmd, %region_22.23_spmd, %region_23.24_spmd} | conditional | flops 19922944 | bytes 20971648 | solution.py:71
  330.0 1.7 fusion.669
  331.7 1.7 fusion.681
  333.5 3.6 fusion.693
  337.8 12.2 %fusion.705 = f32[1,512,256]{2,1,0:T(8,128)S(1)} fusion(f32[2,512,256]{2,1,0:T(8,128)S(1)} %fusion.669, f32[2,512,256]{2,1,0:T(8,128)S(1)} %fusion.681, f32[2,512,256]{2,1,0:T(8,128)S(1)} %fusion.693, f32[2,512,256]{2,1,0:T(8,128)S(1)} %get-tuple-element.375, f32[512,256]{1,0:T(8,128)S(1)} %get-tuple-element.374, f32[]{:T(128)} %bitcast.274, f32[]{:T(128)} %bitcast.273, ...), kind=kLoop, calls=%fused_computation.1353 | loop fusion | flops 3538944 | bytes 5242912 | tf_op jit(solution)/shard_map/cond/branch_2_fun/stack | solution.py:37
  350.0 12.2 %fusion.713 = f32[1,512,256]{2,1,0:T(8,128)S(1)} fusion(f32[2,512,256]{2,1,0:T(8,128)S(1)} %fusion.669, f32[2,512,256]{2,1,0:T(8,128)S(1)} %fusion.681, f32[2,512,256]{2,1,0:T(8,128)S(1)} %fusion.693, f32[2,512,256]{2,1,0:T(8,128)S(1)} %get-tuple-element.375, f32[512,256]{1,0:T(8,128)S(1)} %get-tuple-element.374, f32[]{:T(128)} %bitcast.274, f32[]{:T(128)} %bitcast.273, ...), kind=kLoop, calls=%fused_computation.1361 | loop fusion | flops 3538944 | bytes 5242912 | tf_op jit(solution)/shard_map/cond/branch_2_fun/stack | solution.py:37
  362.5 38.3 %conditional.15 = (f32[2,512,256]{2,1,0:T(8,128)S(1)}) conditional(s32[]{:T(128)} %bitcast.330, (f32[]{:T(128)}, f32[4]{0:T(128)S(1)}, f32[512,256]{1,0:T(8,128)S(1)}, f32[2,512,256]{2,1,0:T(8,128)S(1)}, f32[3]{0:T(128)S(1)}) %tuple.331, (f32[]{:T(128)}, f32[4]{0:T(128)S(1)}, f32[512,256]{1,0:T(8,128)S(1)}, ...), branch_computations={%region_24.25_spmd, %region_25.26_spmd, %region_26.27_spmd} | conditional | flops 20971520 | bytes 20971648 | solution.py:71
  368.2 1.7 fusion.771
  369.9 1.7 fusion.783
  371.7 3.6 fusion.795
  376.0 12.2 %fusion.807 = f32[1,512,256]{2,1,0:T(8,128)S(1)} fusion(f32[2,512,256]{2,1,0:T(8,128)S(1)} %fusion.771, f32[2,512,256]{2,1,0:T(8,128)S(1)} %fusion.783, f32[2,512,256]{2,1,0:T(8,128)S(1)} %fusion.795, f32[2,512,256]{2,1,0:T(8,128)S(1)} %get-tuple-element.390, f32[512,256]{1,0:T(8,128)S(1)} %get-tuple-element.389, f32[]{:T(128)} %bitcast.313, f32[]{:T(128)} %bitcast.312, ...), kind=kLoop, calls=%fused_computation.1548 | loop fusion | flops 4063232 | bytes 5242912 | tf_op jit(solution)/shard_map/cond/branch_2_fun/stack | solution.py:37
  388.2 12.2 %fusion.815 = f32[1,512,256]{2,1,0:T(8,128)S(1)} fusion(f32[2,512,256]{2,1,0:T(8,128)S(1)} %fusion.771, f32[2,512,256]{2,1,0:T(8,128)S(1)} %fusion.783, f32[2,512,256]{2,1,0:T(8,128)S(1)} %fusion.795, f32[2,512,256]{2,1,0:T(8,128)S(1)} %get-tuple-element.390, f32[512,256]{1,0:T(8,128)S(1)} %get-tuple-element.389, f32[]{:T(128)} %bitcast.313, f32[]{:T(128)} %bitcast.312, ...), kind=kLoop, calls=%fused_computation.1556 | loop fusion | flops 4063232 | bytes 5242912 | tf_op jit(solution)/shard_map/cond/branch_2_fun/stack | solution.py:37
  400.8 1.3 stack.225
  403.0 1.8 fusion.822
  406.2 1.5 fusion.819
  407.7 1.9 copy.38
  409.7 4.3 all-to-all-start.1
  415.3 1.5 pad_maximum_fusion.24
  416.8 44.7 %all-to-all-done.1 = f32[16,2,128,128]{3,2,1,0:T(8,128)} async-done(((f32[16,2,128,128]{3,2,1,0:T(8,128)}), f32[16,2,128,128]{3,2,1,0:T(8,128)}, u32[]{:S(2)}, u32[]{:S(2)}) %all-to-all-start.1) | async-done | bytes 2097184 | tf_op jit(solution)/shard_map/all_to_all | solution.py:133
  461.5 3.4 fusion.816
  (66 shorter events, 21.0 us)
Async XLA Ops:
  7.2 44.1 %all-gather.2.cloned.1.call-start = ((), (), s32[]{:S(2)}) async-start(), calls=%async_computation.2 | async-start | bytes 2228224 | tf_op jit(solution)/shard_map/all_gather | solution.py:81
  53.9 1.6 copy-start
  53.9 1.6 copy-start.10
  54.0 1.6 copy-start.11
  95.4 6.7 %copy-start.4 = (f32[2,512,256]{2,1,0:T(8,128)S(1)}, f32[2,512,256]{2,1,0:T(8,128)}, u32[]{:S(2)}) copy-start(f32[2,512,256]{2,1,0:T(8,128)} %get-tuple-element.315) | copy-start | bytes 3145732 | tf_op jit(solution)/shard_map/cond
  134.0 100.2 %collective-permute-start = (f32[2,512,256]{2,1,0:T(8,128)}, f32[2,512,256]{2,1,0:T(8,128)}, u32[]{:S(2)}, u32[]{:S(2)}) collective-permute-start(f32[2,512,256]{2,1,0:T(8,128)} %get-tuple-element.606), channel_id=1, source_target_pairs={{0,1},{1,2},{2,3},{3,4},{4,5},{5,6},{6,7},{7,8},{8,9},{9,10},{10,1... | collective-permute-start | bytes 3145736 | tf_op jit(solution)/shard_map/ppermute | solution.py:16
  173.6 54.3 %copy-start.12 = (s32[1,16]{1,0:T(1,128)S(1)}, s32[1,16]{1,0:T(1,128)}, u32[]{:S(2)}) copy-start(s32[1,16]{1,0:T(1,128)} %param.38) | copy-start | bytes 196
  173.7 54.4 %copy-start.13 = (s32[1,16]{1,0:T(1,128)S(1)}, s32[1,16]{1,0:T(1,128)}, u32[]{:S(2)}) copy-start(s32[1,16]{1,0:T(1,128)} %param.39) | copy-start | bytes 196
  226.0 53.7 %collective-permute-start.1 = (f32[2,512,256]{2,1,0:T(8,128)}, f32[2,512,256]{2,1,0:T(8,128)S(1)}, u32[]{:S(2)}, u32[]{:S(2)}) collective-permute-start(f32[2,512,256]{2,1,0:T(8,128)} %get-tuple-element.608), channel_id=1, source_target_pairs={{0,1},{1,2},{2,3},{3,4},{4,5},{5,6},{6,7},{7,8},{8,9},{9,10},{10,1... | collective-permute-start | bytes 3145736 | tf_op jit(solution)/shard_map/ppermute | solution.py:16
  228.9 180.8 %all-to-all-start = ((s32[16,1,2]{2,1,0:T(1,128)}), s32[16,1,2]{2,1,0:T(1,128)S(1)}, u32[]{:S(2)}, u32[]{:S(2)}) async-start(s32[16,1,2]{2,1,0:T(1,128)} %bitcast.322), calls=%async_computation | async-start | bytes 16384 | tf_op jit(solution)/shard_map/all_to_all | solution.py:134
  279.7 1.0 copy-start.6
  280.6 43.4 %copy-start.1 = (f32[2,512,256]{2,1,0:T(8,128)S(1)}, f32[2,512,256]{2,1,0:T(8,128)}, u32[]{:S(2)}) copy-start(f32[2,512,256]{2,1,0:T(8,128)} %get-tuple-element.604) | copy-start | bytes 3145732
  285.4 6.8 %copy-start.9 = (f32[2,512,256]{2,1,0:T(8,128)S(1)}, f32[2,512,256]{2,1,0:T(8,128)}, u32[]{:S(2)}) copy-start(f32[2,512,256]{2,1,0:T(8,128)} %get-tuple-element.360) | copy-start | bytes 3145732 | tf_op jit(solution)/shard_map/cond
  326.7 35.9 %copy-start.5 = (f32[2,512,256]{2,1,0:T(8,128)S(1)}, f32[2,512,256]{2,1,0:T(8,128)}, u32[]{:S(2)}) copy-start(f32[2,512,256]{2,1,0:T(8,128)} %get-tuple-element.609) | copy-start | bytes 3145732
  409.7 51.8 %all-to-all-start.1 = ((f32[16,2,128,128]{3,2,1,0:T(8,128)}), f32[16,2,128,128]{3,2,1,0:T(8,128)}, u32[]{:S(2)}, u32[]{:S(2)}) async-start(f32[16,2,128,128]{3,2,1,0:T(8,128)} %copy.38), calls=%async_computation.1 | async-start | bytes 4194304 | tf_op jit(solution)/shard_map/all_to_all | solution.py:133
Sparse Core Ops, SparseCore 0:
  10.2 41.0 all-gather.1
where the time goes:
time: 481 us; the launch traced here: 473 us
  other arithmetic  303 us (63%)
  waiting for transfers between devices  83.3 us (17%)
  loops' own time  32.3 us (7%)
  local copies, waits for them, and re-layouts  18.8 us (4%)
  between operations  16.5 us (3%)
  starting transfers between devices  13.5 us (3%)
  matrix products  4.94 us (1%)
    another operation x24, other arithmetic, rotate_add(): return jnp.stack(pieces_out)  205 us
    sub x16, other arithmetic, advance(): series_term = 2.0 * mcclellan(current) - previous  54.3 us
    all_to_all x1, waiting for transfers between devices, local(): lax.all_to_all(buffer, 'depth', split_axis=0, concat_axis=0, tiled=True)  44.7 us
    all_gather x1, waiting for transfers between devices, local(): library = lax.all_gather(vel_tiles, 'depth', axis=0, tiled=True)  37.9 us
    add x8, other arithmetic, mcclellan(): return -0.5 * fields_in + 0.25 * beside + 0.125 * corner  34.1 us
    another operation x8, loops' own time, stepped(): return lax.switch(order_now - 1, branches, wave_state, slowness_now)  32.3 us
  transfers between devices with their start and end apart: 5, of which 2 were waited for; matrix products, arithmetic and copies ran while one was open for 52% of the time, Pallas kernels for 0%

commit v1 on v0

v1 whole, which is shorter than its diff:
```python
from functools import partial

import jax
import jax.numpy as jnp
import numpy as np
from jax import lax
from jax.experimental import pallas as pl
from jax.experimental.pallas import tpu as pltpu
from jax.sharding import PartitionSpec as P

TICKS = 2
CAP = 2
IMG_SLOTS = 8
LANES = 128
SUBS = 8
VMEM = pl.BlockSpec(memory_space=pltpu.VMEM)
SMEM = pl.BlockSpec(memory_space=pltpu.SMEM)
ANY = pl.BlockSpec(memory_space=pl.ANY)
PARAMS = pltpu.CompilerParams(vmem_limit_bytes=56 * 2**20)


def in_powers(terms):
    rows = np.zeros((terms, terms))
    polys = [np.array([1.0]), np.array([-1.0, 1.0])]
    while len(polys) < terms:
        grown = np.convolve(polys[-1], [-2.0, 2.0])
        grown[: len(polys[-2])] -= polys[-2]
        polys.append(grown)
    for k in range(terms):
        rows[k, : len(polys[k])] = polys[k] / 8.0 ** np.arange(len(polys[k]))
    return rows


def fitted():
    nodes = 0.25 * (1.0 - np.cos((np.arange(400) + 0.5) * np.pi / 400)) / 2.0
    r = np.sqrt(nodes)
    sine = np.polynomial.chebyshev.Chebyshev.fit(nodes, np.sqrt(2.0) * np.sin(np.pi * r) / r, 4)
    cosine = np.polynomial.chebyshev.Chebyshev.fit(nodes, np.sqrt(2.0) * np.cos(np.pi * r), 4)
    make = np.polynomial.polynomial.Polynomial
    return (
        [float(c) for c in sine.convert(kind=make).coef],
        [float(c) for c in cosine.convert(kind=make).coef],
    )


SINE, COSINE = fitted()


def horner(x, coefs):
    out = coefs[-1] * x + coefs[-2]
    for c in coefs[-3::-1]:
        out = out * x + c
    return out


def cos_sin(turns):
    r = turns - jnp.round(turns)
    r2 = r * r
    s = r * horner(r2, SINE)
    c = horner(r2, COSINE)
    return 1.0 - s * s, s * c


def lanes_121(blocks):
    lane = lax.broadcasted_iota(jnp.int32, blocks[0].shape, 1)
    first, last = lane == 0, lane == LANES - 1
    turned = [pltpu.roll(b, 1, 1) for b in blocks]
    sums = [
        b + jnp.where(first, turned[i - 1] if i else 0.0, turned[i])
        for i, b in enumerate(blocks)
    ]
    back = [pltpu.roll(s, LANES - 1, 1) for s in sums]
    return [
        s + jnp.where(last, back[i + 1] if i + 1 < len(sums) else blocks[i], back[i])
        for i, s in enumerate(sums)
    ]


class Rows:
    def __init__(self, ref):
        self.ref = ref
        self.planes, padded, _, self.cells_y = ref.shape
        self.R = padded - 2
        self.blocks = self.cells_y // LANES

    def get(self, p, r):
        return [self.ref[p, r + 1, :, b * LANES : (b + 1) * LANES] for b in range(self.blocks)]

    def put(self, p, r, values):
        for b, v in enumerate(values):
            self.ref[p, r + 1, :, b * LANES : (b + 1) * LANES] = v

    def halo(self):
        for p in range(self.planes):
            for b in range(self.blocks):
                at = slice(b * LANES, (b + 1) * LANES)
                sub = lax.broadcasted_iota(jnp.int32, (SUBS, LANES), 0)
                low = pltpu.roll(self.ref[p, self.R, :, at], 1, 0)
                self.ref[p, 0, :, at] = jnp.where(sub == 0, 0.0, low)
                high = pltpu.roll(self.ref[p, 1, :, at], SUBS - 1, 0)
                self.ref[p, self.R + 1, :, at] = jnp.where(sub == SUBS - 1, 0.0, high)


def smoothed(src, unroll, visit):
    planes = range(src.planes)

    def body(r, carry):
        values, kept = [], []
        for p in planes:
            here, below = carry[p]
            nxt = src.get(p, r + 1)
            above = [n + h for n, h in zip(nxt, here)]
            values.append(lanes_121([a + b for a, b in zip(above, below)]))
            kept.append((nxt, above))
        visit(r, values)
        return kept

    start = []
    for p in planes:
        here, before = src.get(p, 0), src.get(p, -1)
        start.append((here, [h + b for h, b in zip(here, before)]))
    lax.fori_loop(0, src.R, body, start, unroll=unroll)


def depth_step(levels, coefs, signs, emit):
    for low, high in zip(levels[:-2], levels[1:-1]):

        def store(r, values, high=high):
            for p, v in enumerate(values):
                high.put(p, r, v)

        smoothed(low, 4, store)
        high.halo()

    def combine(r, values):
        result = [None] * len(values)
        terms = len(levels)
        for k in range(terms):
            for b in range(levels[0].blocks):
                at = slice(b * LANES, (b + 1) * LANES)
                a = coefs[2 * k, r, :, at]
                s = coefs[2 * k + 1, r, :, at]
                for pair, sign in enumerate(signs):
                    if k == terms - 1:
                        re, im = values[2 * pair][b], values[2 * pair + 1][b]
                    else:
                        re, im = (levels[k].get(2 * pair + i, r)[b] for i in (0, 1))
                    x, y = a * re, a * im
                    u, v = s * im, s * re
                    x, y = (x - u, y + v) if sign > 0 else (x + u, y - v)
                    for i, w in ((0, x), (1, y)):
                        slot = result[2 * pair + i] = result[2 * pair + i] or [None] * levels[0].blocks
                        slot[b] = w if slot[b] is None else slot[b] + w
        emit(r, result)

    smoothed(levels[-2], 2, combine)


def fetch(field_ref, flat, sem):
    copies = [
        pltpu.make_async_copy(field_ref.at[:, :, pl.ds(b * LANES, LANES)], flat.at[:, b], sem.at[b])
        for b in range(flat.shape[1])
    ]
    for copy in copies:
        copy.start()
    return copies


def load_rows(flat, state):
    def body(r, _):
        for p in range(state.planes):
            state.put(
                p, r, [flat[p, b, pl.ds(r, SUBS, stride=state.R), :] for b in range(state.blocks)]
            )
        return 0

    lax.fori_loop(0, state.R, body, 0, unroll=4)
    state.halo()


def product(source, receiver, b):
    return source[0][b] * receiver[0][b] + source[1][b] * receiver[1][b]


def coefs_kernel(
    axis, pieces, ids_ref, orders_ref, ids_up_ref, orders_up_ref, weights_ref, rates_ref, *rest
):
    tiles, (fields_ref, coefs_ref, image_ref), (library, slow, sems, flat, flat_sem, *levels) = (
        rest[: len(pieces)],
        rest[len(pieces) : len(pieces) + 3],
        rest[len(pieces) + 3 :],
    )
    arriving = fetch(fields_ref, flat, flat_sem)
    per = library.shape[0] // sum(len(at) for at in pieces)
    copies = []
    for ref, at in zip(tiles, pieces):
        for i, k in enumerate(at):
            source = ref.at[i] if len(at) > 1 else ref
            copies.append(
                pltpu.make_async_copy(source, library.at[pl.ds(k * per, per)], sems.at[len(copies)])
            )
            copies[-1].start()
    for copy in copies:
        copy.wait()
    me = lax.axis_index(axis)
    steps, tiles_x, tiles_y = ids_ref.shape[-3:]
    size = library.shape[1]
    terms = rates_ref.shape[0]
    powers = in_powers(terms)
    R = coefs_ref.shape[3]
    blocks = coefs_ref.shape[5] // LANES
    total = weights_ref[0]
    for k in range(1, terms - 1):
        total = total + weights_ref[k]
    base = [1.0 - total] + [weights_ref[k] for k in range(terms - 1)]
    turn = [rates_ref[k] * (0.5 / np.pi) for k in range(terms)]
    for which, (ids, orders) in enumerate(((ids_up_ref, orders_up_ref), (ids_ref, orders_ref))):
        for j in range(steps):
            for a in range(tiles_x):
                for b in range(tiles_y):
                    tile = ids[0, j, a, b]
                    at = (tile // per ^ me) * per + tile % per
                    slow[b, a * size : (a + 1) * size, :] = library[at]
            scale = [jnp.where(k <= orders[0, j], base[k], 0.0) for k in range(terms)]

            def body(r, _):
                for b in range(blocks):
                    at = slice(b * LANES, (b + 1) * LANES)
                    here = slow[b, pl.ds(r, SUBS, stride=R), :]
                    parts = []
                    for k in range(terms):
                        c, s = cos_sin(here * turn[k])
                        parts.append((c * scale[k], s * scale[k]))
                    for m in range(terms):
                        for i in (0, 1):
                            out = None
                            for k in range(m, terms):
                                w = float(powers[k, m])
                                term = parts[k][i] if w == 1.0 else parts[k][i] * w
                                out = term if out is None else out + term
                            coefs_ref[which, j, 2 * m + i, r, :, at] = out
                return 0

            lax.fori_loop(0, R, body, 0, unroll=2)
    levels = [Rows(ref) for ref in levels]
    for copy in arriving:
        copy.wait()
    load_rows(flat, levels[0])
    for j in range(steps):

        def emit(r, result, j=j):
            for p, v in enumerate(result):
                levels[0].put(p, r, v)
            for b in range(blocks):
                image_ref[j, r, :, b * LANES : (b + 1) * LANES] = product(result[:2], result[2:], b)

        depth_step(levels, coefs_ref.at[1, j], (1, -1), emit)
        levels[0].halo()


def receiver_kernel(fields_ref, coefs_ref, states_ref, flat, flat_sem, *levels):
    arriving = fetch(fields_ref, flat, flat_sem)
    levels = [Rows(ref) for ref in levels]
    steps = coefs_ref.shape[1]
    for copy in arriving:
        copy.wait()
    load_rows(flat, levels[0])
    for which in range(TICKS):
        for j in range(steps):

            def emit(r, result, j=j, which=which):
                for p, v in enumerate(result):
                    levels[0].put(p, r, v)
                    if which == TICKS - 1:
                        for b, w in enumerate(v):
                            states_ref[j, p, r, :, b * LANES : (b + 1) * LANES] = w

            depth_step(levels, coefs_ref.at[which, j], (-1,), emit)
            levels[0].halo()


def source_kernel(
    fields_ref, coefs_ref, receivers_ref, image_ref, owners_ref, slots_ref,
    buffer_ref, state_ref, images, slot_rows, held, sem, slot_sem, flat, flat_sem, *levels
):
    arriving = fetch(fields_ref, flat, flat_sem)
    levels = [Rows(ref) for ref in levels]
    steps = coefs_ref.shape[1]
    blocks = levels[0].blocks
    R = levels[0].R
    for copy in arriving:
        copy.wait()
    load_rows(flat, levels[0])
    for which in range(TICKS):
        for j in range(steps):

            def emit(r, result, j=j, which=which):
                for p, v in enumerate(result):
                    if which == TICKS - 1 and j == steps - 1:
                        for b, w in enumerate(v):
                            state_ref[p, r, :, b * LANES : (b + 1) * LANES] = w
                    else:
                        levels[0].put(p, r, v)
                if which == TICKS - 1:
                    for b in range(blocks):
                        at = slice(b * LANES, (b + 1) * LANES)
                        there = [[receivers_ref[j, p, r, :, at]] for p in (0, 1)]
                        here = [[result[p][b]] for p in (0, 1)]
                        images[j, b, pl.ds(r, SUBS, stride=R), :] = (
                            image_ref[j, r, :, at] + product(here, there, 0)
                        )

            depth_step(levels, coefs_ref.at[which, j], (1,), emit)
            levels[0].halo()
    size = buffer_ref.shape[2]
    peers = buffer_ref.shape[0]
    extra = slot_rows.shape[1]
    tiles_x, tiles_y = images.shape[2] // size, images.shape[1]
    rows = (buffer_ref.shape[1] - extra) // CAP
    for o in range(peers * CAP):
        held[o] = -1
    copies = []
    for p in range(steps * tiles_x * tiles_y):
        j, a, b = p // (tiles_x * tiles_y), p // tiles_y % tiles_x, p % tiles_y
        owner = owners_ref[0, p]
        rank = jnp.int32(0)
        for before in range(p):
            rank = rank + (owners_ref[0, before] == owner).astype(jnp.int32)
        held[owner * CAP + rank] = slots_ref[0, p]
        copies.append(
            pltpu.make_async_copy(
                images.at[j, b, pl.ds(a * rows, rows)],
                buffer_ref.at[owner, pl.ds(pl.multiple_of(rank * rows, rows), rows)],
                sem.at[p],
            )
        )
        copies[-1].start()
    row = lax.broadcasted_iota(jnp.int32, slot_rows.shape[1:], 0)
    for o in range(peers):
        out = jnp.full(slot_rows.shape[1:], -1, jnp.int32)
        for i in range(CAP):
            out = jnp.where(row == i, held[o * CAP + i], out)
        slot_rows[o] = out.astype(jnp.float32)
    last = pltpu.make_async_copy(slot_rows, buffer_ref.at[:, pl.ds(CAP * rows, extra)], slot_sem)
    last.start()
    for copy in copies:
        copy.wait()
    last.wait()


def output_kernel(source_ref, receivers_ref, out_ref, flat, sems):
    R = source_ref.shape[1]
    blocks = flat.shape[2]

    def body(r, _):
        for b in range(blocks):
            at = slice(b * LANES, (b + 1) * LANES)
            for p in (0, 1):
                flat[0, p, b, pl.ds(r, SUBS, stride=R), :] = source_ref[p, r, :, at]
                flat[1, p, b, pl.ds(r, SUBS, stride=R), :] = receivers_ref[receivers_ref.shape[0] - 1, p, r, :, at]
        return 0

    lax.fori_loop(0, R, body, 0, unroll=4)
    copies = [
        pltpu.make_async_copy(flat.at[:, :, b], out_ref.at[:, :, :, pl.ds(b * LANES, LANES)], sems.at[b])
        for b in range(blocks)
    ]
    for copy in copies:
        copy.start()
    for copy in copies:
        copy.wait()


def volume_kernel(received_any, received_ref, out_ref, slots, sem):
    peers, rows, _ = received_ref.shape
    size = out_ref.shape[1]
    copy = pltpu.make_async_copy(received_any.at[:, pl.ds(CAP * size, rows - CAP * size)], slots, sem)
    copy.start()
    out_ref[...] = jnp.zeros_like(out_ref)
    copy.wait()
    for s in range(peers):
        for i in range(CAP):
            slot = slots[s, i, 0].astype(jnp.int32)

            @pl.when(slot >= 0)
            def _(s=s, i=i, slot=slot):
                out_ref[slot] += received_ref[s, i * size : (i + 1) * size, :]


def shifted(shard, axis, by):
    peers = lax.axis_size(axis)
    return lax.ppermute(shard, axis, [(i, i + by) for i in range(peers - by)])


def swapped(shard, axis, bits):
    return lax.ppermute(shard, axis, [(i, i ^ bits) for i in range(lax.axis_size(axis))])


def local(fields, vel_tiles, tile_ids, orders, term_weights, phase_rates, owners, image_slots):
    axis = "depth"
    peers = lax.axis_size(axis)
    cells_x, cells_y = fields.shape[3:]
    size = vel_tiles.shape[1]
    steps, tiles_x, tiles_y = tile_ids.shape[1:]
    terms = phase_rates.shape[0]
    R = cells_x // SUBS
    f32 = jnp.float32

    source_up = shifted(fields[0, 0], axis, 1)
    receiver_up = shifted(fields[0, 1], axis, 1)
    small = shifted(jnp.concatenate([tile_ids.reshape(-1), orders.reshape(-1)])[None], axis, 1)
    ids_up = small[:, : tile_ids.size].reshape(tile_ids.shape)
    orders_up = small[:, tile_ids.size :].reshape(orders.shape)

    far = [(4 * i, swapped(vel_tiles, axis, 4 * i)) for i in range(1, peers // 4)]
    near = [(2, swapped(vel_tiles, axis, 2))]
    near += [(k + 2, swapped(v, axis, 2)) for k, v in far]
    held = [(0, vel_tiles)] + far + near
    half = jnp.stack([v for _, v in held])
    other = swapped(half, axis, 1)
    pieces = [[k for k, _ in held], [k ^ 1 for k, _ in held]]

    blocks = cells_y // LANES
    assert size == LANES and cells_x % SUBS == 0 and cells_y % LANES == 0

    def level(planes):
        return pltpu.VMEM((planes, R + 2, SUBS, cells_y), f32)

    def flat(planes):
        return [pltpu.VMEM((planes, blocks, cells_x, LANES), f32), pltpu.SemaphoreType.DMA((blocks,))]

    coefs, image = pl.pallas_call(
        partial(coefs_kernel, axis, pieces),
        out_shape=(
            jax.ShapeDtypeStruct((TICKS, steps, 2 * terms, R, SUBS, cells_y), f32),
            jax.ShapeDtypeStruct((steps, R, SUBS, cells_y), f32),
        ),
        in_specs=[SMEM] * 6 + [ANY] * 3,
        out_specs=(VMEM, VMEM),
        scratch_shapes=[
            pltpu.VMEM((peers * vel_tiles.shape[0], size, size), f32),
            pltpu.VMEM((blocks, cells_x, LANES), f32),
            pltpu.SemaphoreType.DMA((peers,)),
        ]
        + flat(4)
        + [level(4)] * terms,
        compiler_params=PARAMS,
        name="coefs_and_first_tick",
    )(
        tile_ids, orders, ids_up, orders_up, term_weights, phase_rates, half, other,
        fields.reshape(4, cells_x, cells_y),
    )
    receivers = pl.pallas_call(
        receiver_kernel,
        out_shape=jax.ShapeDtypeStruct((steps, 2, R, SUBS, cells_y), f32),
        in_specs=[ANY, VMEM],
        out_specs=VMEM,
        scratch_shapes=flat(2) + [level(2)] * terms,
        compiler_params=PARAMS,
        name="receiver_ticks",
    )(receiver_up, coefs)
    extra = SUBS
    buffer, source = pl.pallas_call(
        source_kernel,
        out_shape=(
            jax.ShapeDtypeStruct((peers, CAP * size + extra, size), f32),
            jax.ShapeDtypeStruct((2, R, SUBS, cells_y), f32),
        ),
        in_specs=[ANY] + [VMEM] * 3 + [SMEM] * 2,
        out_specs=(ANY, VMEM),
        scratch_shapes=[
            pltpu.VMEM((steps, blocks, cells_x, LANES), f32),
            pltpu.VMEM((peers, extra, size), f32),
            pltpu.SMEM((peers * CAP,), jnp.int32),
            pltpu.SemaphoreType.DMA((steps * tiles_x * tiles_y,)),
            pltpu.SemaphoreType.DMA,
        ]
        + flat(2)
        + [level(2)] * terms,
        compiler_params=PARAMS,
        name="source_ticks_and_seats",
    )(source_up, coefs, receivers, image, owners, image_slots)
    received = lax.all_to_all(buffer, axis, split_axis=0, concat_axis=0, tiled=True)
    wavefields = pl.pallas_call(
        output_kernel,
        out_shape=jax.ShapeDtypeStruct((2, 2, cells_x, cells_y), f32),
        in_specs=[VMEM, VMEM],
        out_specs=ANY,
        scratch_shapes=[pltpu.VMEM((2, 2, blocks, cells_x, LANES), f32), pltpu.SemaphoreType.DMA((blocks,))],
        compiler_params=PARAMS,
        name="wavefields",
    )(source, receivers)
    volume = pl.pallas_call(
        volume_kernel,
        out_shape=jax.ShapeDtypeStruct((IMG_SLOTS, size, size), f32),
        in_specs=[ANY, VMEM],
        out_specs=VMEM,
        scratch_shapes=[pltpu.SMEM((peers, extra, size), f32), pltpu.SemaphoreType.DMA],
        compiler_params=PARAMS,
        name="image_volume",
    )(received, received)
    return volume, wavefields[None]


def solution(mesh):
    placed = (
        P(("groups", "depth"), None, None, None, None),
        P(("groups", "depth"), None, None),
        P(("groups", "depth"), None, None, None),
        P(("groups", "depth"), None),
        P(),
        P(),
        P(("groups", "depth"), None),
        P(("groups", "depth"), None),
    )
    return jax.shard_map(
        local,
        mesh=mesh,
        in_specs=placed,
        out_specs=(
            P(("groups", "depth"), None, None),
            P(("groups", "depth"), None, None, None, None),
        ),
        check_vma=False,
    )
```

time: 481 us -> 262 us (0.54); the launches traced: 473 us -> 261 us
  other arithmetic: 303 us -> 0.08 us
  Pallas kernels: 0 us -> 154 us
  loops' own time: 32.3 us -> 0 us
  between operations: 16.5 us -> 0.82 us
  local copies, waits for them, and re-layouts: 18.8 us -> 7.61 us
  starting transfers between devices: 13.5 us -> 22.9 us
  waiting for transfers between devices: 83.3 us -> 75 us
  matrix products: 4.94 us -> 0 us
    another operation x25 -> x0, other arithmetic: 206 us -> none  [the longest x24 205 us: rotate_add(): return jnp.stack(pieces_out)]
    pallas_call x0 -> x5, Pallas kernels: none -> 154 us  [the longest x1 51.6 us: local(): pl.pallas_call(source_kernel, out_shape=(jax.ShapeDtypeStruct((peers, CAP...]
    sub x17 -> x0, other arithmetic: 54.3 us -> none  [the longest x16 54.3 us: advance(): series_term = 2.0 * mcclellan(current) - previous]
    add x10 -> x0, other arithmetic: 38.4 us -> none  [the longest x8 34.1 us: mcclellan(): return -0.5 * fields_in + 0.25 * beside + 0.125 * corner]
    all_gather x1 -> x0, waiting for transfers between devices: 37.9 us -> none  [local(): library = lax.all_gather(vel_tiles, 'depth', axis=0, tiled=True)]
    another operation x8 -> x0, loops' own time: 32.3 us -> none  [stepped(): return lax.switch(order_now - 1, branches, wave_state, slowness_now)]
    ppermute x2 -> x11, waiting for transfers between devices: 0.01 us -> 31.5 us  [the longest x3 17.5 us: shifted(): return lax.ppermute(shard, axis, [(i, i + by) for i in range(peers - by)])]
    ppermute x2 -> x11, starting transfers between devices: 3.84 us -> 14.6 us  [the longest x3 9.04 us: shifted(): return lax.ppermute(shard, axis, [(i, i + by) for i in range(peers - by)])]
  transfers between devices with their start and end apart: 5 -> 12, of which waited for: 2 -> 6; matrix products, arithmetic and copies ran while one was open for 52% -> 2% of each run, Pallas kernels for 0% -> 38%
where the time goes in v1:
time: 262 us; the launch traced here: 261 us
  Pallas kernels  154 us (59%)
  waiting for transfers between devices  75 us (29%)
  starting transfers between devices  22.9 us (9%)
  local copies, waits for them, and re-layouts  7.61 us (3%)
    pallas_call x1, Pallas kernels, local(): pl.pallas_call(source_kernel, out_shape=(jax.ShapeDtypeStruct((peers, CAP...  51.6 us
    pallas_call x1, Pallas kernels, local(): pl.pallas_call(receiver_kernel, out_shape=jax.ShapeDtypeStruct((steps, 2,...  49.2 us
    pallas_call x1, Pallas kernels, local(): pl.pallas_call(partial(coefs_kernel, axis, pieces), out_shape=(jax.ShapeD...  43.8 us
    all_to_all x1, waiting for transfers between devices, local(): lax.all_to_all(buffer, axis, split_axis=0, concat_axis=0, tiled=True)  43.5 us
    ppermute x3, waiting for transfers between devices, shifted(): return lax.ppermute(shard, axis, [(i, i + by) for i in range(peers - by)])  17.5 us
    ppermute x8, waiting for transfers between devices, swapped(): lax.ppermute(shard, axis, [(i, i ^ bits) for i in range(lax.axis_size(axi...  14.1 us
    ppermute x3, starting transfers between devices, shifted(): return lax.ppermute(shard, axis, [(i, i + by) for i in range(peers - by)])  9.04 us
    all_to_all x1, starting transfers between devices, local(): lax.all_to_all(buffer, axis, split_axis=0, concat_axis=0, tiled=True)  8.23 us
  transfers between devices with their start and end apart: 12, of which 6 were waited for; matrix products, arithmetic and copies ran while one was open for 2% of the time, Pallas kernels for 38%

profile of v1, /device:TPU:15, one launch (start us, length us, event | category | flops | bytes accessed | tf_op | source)
XLA Modules:
  0.0 260.9 jit_solution(6740783803744144848)
XLA Ops:
  0.6 2.4 collective-permute-start.3
  3.0 0.2 collective-permute-start.2
  3.2 0.2 collective-permute-start.5
  3.4 0.2 collective-permute-start.4
  3.6 0.9 bitcast_dynamic-update-slice_fusion.7
  4.5 5.2 %collective-permute-done.3 = f32[2,128,128]{2,1,0:T(8,128)S(1)} collective-permute-done((f32[2,128,128]{2,1,0:T(8,128)}, f32[2,128,128]{2,1,0:T(8,128)S(1)}, u32[]{:S(2)}, u32[]{:S(2)}) %collective-permute-start.3) | collective-permute-done | bytes 131104 | tf_op jit(solution)/shard_map/ppermute | solution.py:396
  9.8 0.2 collective-permute-start.7
  10.0 0.0 collective-permute-done.2
  10.0 1.2 collective-permute-start.6
  11.3 3.6 %collective-permute-done.4 = f32[2,128,128]{2,1,0:T(8,128)S(1)} collective-permute-done((f32[2,128,128]{2,1,0:T(8,128)}, f32[2,128,128]{2,1,0:T(8,128)S(1)}, u32[]{:S(2)}, u32[]{:S(2)}) %collective-permute-start.4) | collective-permute-done | bytes 131104 | tf_op jit(solution)/shard_map/ppermute | solution.py:396
  14.9 0.2 collective-permute-start.8
  15.1 0.0 collective-permute-done.5
  15.2 1.5 collective-permute-done.6
  16.7 0.0 collective-permute-done.7
  16.7 3.7 %collective-permute-done.8 = f32[2,128,128]{2,1,0:T(8,128)S(1)} collective-permute-done((f32[2,128,128]{2,1,0:T(8,128)S(1)}, f32[2,128,128]{2,1,0:T(8,128)S(1)}, u32[]{:S(2)}, u32[]{:S(2)}) %collective-permute-start.8) | collective-permute-done | bytes 131104 | tf_op jit(solution)/shard_map/ppermute | solution.py:396
  20.4 0.0 copy-start.1
  20.5 0.0 copy-start.4
  20.5 0.0 copy-start.5
  20.5 0.9 collective-permute-start.9
  21.4 2.7 %slice_bitcast_fusion = (f32[2,512,256]{2,1,0:T(8,128)}, f32[2,512,256]{2,1,0:T(8,128)S(1)}) fusion(f32[1,2,2,512,256]{4,3,2,1,0:T(8,128)} %param.8), kind=kLoop, calls=%fused_computation | loop fusion | bytes 4194304 | tf_op jit(solution)/shard_map/squeeze | solution.py:410
  24.1 0.0 copy-done.1
  24.1 3.6 %collective-permute-start.10 = (f32[2,512,256]{2,1,0:T(8,128)}, f32[2,512,256]{2,1,0:T(8,128)S(1)}, u32[]{:S(2)}, u32[]{:S(2)}) collective-permute-start(f32[2,512,256]{2,1,0:T(8,128)} %get-tuple-element.10), channel_id=1, source_target_pairs={{0,1},{1,2},{2,3},{3,4},{4,5},{5,6},{6,7},{7,8},{8,9},{9,10},{10,1... | collective-permute-start | bytes 3145736 | tf_op jit(solution)/shard_map/ppermute | solution.py:392
  27.7 2.1 collective-permute-start
  29.8 0.0 copy-done.4
  29.9 0.1 copy.13.ids_ref
  30.0 0.0 copy-start.3
  30.0 0.1 reshape.16
  30.0 0.0 copy-done.5
  30.0 0.1 add_bitcast_fusion
  30.1 3.3 %collective-permute-start.1 = (s32[1,18]{1,0:T(1,128)S(1)}, s32[1,18]{1,0:T(1,128)S(1)}, u32[]{:S(2)}, u32[]{:S(2)}) collective-permute-start(s32[1,18]{1,0:T(1,128)S(1)} %add_bitcast_fusion), channel_id=1, source_target_pairs={{0,1},{1,2},{2,3},{3,4},{4,5},{5,6},{6,7},{7,8},{8,9},{9,10},{10,1... | collective-permute-start | bytes 224 | tf_op jit(solution)/shard_map/ppermute | solution.py:392
  33.5 17.5 %collective-permute-done.1 = s32[1,18]{1,0:T(1,128)S(1)} collective-permute-done((s32[1,18]{1,0:T(1,128)S(1)}, s32[1,18]{1,0:T(1,128)S(1)}, u32[]{:S(2)}, u32[]{:S(2)}) %collective-permute-start.1) | collective-permute-done | bytes 104 | tf_op jit(solution)/shard_map/ppermute | solution.py:392
  51.0 0.7 reshape.18.ids_up_ref
  51.6 0.7 slice.14.orders_up_ref
  52.3 0.0 collective-permute-done.9.rest_1_
  52.3 0.0 copy-done.3
  52.3 43.8 %coefs_and_first_tick.1 = (f32[2,2,8,64,8,256]{5,4,3,2,1,0:T(8,128)}, f32[2,64,8,256]{3,2,1,0:T(8,128)}) custom-call(s32[1,2,4,2]{3,2,1,0:T(4,128)} %copy-done.3, s32[1,2]{1,0:T(1,128)} %orders_ref.1, s32[1,2,4,2]{3,2,1,0:T(4,128)} %reshape.18.ids_up_ref, s32[1,2]{1,0:T(1,128)} %slice.14.orders_up_ref, f32[3]{0:T(128)} %weights_ref.1, f32[4]{0:T(128)} %rates_ref.1, ...), custom_call_target="tpu_custom_call" | custom-call | tf_op jit(solution)/shard_map/coefs_and_first_tick/pallas_call | solution.py:432
  96.1 0.0 collective-permute-done.10.fields_ref
  96.1 0.0 copy-start.2
  96.1 1.0 copy-done.2
  97.1 49.2 %receiver_ticks.1.receivers_ref = f32[2,2,64,8,256]{4,3,2,1,0:T(8,128)} custom-call(f32[2,512,256]{2,1,0:T(8,128)} %copy-done.2, f32[2,2,8,64,8,256]{5,4,3,2,1,0:T(8,128)} %get-tuple-element.6.coefs_ref), custom_call_target="tpu_custom_call" | custom-call | tf_op jit(solution)/shard_map/receiver_ticks/pallas_call | solution.py:453
  146.3 0.0 collective-permute-done.fields_ref
  146.3 51.6 %source_ticks_and_seats.1 = (f32[16,264,128]{2,1,0:T(8,128)}, f32[2,64,8,256]{3,2,1,0:T(8,128)}) custom-call(f32[2,512,256]{2,1,0:T(8,128)} %collective-permute-done.fields_ref, f32[2,2,8,64,8,256]{5,4,3,2,1,0:T(8,128)} %get-tuple-element.6.coefs_ref, f32[2,2,64,8,256]{4,3,2,1,0:T(8,128)} %receiver_ticks.1.receivers_ref, ...), custom_call_target="tpu_custom_call" | custom-call | tf_op jit(solution)/shard_map/source_ticks_and_seats/pallas_call | solution.py:463
  197.9 8.2 %all-to-all-start = ((f32[16,264,128]{2,1,0:T(8,128)}), f32[16,264,128]{2,1,0:T(8,128)S(1)}, u32[]{:S(2)}, u32[]{:S(2)}) async-start(f32[16,264,128]{2,1,0:T(8,128)} %get-tuple-element.8), calls=%async_computation | async-start | bytes 4325376 | tf_op jit(solution)/shard_map/all_to_all | solution.py:483
  206.1 5.3 %wavefields.1 = f32[2,2,512,256]{3,2,1,0:T(8,128)} custom-call(f32[2,64,8,256]{3,2,1,0:T(8,128)} %get-tuple-element.9.source_ref, f32[2,2,64,8,256]{4,3,2,1,0:T(8,128)} %receiver_ticks.1.receivers_ref), custom_call_target="tpu_custom_call" | custom-call | tf_op jit(solution)/shard_map/wavefields/pallas_call | solution.py:484
  211.5 43.5 %all-to-all-done.received_any.received_ref = f32[16,264,128]{2,1,0:T(8,128)S(1)} async-done(((f32[16,264,128]{2,1,0:T(8,128)}), f32[16,264,128]{2,1,0:T(8,128)S(1)}, u32[]{:S(2)}, u32[]{:S(2)}) %all-to-all-start) | async-done | bytes 2162720 | tf_op jit(solution)/shard_map/all_to_all | solution.py:483
  255.0 0.0 copy-start
  255.0 1.3 copy-done
  256.3 4.6 %image_volume.1 = f32[8,128,128]{2,1,0:T(8,128)} custom-call(f32[16,264,128]{2,1,0:T(8,128)} %copy-done, f32[16,264,128]{2,1,0:T(8,128)} %copy-done), custom_call_target="tpu_custom_call" | custom-call | tf_op jit(solution)/shard_map/image_volume/pallas_call | solution.py:493
  (8 shorter events, 0.1 us)
Async XLA Ops:
  0.6 9.2 %collective-permute-start.3 = (f32[2,128,128]{2,1,0:T(8,128)}, f32[2,128,128]{2,1,0:T(8,128)S(1)}, u32[]{:S(2)}, u32[]{:S(2)}) collective-permute-start(f32[2,128,128]{2,1,0:T(8,128)} %param.9), channel_id=1, source_target_pairs={{0,8},{1,9},{2,10},{3,11},{4,12},{5,13},{6,14},{7,15},{8,0},{9,1},... | collective-permute-start | bytes 393224 | tf_op jit(solution)/shard_map/ppermute | solution.py:396
  3.0 7.0 %collective-permute-start.2 = (f32[2,128,128]{2,1,0:T(8,128)}, f32[2,128,128]{2,1,0:T(8,128)S(1)}, u32[]{:S(2)}, u32[]{:S(2)}) collective-permute-start(f32[2,128,128]{2,1,0:T(8,128)} %param.9), channel_id=1, source_target_pairs={{0,4},{1,5},{2,6},{3,7},{4,0},{5,1},{6,2},{7,3},{8,12},{9,13},{10,... | collective-permute-start | bytes 393224 | tf_op jit(solution)/shard_map/ppermute | solution.py:396
  3.2 12.0 %collective-permute-start.5 = (f32[2,128,128]{2,1,0:T(8,128)}, f32[2,128,128]{2,1,0:T(8,128)S(1)}, u32[]{:S(2)}, u32[]{:S(2)}) collective-permute-start(f32[2,128,128]{2,1,0:T(8,128)} %param.9), channel_id=1, source_target_pairs={{0,2},{1,3},{2,0},{3,1},{4,6},{5,7},{6,4},{7,5},{8,10},{9,11},{10,... | collective-permute-start | bytes 393224 | tf_op jit(solution)/shard_map/ppermute | solution.py:396
  3.4 11.4 %collective-permute-start.4 = (f32[2,128,128]{2,1,0:T(8,128)}, f32[2,128,128]{2,1,0:T(8,128)S(1)}, u32[]{:S(2)}, u32[]{:S(2)}) collective-permute-start(f32[2,128,128]{2,1,0:T(8,128)} %param.9), channel_id=1, source_target_pairs={{0,12},{1,13},{2,14},{3,15},{4,8},{5,9},{6,10},{7,11},{8,4},{9,5},... | collective-permute-start | bytes 393224 | tf_op jit(solution)/shard_map/ppermute | solution.py:396
  9.8 6.9 %collective-permute-start.7 = (f32[2,128,128]{2,1,0:T(8,128)S(1)}, f32[2,128,128]{2,1,0:T(8,128)S(1)}, u32[]{:S(2)}, u32[]{:S(2)}) collective-permute-start(f32[2,128,128]{2,1,0:T(8,128)S(1)} %collective-permute-done.3), channel_id=1, source_target_pairs={{0,2},{1,3},{2,0},{3,1},{4,6},{5,7},{6,4},{7,5},{8,10},{9,11},{10,... | collective-permute-start | bytes 393224 | tf_op jit(solution)/shard_map/ppermute | solution.py:396
  10.0 6.6 %collective-permute-start.6 = (f32[2,128,128]{2,1,0:T(8,128)S(1)}, f32[2,128,128]{2,1,0:T(8,128)S(1)}, u32[]{:S(2)}, u32[]{:S(2)}) collective-permute-start(f32[2,128,128]{2,1,0:T(8,128)S(1)} %collective-permute-done.2), channel_id=1, source_target_pairs={{0,2},{1,3},{2,0},{3,1},{4,6},{5,7},{6,4},{7,5},{8,10},{9,11},{10,... | collective-permute-start | bytes 393224 | tf_op jit(solution)/shard_map/ppermute | solution.py:396
  14.9 5.6 %collective-permute-start.8 = (f32[2,128,128]{2,1,0:T(8,128)S(1)}, f32[2,128,128]{2,1,0:T(8,128)S(1)}, u32[]{:S(2)}, u32[]{:S(2)}) collective-permute-start(f32[2,128,128]{2,1,0:T(8,128)S(1)} %collective-permute-done.4), channel_id=1, source_target_pairs={{0,2},{1,3},{2,0},{3,1},{4,6},{5,7},{6,4},{7,5},{8,10},{9,11},{10,... | collective-permute-start | bytes 393224 | tf_op jit(solution)/shard_map/ppermute | solution.py:396
  20.4 3.7 %copy-start.1 = (f32[8,2,128,128]{3,2,1,0:T(8,128)}, f32[8,2,128,128]{3,2,1,0:T(8,128)S(1)}, u32[]{:S(2)}) copy-start(f32[8,2,128,128]{3,2,1,0:T(8,128)S(1)} %bitcast_dynamic-update-slice_fusion.rest_0_) | copy-start | bytes 3145732
  20.5 9.4 %copy-start.4 = (s32[1,2,4,2]{2,3,1,0:T(2,128)S(1)}, s32[1,2,4,2]{2,3,1,0:T(2,128)}, u32[]{:S(2)}) copy-start(s32[1,2,4,2]{2,3,1,0:T(2,128)} %param.10) | copy-start | bytes 196
  20.5 9.6 %copy-start.5 = (s32[1,2]{1,0:T(1,128)S(1)}, s32[1,2]{1,0:T(1,128)}, u32[]{:S(2)}) copy-start(s32[1,2]{1,0:T(1,128)} %orders_ref.1) | copy-start | bytes 28
  20.5 31.8 %collective-permute-start.9 = (f32[8,2,128,128]{3,2,1,0:T(8,128)S(1)}, f32[8,2,128,128]{3,2,1,0:T(8,128)}, u32[]{:S(2)}, u32[]{:S(2)}) collective-permute-start(f32[8,2,128,128]{3,2,1,0:T(8,128)S(1)} %bitcast_dynamic-update-slice_fusion.rest_0_), channel_id=1, source_target_pairs={{0,1},{1,0},{2,3},{3,2},{4,5},{5,4},{6,7},{7,6},{8,9},{9,8},{10,11... | collective-permute-start | bytes 3145736 | tf_op jit(solution)/shard_map/ppermute | solution.py:396
  24.1 72.0 %collective-permute-start.10 = (f32[2,512,256]{2,1,0:T(8,128)}, f32[2,512,256]{2,1,0:T(8,128)S(1)}, u32[]{:S(2)}, u32[]{:S(2)}) collective-permute-start(f32[2,512,256]{2,1,0:T(8,128)} %get-tuple-element.10), channel_id=1, source_target_pairs={{0,1},{1,2},{2,3},{3,4},{4,5},{5,6},{6,7},{7,8},{8,9},{9,10},{10,1... | collective-permute-start | bytes 3145736 | tf_op jit(solution)/shard_map/ppermute | solution.py:392
  27.7 118.5 %collective-permute-start = (f32[2,512,256]{2,1,0:T(8,128)S(1)}, f32[2,512,256]{2,1,0:T(8,128)}, u32[]{:S(2)}, u32[]{:S(2)}) collective-permute-start(f32[2,512,256]{2,1,0:T(8,128)S(1)} %get-tuple-element.11), channel_id=1, source_target_pairs={{0,1},{1,2},{2,3},{3,4},{4,5},{5,6},{6,7},{7,8},{8,9},{9,10},{10,1... | collective-permute-start | bytes 3145736 | tf_op jit(solution)/shard_map/ppermute | solution.py:392
  30.0 22.4 %copy-start.3 = (s32[1,2,4,2]{3,2,1,0:T(4,128)}, s32[1,2,4,2]{3,2,1,0:T(4,128)S(1)}, u32[]{:S(2)}) copy-start(s32[1,2,4,2]{3,2,1,0:T(4,128)S(1)} %copy.13.ids_ref) | copy-start | bytes 196
  30.1 20.8 %collective-permute-start.1 = (s32[1,18]{1,0:T(1,128)S(1)}, s32[1,18]{1,0:T(1,128)S(1)}, u32[]{:S(2)}, u32[]{:S(2)}) collective-permute-start(s32[1,18]{1,0:T(1,128)S(1)} %add_bitcast_fusion), channel_id=1, source_target_pairs={{0,1},{1,2},{2,3},{3,4},{4,5},{5,6},{6,7},{7,8},{8,9},{9,10},{10,1... | collective-permute-start | bytes 224 | tf_op jit(solution)/shard_map/ppermute | solution.py:392
  96.1 1.0 copy-start.2
  197.9 57.1 %all-to-all-start = ((f32[16,264,128]{2,1,0:T(8,128)}), f32[16,264,128]{2,1,0:T(8,128)S(1)}, u32[]{:S(2)}, u32[]{:S(2)}) async-start(f32[16,264,128]{2,1,0:T(8,128)} %get-tuple-element.8), calls=%async_computation | async-start | bytes 4325376 | tf_op jit(solution)/shard_map/all_to_all | solution.py:483
  255.0 1.3 copy-start

commit v2 on v1

v2 whole, which is shorter than its diff:
```python
from functools import partial

import jax
import jax.numpy as jnp
import numpy as np
from jax import lax
from jax.experimental import pallas as pl
from jax.experimental.pallas import tpu as pltpu
from jax.sharding import PartitionSpec as P

TICKS = 2
CAP = 2
IMG_SLOTS = 8
LANES = 128
SUBS = 8
VMEM = pl.BlockSpec(memory_space=pltpu.VMEM)
SMEM = pl.BlockSpec(memory_space=pltpu.SMEM)
ANY = pl.BlockSpec(memory_space=pl.ANY)
PARAMS = pltpu.CompilerParams(vmem_limit_bytes=18 * 2**20)


def in_vmem(x):
    return pltpu.with_memory_space_constraint(x, pltpu.VMEM)


def in_powers(terms):
    rows = np.zeros((terms, terms))
    polys = [np.array([1.0]), np.array([-1.0, 1.0])]
    while len(polys) < terms:
        grown = np.convolve(polys[-1], [-2.0, 2.0])
        grown[: len(polys[-2])] -= polys[-2]
        polys.append(grown)
    for k in range(terms):
        rows[k, : len(polys[k])] = polys[k] / 8.0 ** np.arange(len(polys[k]))
    return rows


def fitted():
    nodes = 0.25 * (1.0 - np.cos((np.arange(400) + 0.5) * np.pi / 400)) / 2.0
    r = np.sqrt(nodes)
    sine = np.polynomial.chebyshev.Chebyshev.fit(nodes, np.sqrt(2.0) * np.sin(np.pi * r) / r, 4)
    cosine = np.polynomial.chebyshev.Chebyshev.fit(nodes, np.sqrt(2.0) * np.cos(np.pi * r), 4)
    make = np.polynomial.polynomial.Polynomial
    return (
        [float(c) for c in sine.convert(kind=make).coef],
        [float(c) for c in cosine.convert(kind=make).coef],
    )


SINE, COSINE = fitted()


def horner(x, coefs):
    out = coefs[-1] * x + coefs[-2]
    for c in coefs[-3::-1]:
        out = out * x + c
    return out


def cos_sin(turns):
    r = turns - jnp.round(turns)
    r2 = r * r
    s = r * horner(r2, SINE)
    c = horner(r2, COSINE)
    return 1.0 - s * s, s * c


def lane_sums(cells_y, terms):
    one = 2 * np.eye(cells_y) + np.eye(cells_y, k=1) + np.eye(cells_y, k=-1)
    side = np.concatenate([np.linalg.matrix_power(one, k) for k in range(1, terms)], 1)
    return jnp.asarray(np.concatenate([side, side], 0), jnp.bfloat16)


class Rows:
    def __init__(self, ref, edge, first=0, planes=None):
        self.ref, self.edge, self.first = ref, edge, first
        self.planes = ref.shape[0] if planes is None else planes
        self.R = ref.shape[1] - 2 * edge
        self.blocks = ref.shape[3] // LANES

    def get(self, p, r, b):
        return self.ref[self.first + p, r + self.edge, :, b * LANES : (b + 1) * LANES]

    def put(self, p, r, b, value):
        self.ref[self.first + p, r + self.edge, :, b * LANES : (b + 1) * LANES] = value

    def halo(self):
        sub = lax.broadcasted_iota(jnp.int32, (SUBS, LANES), 0)
        R = self.R
        for p in range(self.planes):
            for b in range(self.blocks):
                for h in range(1, self.edge + 1):
                    low = 0.0 if h == 1 else -self.get(p, h - 2, b)
                    self.put(p, -h, b, jnp.where(sub == 0, low, pltpu.roll(self.get(p, R - h, b), 1, 0)))
                    high = 0.0 if h == 1 else -self.get(p, R + 1 - h, b)
                    turned = pltpu.roll(self.get(p, h - 1, b), SUBS - 1, 0)
                    self.put(p, R - 1 + h, b, jnp.where(sub == SUBS - 1, high, turned))


def along_y(state, sides_ref, sums):
    rows, cells_y = state.ref.shape[1], state.ref.shape[3]
    side = sides_ref[...]
    for p in range(state.planes):
        here = state.ref[state.first + p].reshape(rows * SUBS, cells_y)
        high = here.astype(jnp.bfloat16)
        low = (here - high.astype(jnp.float32)).astype(jnp.bfloat16)
        out = jnp.dot(jnp.concatenate([high, low], 1), side, preferred_element_type=jnp.float32)
        for k in range(sums.shape[0]):
            sums[k, p] = out[:, k * cells_y : (k + 1) * cells_y].reshape(rows, SUBS, cells_y)


def chained(carry, value, length):
    kept = []
    for c in carry:
        kept.append(value)
        value = value + c
    if len(carry) < length:
        kept.append(value)
    return kept, value


def depth_step(state, sums, coefs, sign, emit, unroll=8):
    terms, edge = sums.shape[0] + 1, state.edge
    for b in range(state.blocks):
        at = slice(b * LANES, (b + 1) * LANES)

        def body(r, carry):
            kept, total = [], [None, None]
            for k in range(terms):
                if k == 0:
                    re, im = state.get(0, r, b), state.get(1, r, b)
                else:
                    both = []
                    for p in (0, 1):
                        new, value = chained(
                            carry[2 * (k - 1) + p], sums[k - 1, p, r + edge + k, :, at], 2 * k
                        )
                        kept.append(new)
                        both.append(value)
                    re, im = both
                a, s = coefs[2 * k, r, :, at], coefs[2 * k + 1, r, :, at]
                x, y, u, v = a * re, a * im, s * im, s * re
                x, y = (x - u, y + v) if sign > 0 else (x + u, y - v)
                total = [x, y] if k == 0 else [total[0] + x, total[1] + y]
            emit(r, b, *total)
            return kept

        start = []
        for k in range(1, terms):
            for p in (0, 1):
                chain = []
                for r in range(-k, k):
                    chain, _ = chained(chain, sums[k - 1, p, r + edge, :, at], 2 * k)
                start.append(chain)
        lax.fori_loop(0, state.R, body, start, unroll=unroll)


def fetch(field_ref, flat, sem):
    copies = [
        pltpu.make_async_copy(field_ref.at[:, :, pl.ds(b * LANES, LANES)], flat.at[:, b], sem.at[b])
        for b in range(flat.shape[1])
    ]
    for copy in copies:
        copy.start()
    return copies


def load_rows(flat, state):
    def body(r, _):
        for p in range(state.planes):
            for b in range(state.blocks):
                state.put(p, r, b, flat[state.first + p, b, pl.ds(r, SUBS, stride=state.R), :])
        return 0

    lax.fori_loop(0, state.R, body, 0, unroll=4)
    state.halo()


def stack_kernel(*refs):
    parts, (ext, out, rows, sems) = refs[:-4], refs[-4:]
    edge = (ext.shape[1] - rows.shape[1]) // 2
    copies = [pltpu.make_async_copy(part, out.at[i], sems.at[i]) for i, part in enumerate(parts)]
    copies.append(
        pltpu.make_async_copy(
            ext.at[pl.ds(2, 2), pl.ds(edge, rows.shape[1])], rows, sems.at[len(parts)]
        )
    )
    for copy in copies:
        copy.start()
    for copy in copies:
        copy.wait()


def along_kernel(fields_ref, sides_ref, ids_ref, orders_ref, ext, sums, flat, flat_sem):
    for copy in fetch(fields_ref, flat, flat_sem):
        copy.wait()
    edge = sums.shape[1]
    load_rows(flat, Rows(ext, edge))
    for pair in (0, 1):
        along_y(Rows(ext, edge, 2 * pair, 2), sides_ref, sums.at[pair])


def series(slow, orders_ref, weights_ref, rates_ref, coefs_ref, j):
    terms = rates_ref.shape[0]
    powers = in_powers(terms)
    R = coefs_ref.shape[2]
    total = weights_ref[0]
    for k in range(1, terms - 1):
        total = total + weights_ref[k]
    base = [1.0 - total] + [weights_ref[k] for k in range(terms - 1)]
    turn = [rates_ref[k] * (0.5 / np.pi) for k in range(terms)]
    scale = [jnp.where(k <= orders_ref[0, j], base[k], 0.0) for k in range(terms)]

    def body(r, _):
        for b in range(slow.shape[0]):
            at = slice(b * LANES, (b + 1) * LANES)
            here = slow[b, pl.ds(r, SUBS, stride=R), :]
            parts = []
            for k in range(terms):
                c, s = cos_sin(here * turn[k])
                parts.append((c * scale[k], s * scale[k]))
            for m in range(terms):
                for i in (0, 1):
                    out = None
                    for k in range(m, terms):
                        w = float(powers[k, m])
                        term = parts[k][i] if abs(w) == 1.0 else parts[k][i] * abs(w)
                        if out is None:
                            out = term if w > 0 else -term
                        else:
                            out = out + term if w > 0 else out - term
                    coefs_ref[j, 2 * m + i, r, :, at] = out
        return 0

    lax.fori_loop(0, R, body, 0, unroll=4)


def first_source_kernel(
    axis, pieces, ids_ref, orders_ref, ids_up_ref, weights_ref, rates_ref, sides_ref, ext_in, sums_in, *rest
):
    tiles, (coefs_ref, states_ref, out_ref, slow_up), (library, slow, sems, out_sem, ext, sums) = (
        rest[: len(pieces)],
        rest[len(pieces) : len(pieces) + 4],
        rest[len(pieces) + 4 :],
    )
    per = library.shape[0] // sum(len(at) for at in pieces)
    copies = []
    for ref, at in zip(tiles, pieces):
        for i, k in enumerate(at):
            copies.append(
                pltpu.make_async_copy(ref.at[i], library.at[pl.ds(k * per, per)], sems.at[len(copies)])
            )
            copies[-1].start()
    for copy in copies:
        copy.wait()
    me = lax.axis_index(axis)
    steps, tiles_x, tiles_y = ids_ref.shape[-3:]
    size = library.shape[1]
    for j in range(steps):
        for a in range(tiles_x):
            for b in range(tiles_y):
                for ids, to in ((ids_ref, slow), (ids_up_ref, slow_up.at[j])):
                    tile = ids[0, j, a, b]
                    to[b, a * size : (a + 1) * size, :] = library[(tile // per ^ me) * per + tile % per]
        series(slow, orders_ref, weights_ref, rates_ref, coefs_ref, j)
        edge = sums.shape[0]
        state = Rows(ext_in if j == 0 else ext, edge, 0, 2)
        into = Rows(ext, edge)
        if j:
            state.halo()
            along_y(state, sides_ref, sums)

        def emit(r, b, re, im, j=j, into=into):
            for p, value in enumerate((re, im)):
                states_ref[j, p, r, :, b * LANES : (b + 1) * LANES] = value
                if j + 1 < steps:
                    into.put(p, r, b, value)

        depth_step(state, sums if j else sums_in.at[0], coefs_ref.at[j], 1, emit)
    copy = pltpu.make_async_copy(states_ref.at[steps - 1], out_ref, out_sem)
    copy.start()
    copy.wait()


def first_image_kernel(
    orders_up_ref, weights_ref, rates_ref, slow_up, sides_ref, ext_in, sums_in, coefs_ref, states_ref,
    coefs_up_ref, image_ref, ext, sums
):
    steps = coefs_ref.shape[0]
    edge = sums.shape[0]
    into = Rows(ext, edge)
    for j in range(steps):
        series(slow_up.at[j], orders_up_ref, weights_ref, rates_ref, coefs_up_ref, j)
        state = into if j else Rows(ext_in, edge, 2, 2)
        if j:
            state.halo()
            along_y(state, sides_ref, sums)

        def emit(r, b, re, im, j=j):
            at = slice(b * LANES, (b + 1) * LANES)
            image_ref[j, r, :, at] = re * states_ref[j, 0, r, :, at] + im * states_ref[j, 1, r, :, at]
            if j + 1 < steps:
                into.put(0, r, b, re)
                into.put(1, r, b, im)

        depth_step(state, sums if j else sums_in.at[1], coefs_ref.at[j], -1, emit)


def take_rows(rows_ref, state, sem):
    copy = pltpu.make_async_copy(rows_ref, state.ref.at[:, pl.ds(state.edge, state.R)], sem)
    copy.start()
    copy.wait()
    state.halo()


def receiver_kernel(rows_ref, coefs_up_ref, coefs_ref, sides_ref, states_ref, sem, ext, sums):
    steps = coefs_ref.shape[0]
    state = Rows(ext, sums.shape[0])
    take_rows(rows_ref, state, sem)
    for which, coefs in enumerate((coefs_up_ref, coefs_ref)):
        for j in range(steps):
            final = which == 1 and j == steps - 1

            def emit(r, b, re, im, j=j, which=which, final=final):
                for p, value in enumerate((re, im)):
                    if not final:
                        state.put(p, r, b, value)
                    if which == 1:
                        states_ref[j, p, r, :, b * LANES : (b + 1) * LANES] = value

            along_y(state, sides_ref, sums)
            depth_step(state, sums, coefs.at[j], -1, emit)
            if not final:
                state.halo()


def source_kernel(
    rows_ref, coefs_ref, sides_ref, receivers_ref, image_ref, owners_ref, slots_ref,
    buffer_ref, state_ref, images, slot_rows, held, sem, slot_sem, ext, sums
):
    steps = coefs_ref.shape[0]
    state = Rows(ext, sums.shape[0])
    R = state.R
    take_rows(rows_ref, state, slot_sem)
    for j in range(steps):
        final = j == steps - 1

        def emit(r, b, re, im, j=j, final=final):
            at = slice(b * LANES, (b + 1) * LANES)
            for p, value in enumerate((re, im)):
                if final:
                    state_ref[p, r, :, at] = value
                else:
                    state.put(p, r, b, value)
            images[j, b, pl.ds(r, SUBS, stride=R), :] = (
                image_ref[j, r, :, at]
                + re * receivers_ref[j, 0, r, :, at]
                + im * receivers_ref[j, 1, r, :, at]
            )

        along_y(state, sides_ref, sums)
        depth_step(state, sums, coefs_ref.at[j], 1, emit)
        if not final:
            state.halo()
    size = buffer_ref.shape[2]
    peers = buffer_ref.shape[0]
    extra = slot_rows.shape[1]
    tiles_x, tiles_y = images.shape[2] // size, images.shape[1]
    rows = (buffer_ref.shape[1] - extra) // CAP
    for o in range(peers * CAP):
        held[o] = -1
    copies = []
    for p in range(steps * tiles_x * tiles_y):
        j, a, b = p // (tiles_x * tiles_y), p // tiles_y % tiles_x, p % tiles_y
        owner = owners_ref[0, p]
        rank = jnp.int32(0)
        for before in range(p):
            rank = rank + (owners_ref[0, before] == owner).astype(jnp.int32)
        held[owner * CAP + rank] = slots_ref[0, p]
        copies.append(
            pltpu.make_async_copy(
                images.at[j, b, pl.ds(a * rows, rows)],
                buffer_ref.at[owner, pl.ds(pl.multiple_of(rank * rows, rows), rows)],
                sem.at[p],
            )
        )
        copies[-1].start()
    lane = lax.broadcasted_iota(jnp.int32, slot_rows.shape[1:], 1)
    for o in range(peers):
        out = jnp.full(slot_rows.shape[1:], -1, jnp.int32)
        for i in range(CAP):
            out = jnp.where(lane == i, held[o * CAP + i], out)
        slot_rows[o] = out.astype(jnp.float32)
    last = pltpu.make_async_copy(slot_rows, buffer_ref.at[:, pl.ds(CAP * rows, extra)], slot_sem)
    last.start()
    for copy in copies:
        copy.wait()
    last.wait()


def output_kernel(source_ref, receivers_ref, out_ref, flat, sems):
    R = source_ref.shape[1]
    blocks = flat.shape[2]

    def body(r, _):
        for b in range(blocks):
            at = slice(b * LANES, (b + 1) * LANES)
            for p in (0, 1):
                flat[0, p, b, pl.ds(r, SUBS, stride=R), :] = source_ref[p, r, :, at]
                flat[1, p, b, pl.ds(r, SUBS, stride=R), :] = receivers_ref[receivers_ref.shape[0] - 1, p, r, :, at]
        return 0

    lax.fori_loop(0, R, body, 0, unroll=4)
    copies = [
        pltpu.make_async_copy(flat.at[:, :, b], out_ref.at[:, :, :, pl.ds(b * LANES, LANES)], sems.at[b])
        for b in range(blocks)
    ]
    for copy in copies:
        copy.start()
    for copy in copies:
        copy.wait()


def volume_kernel(received_ref, out_ref, slots, sem):
    peers, rows, _ = received_ref.shape
    size = out_ref.shape[1]
    copy = pltpu.make_async_copy(received_ref.at[:, pl.ds(CAP * size, 1)], slots, sem)
    copy.start()
    out_ref[...] = jnp.zeros_like(out_ref)
    copy.wait()
    for s in range(peers):
        for i in range(CAP):
            slot = slots[s, 0, i].astype(jnp.int32)

            @pl.when(slot >= 0)
            def _(s=s, i=i, slot=slot):
                out_ref[slot] += received_ref[s, i * size : (i + 1) * size, :]


def shifted(shard, axis, by):
    peers = lax.axis_size(axis)
    return lax.ppermute(shard, axis, [(i, i + by) for i in range(peers - by)])


def swapped(shard, axis, bits):
    return lax.ppermute(shard, axis, [(i, i ^ bits) for i in range(lax.axis_size(axis))])


def local(fields, vel_tiles, tile_ids, orders, term_weights, phase_rates, owners, image_slots):
    axis = "depth"
    peers = lax.axis_size(axis)
    cells_x, cells_y = fields.shape[3:]
    size = vel_tiles.shape[1]
    steps, tiles_x, tiles_y = tile_ids.shape[1:]
    terms = phase_rates.shape[0]
    R = cells_x // SUBS
    f32 = jnp.float32

    ids_up = shifted(tile_ids, axis, 1)
    orders_up = shifted(orders, axis, 1)
    far = [(4 * i, swapped(vel_tiles, axis, 4 * i)) for i in range(1, peers // 4)]
    beside = [(2, swapped(vel_tiles, axis, 2))]
    beside += [(k + 2, swapped(v, axis, 2)) for k, v in far]
    held = [(0, vel_tiles)] + far + beside
    blocks = cells_y // LANES
    assert size == LANES and cells_x % SUBS == 0 and cells_y % LANES == 0

    edge = terms - 1
    sides = lane_sums(cells_y, terms)

    def flat(planes):
        return [pltpu.VMEM((planes, blocks, cells_x, LANES), f32), pltpu.SemaphoreType.DMA((blocks,))]

    def work(planes):
        return [
            pltpu.VMEM((planes, R + 2 * edge, SUBS, cells_y), f32),
            pltpu.VMEM((edge, 2, R + 2 * edge, SUBS, cells_y), f32),
        ]

    planes = (R, SUBS, cells_y)
    padded = (R + 2 * edge, SUBS, cells_y)
    call = partial(pl.pallas_call, compiler_params=PARAMS)
    ext, sums = call(
        along_kernel,
        out_shape=(pltpu.VMEM((4,) + padded, f32), pltpu.VMEM((2, edge, 2) + padded, f32)),
        in_specs=[ANY, VMEM, SMEM, SMEM],
        out_specs=(VMEM, VMEM),
        scratch_shapes=flat(4),
        cost_estimate=pl.CostEstimate(flops=2**32, bytes_accessed=2**23, transcendentals=0),
        name="along_y",
    )(fields.reshape(4, cells_x, cells_y), sides, ids_up, orders_up)
    ext, sums = in_vmem(ext), in_vmem(sums)
    half, rows = call(
        stack_kernel,
        out_shape=(
            pltpu.VMEM((len(held),) + vel_tiles.shape, f32),
            pltpu.VMEM((2,) + planes, f32),
        ),
        in_specs=[ANY] * len(held) + [VMEM],
        out_specs=(VMEM, VMEM),
        scratch_shapes=[pltpu.SemaphoreType.DMA((len(held) + 1,))],
        name="stack_tiles",
    )(*[v for _, v in held], ext)
    other = swapped(half, axis, 1)
    pieces = [[k for k, _ in held], [k ^ 1 for k, _ in held]]
    receiver_up = shifted(rows, axis, 1)
    coefs, states, sent, slow_up = call(
        partial(first_source_kernel, axis, pieces),
        out_shape=(
            pltpu.VMEM((steps, 2 * terms) + planes, f32),
            pltpu.VMEM((steps, 2) + planes, f32),
            pltpu.HBM((2,) + planes, f32),
            pltpu.VMEM((steps, blocks, cells_x, LANES), f32),
        ),
        in_specs=[SMEM] * 5 + [VMEM] * 3 + [ANY] * 2,
        out_specs=(VMEM, VMEM, ANY, VMEM),
        scratch_shapes=[
            pltpu.VMEM((peers * vel_tiles.shape[0], size, size), f32),
            pltpu.VMEM((blocks, cells_x, LANES), f32),
            pltpu.SemaphoreType.DMA((peers,)),
            pltpu.SemaphoreType.DMA,
        ]
        + work(2),
        name="first_sources",
    )(tile_ids, orders, ids_up, term_weights, phase_rates, sides, ext, sums, half, other)
    source_up = shifted(sent, axis, 1)
    coefs, states, slow_up = in_vmem(coefs), in_vmem(states), in_vmem(slow_up)
    coefs_up, image = call(
        first_image_kernel,
        out_shape=(
            pltpu.VMEM((steps, 2 * terms) + planes, f32),
            pltpu.VMEM((steps,) + planes, f32),
        ),
        in_specs=[SMEM] * 3 + [VMEM] * 6,
        out_specs=(VMEM, VMEM),
        scratch_shapes=work(2),
        name="first_images",
    )(orders_up, term_weights, phase_rates, slow_up, sides, ext, sums, coefs, states)
    receivers = in_vmem(
        call(
            receiver_kernel,
            out_shape=pltpu.VMEM((steps, 2) + planes, f32),
            in_specs=[ANY] + [VMEM] * 3,
            out_specs=VMEM,
            scratch_shapes=[pltpu.SemaphoreType.DMA] + work(2),
            name="receiver_ticks",
        )(receiver_up, in_vmem(coefs_up), coefs, sides)
    )
    extra = SUBS
    buffer, source = call(
        source_kernel,
        out_shape=(
            pltpu.HBM((peers, CAP * size + extra, size), f32),
            pltpu.HBM((2,) + planes, f32),
        ),
        in_specs=[ANY] + [VMEM] * 4 + [SMEM] * 2,
        out_specs=(ANY, VMEM),
        scratch_shapes=[
            pltpu.VMEM((steps, blocks, cells_x, LANES), f32),
            pltpu.VMEM((peers, extra, size), f32),
            pltpu.SMEM((peers * CAP,), jnp.int32),
            pltpu.SemaphoreType.DMA((steps * tiles_x * tiles_y,)),
            pltpu.SemaphoreType.DMA,
        ]
        + work(2),
        name="source_tick_and_seats",
    )(source_up, coefs, sides, receivers, in_vmem(image), owners, image_slots)
    received = lax.all_to_all(buffer, axis, split_axis=0, concat_axis=0, tiled=True)
    wavefields = pl.pallas_call(
        output_kernel,
        out_shape=jax.ShapeDtypeStruct((2, 2, cells_x, cells_y), f32),
        in_specs=[VMEM, VMEM],
        out_specs=ANY,
        scratch_shapes=[
            pltpu.VMEM((2, 2, blocks, cells_x, LANES), f32),
            pltpu.SemaphoreType.DMA((blocks,)),
        ],
        compiler_params=PARAMS,
        name="wavefields",
    )(source, receivers)
    volume = pl.pallas_call(
        volume_kernel,
        out_shape=jax.ShapeDtypeStruct((IMG_SLOTS, size, size), f32),
        in_specs=[VMEM],
        out_specs=VMEM,
        scratch_shapes=[pltpu.SMEM((peers, 1, size), f32), pltpu.SemaphoreType.DMA],
        compiler_params=PARAMS,
        name="image_volume",
    )(in_vmem(received))
    return volume, wavefields[None]


def solution(mesh):
    placed = (
        P(("groups", "depth"), None, None, None, None),
        P(("groups", "depth"), None, None),
        P(("groups", "depth"), None, None, None),
        P(("groups", "depth"), None),
        P(),
        P(),
        P(("groups", "depth"), None),
        P(("groups", "depth"), None),
    )
    return jax.shard_map(
        local,
        mesh=mesh,
        in_specs=placed,
        out_specs=(
            P(("groups", "depth"), None, None),
            P(("groups", "depth"), None, None, None, None),
        ),
        check_vma=False,
    )
```

time: 262 us -> 131 us (0.50)
  Pallas kernels: 154 us -> 50.6 us
  waiting for transfers between devices: 75 us -> 47.4 us
  starting transfers between devices: 22.9 us -> 27.6 us
  local copies, waits for them, and re-layouts: 7.61 us -> 3.55 us
    pallas_call x3 -> x6, Pallas kernels: 145 us -> 43.7 us  [the longest x1 13.2 us: local(): call(partial(first_source_kernel, axis, pieces), out_shape=(pltpu.VMEM((s...]
    ppermute x3 -> x4, waiting for transfers between devices: 17.5 us -> 2.27 us  [shifted(): return lax.ppermute(shard, axis, [(i, i + by) for i in range(peers - by)])]
    ppermute x8, waiting for transfers between devices: 14.1 us -> 0.04 us  [swapped(): lax.ppermute(shard, axis, [(i, i ^ bits) for i in range(lax.axis_size(axi...]
    ppermute x3 -> x4, starting transfers between devices: 9.04 us -> 17.7 us  [shifted(): return lax.ppermute(shard, axis, [(i, i + by) for i in range(peers - by)])]
    all_to_all x1, starting transfers between devices: 8.23 us -> 4.49 us  [local(): lax.all_to_all(buffer, axis, split_axis=0, concat_axis=0, tiled=True)]
    squeeze x1 -> x0, local copies, waits for them, and re-layouts: 2.71 us -> none  [local(): receiver_up = shifted(fields[0, 1], axis, 1)]
  transfers between devices with their start and end apart: 12 -> 13, of which waited for: 6 -> 2; matrix products, arithmetic and copies ran while one was open for 2% -> 1% of each run, Pallas kernels for 38% -> 29%
where the time goes in v2:
time: 131 us; the launch traced here: 130 us
  Pallas kernels  50.6 us (39%)
  waiting for transfers between devices  47.4 us (36%)
  starting transfers between devices  27.6 us (21%)
  local copies, waits for them, and re-layouts  3.55 us (3%)
    all_to_all x1, waiting for transfers between devices, local(): lax.all_to_all(buffer, axis, split_axis=0, concat_axis=0, tiled=True)  45.1 us
    ppermute x4, starting transfers between devices, shifted(): return lax.ppermute(shard, axis, [(i, i + by) for i in range(peers - by)])  17.7 us
    pallas_call x1, Pallas kernels, local(): call(partial(first_source_kernel, axis, pieces), out_shape=(pltpu.VMEM((s...  13.2 us
    pallas_call x1, Pallas kernels, local(): call(first_image_kernel, out_shape=(pltpu.VMEM((steps, 2 * terms) + plane...  9 us
    pallas_call x1, Pallas kernels, local(): call(receiver_kernel, out_shape=pltpu.VMEM((steps, 2) + planes, f32), in_...  8.54 us
    pallas_call x1, Pallas kernels, local(): call(source_kernel, out_shape=(pltpu.HBM((peers, CAP * size + extra, size...  7.3 us
    ppermute x8, starting transfers between devices, swapped(): lax.ppermute(shard, axis, [(i, i ^ bits) for i in range(lax.axis_size(axi...  5.46 us
    all_to_all x1, starting transfers between devices, local(): lax.all_to_all(buffer, axis, split_axis=0, concat_axis=0, tiled=True)  4.49 us
  transfers between devices with their start and end apart: 13, of which 2 were waited for; matrix products, arithmetic and copies ran while one was open for 1% of the time, Pallas kernels for 29%

profile of v2, /device:TPU:15, one launch (start us, length us, event | category | flops | bytes accessed | tf_op | source)
XLA Modules:
  0.0 130.3 jit_solution(10388366444959595730)
XLA Ops:
  0.6 1.4 %collective-permute-start.4 = (f32[2,128,128]{2,1,0:T(8,128)}, f32[2,128,128]{2,1,0:T(8,128)S(1)}, u32[]{:S(2)}, u32[]{:S(2)}) collective-permute-start(f32[2,128,128]{2,1,0:T(8,128)} %refs_0_.1), channel_id=1, source_target_pairs={{0,12},{1,13},{2,14},{3,15},{4,8},{5,9},{6,10},{7,11},{8,4},{9,5},... | collective-permute-start | bytes 393224 | tf_op jit(solution)/shard_map/ppermute | solution.py:446
  2.0 1.1 collective-permute-start.3
  3.1 1.1 collective-permute-start.2
  4.2 0.2 collective-permute-start.5
  4.4 5.4 %collective-permute-start.1 = (s32[1,2]{1,0:T(1,128)}, s32[1,2]{1,0:T(1,128)S(1)}, u32[]{:S(2)}, u32[]{:S(2)}) collective-permute-start(s32[1,2]{1,0:T(1,128)} %orders_ref.1), channel_id=1, source_target_pairs={{0,1},{1,2},{2,3},{3,4},{4,5},{5,6},{6,7},{7,8},{8,9},{9,10},{10,1... | collective-permute-start | bytes 32 | tf_op jit(solution)/shard_map/ppermute | solution.py:442
  9.9 0.8 copy.12.ids_ref
  10.6 2.3 %collective-permute-done.1.orders_ref.orders_up_ref = s32[1,2]{1,0:T(1,128)S(1)} collective-permute-done((s32[1,2]{1,0:T(1,128)}, s32[1,2]{1,0:T(1,128)S(1)}, u32[]{:S(2)}, u32[]{:S(2)}) %collective-permute-start.1) | collective-permute-done | bytes 40 | tf_op jit(solution)/shard_map/ppermute | solution.py:442
  12.9 5.2 %collective-permute-start = (s32[1,2,4,2]{3,2,1,0:T(4,128)S(1)}, s32[1,2,4,2]{3,2,1,0:T(4,128)S(1)}, u32[]{:S(2)}, u32[]{:S(2)}) collective-permute-start(s32[1,2,4,2]{3,2,1,0:T(4,128)S(1)} %copy.12.ids_ref), channel_id=1, source_target_pairs={{0,1},{1,2},{2,3},{3,4},{4,5},{5,6},{6,7},{7,8},{8,9},{9,10},{10,1... | collective-permute-start | bytes 200 | tf_op jit(solution)/shard_map/ppermute | solution.py:442
  18.1 0.0 collective-permute-done.4.refs_3_
  18.1 0.1 collective-permute-start.8
  18.1 0.0 collective-permute-done.3.refs_2_
  18.2 1.4 %collective-permute-start.7 = (f32[2,128,128]{2,1,0:T(8,128)S(1)}, f32[2,128,128]{2,1,0:T(8,128)S(1)}, u32[]{:S(2)}, u32[]{:S(2)}) collective-permute-start(f32[2,128,128]{2,1,0:T(8,128)S(1)} %collective-permute-done.3.refs_2_), channel_id=1, source_target_pairs={{0,2},{1,3},{2,0},{3,1},{4,6},{5,7},{6,4},{7,5},{8,10},{9,11},{10,... | collective-permute-start | bytes 393224 | tf_op jit(solution)/shard_map/ppermute | solution.py:446
  19.6 0.0 collective-permute-done.2.refs_1_
  19.6 0.1 collective-permute-start.6
  19.7 0.0 collective-permute-done.ids_ref.ids_up_ref
  19.7 0.0 copy-start
  19.7 1.1 copy-done
  20.8 0.0 copy-start.9
  20.8 1.6 %copy-done.9 = f32[1,2,2,512,256]{4,3,2,1,0:T(8,128)S(1)} copy-done((f32[1,2,2,512,256]{4,3,2,1,0:T(8,128)S(1)}, f32[1,2,2,512,256]{4,3,2,1,0:T(8,128)}, u32[]{:S(2)}) %copy-start.9) | copy-done | bytes 2097176
  22.4 0.0 copy-start.3
  22.4 4.2 %along_y.1 = (f32[4,70,8,256]{3,2,1,0:T(8,128)S(1)}, f32[2,3,2,70,8,256]{5,4,3,2,1,0:T(8,128)S(1)}) custom-call(f32[4,512,256]{2,1,0:T(8,128)S(1)} %bitcast.2, bf16[512,768]{1,0:T(8,128)(2,1)S(1)} %copy-done, s32[1,2,4,2]{3,2,1,0:T(4,128)S(1)} %collective-permute-done.ids_ref.ids_up_ref, s32[1,2]{1,0:T(1,128)S(1)} %collective-permute-done.1.orders_ref.orders_up_ref), custom_call_target="tpu_custom_call" | custom-call | flops 4294967296 | bytes 8388608 | tf_op jit(solution)/shard_map/along_y/pallas_call | solution.py:483
  26.6 0.0 copy-start.1
  26.6 0.0 copy-start.4
  26.7 0.0 copy-start.5
  26.7 0.0 copy-start.6
  26.7 0.0 collective-permute-done.5.refs_4_
  26.7 0.0 collective-permute-done.8.refs_7_
  26.7 0.0 collective-permute-done.7.refs_6_
  26.7 0.0 collective-permute-done.6.refs_5_
  26.7 0.0 copy-done.3
  26.7 1.5 %stack_tiles.1 = (f32[8,2,128,128]{3,2,1,0:T(8,128)S(1)}, f32[2,64,8,256]{3,2,1,0:T(8,128)S(1)}) custom-call(f32[2,128,128]{2,1,0:T(8,128)S(1)} %copy-done.3, f32[2,128,128]{2,1,0:T(8,128)S(1)} %collective-permute-done.2.refs_1_, f32[2,128,128]{2,1,0:T(8,128)S(1)} %collective-permute-done.3.refs_2_, f32[2,128,128]{2,1,0:T(8,128)S(1)} %collective-permute-done.4.refs_3_, ...), custom_call_target="tpu_custom_call" | custom-call | tf_op jit(solution)/shard_map/stack_tiles/pallas_call | solution.py:493
  28.3 0.1 collective-permute-start.9
  28.3 4.3 %collective-permute-start.11 = (f32[2,64,8,256]{3,2,1,0:T(8,128)S(1)}, f32[2,64,8,256]{3,2,1,0:T(8,128)S(1)}, u32[]{:S(2)}, u32[]{:S(2)}) collective-permute-start(f32[2,64,8,256]{3,2,1,0:T(8,128)S(1)} %get-tuple-element.19), channel_id=1, source_target_pairs={{0,1},{1,2},{2,3},{3,4},{4,5},{5,6},{6,7},{7,8},{8,9},{9,10},{10,1... | collective-permute-start | bytes 3145736 | tf_op jit(solution)/shard_map/ppermute | solution.py:442
  32.6 0.0 collective-permute-done.9.rest_1_
  32.6 0.0 copy-done.1
  32.6 0.0 copy-done.4
  32.7 0.0 copy-done.5
  32.7 0.0 copy-done.6
  32.7 13.2 %first_sources.1 = (f32[2,8,64,8,256]{4,3,2,1,0:T(8,128)S(1)}, f32[2,2,64,8,256]{4,3,2,1,0:T(8,128)S(1)}, f32[2,64,8,256]{3,2,1,0:T(8,128)}, f32[2,2,512,128]{3,2,1,0:T(8,128)S(1)}) custom-call(s32[1,2,4,2]{3,2,1,0:T(4,128)S(1)} %copy.12.ids_ref, s32[1,2]{1,0:T(1,128)S(1)} %copy-done.6, s32[1,2,4,2]{3,2,1,0:T(4,128)S(1)} %collective-permute-done.ids_ref.ids_up_ref, ...), custom_call_target="tpu_custom_call" | custom-call | tf_op jit(solution)/shard_map/first_sources/pallas_call | solution.py:507
  45.9 2.8 %collective-permute-start.10 = (f32[2,64,8,256]{3,2,1,0:T(8,128)}, f32[2,64,8,256]{3,2,1,0:T(8,128)S(1)}, u32[]{:S(2)}, u32[]{:S(2)}) collective-permute-start(f32[2,64,8,256]{3,2,1,0:T(8,128)} %get-tuple-element.17), channel_id=1, source_target_pairs={{0,1},{1,2},{2,3},{3,4},{4,5},{5,6},{6,7},{7,8},{8,9},{9,10},{10,1... | collective-permute-start | bytes 3145736 | tf_op jit(solution)/shard_map/ppermute | solution.py:442
  48.7 9.0 %first_images.1 = (f32[2,8,64,8,256]{4,3,2,1,0:T(8,128)S(1)}, f32[2,64,8,256]{3,2,1,0:T(8,128)S(1)}) custom-call(s32[1,2]{1,0:T(1,128)S(1)} %collective-permute-done.1.orders_ref.orders_up_ref, f32[3]{0:T(128)S(1)} %copy-done.4, f32[4]{0:T(128)S(1)} %copy-done.5, f32[2,2,512,128]{3,2,1,0:T(8,128)S(1)} %get-tuple-element.20.slow_up, ...), custom_call_target="tpu_custom_call" | custom-call | tf_op jit(solution)/shard_map/first_images/pallas_call | solution.py:528
  57.7 0.0 collective-permute-done.11.rows_ref
  57.7 0.0 copy-start.7
  57.7 0.0 copy-start.8
  57.7 8.5 %receiver_ticks.1.receivers_ref = f32[2,2,64,8,256]{4,3,2,1,0:T(8,128)S(1)} custom-call(f32[2,64,8,256]{3,2,1,0:T(8,128)S(1)} %collective-permute-done.11.rows_ref, f32[2,8,64,8,256]{4,3,2,1,0:T(8,128)S(1)} %get-tuple-element.22.coefs_up_ref, f32[2,8,64,8,256]{4,3,2,1,0:T(8,128)S(1)} %get-tuple-element.18.coefs_ref, bf16[512,768]{1,0:T(8,128)(2,1)S(1)} %copy-done.1), custom_call_target="tpu_custom_call" | custom-call | tf_op jit(solution)/shard_map/receiver_ticks/pallas_call | solution.py:540
  66.3 0.0 collective-permute-done.10.rows_ref
  66.3 0.0 copy-done.7
  66.3 0.0 copy-done.8
  66.3 7.3 %source_tick_and_seats.1 = (f32[16,264,128]{2,1,0:T(8,128)}, f32[2,64,8,256]{3,2,1,0:T(8,128)}) custom-call(f32[2,64,8,256]{3,2,1,0:T(8,128)S(1)} %collective-permute-done.10.rows_ref, f32[2,8,64,8,256]{4,3,2,1,0:T(8,128)S(1)} %get-tuple-element.18.coefs_ref, bf16[512,768]{1,0:T(8,128)(2,1)S(1)} %copy-done.1, ...), custom_call_target="tpu_custom_call" | custom-call | tf_op jit(solution)/shard_map/source_tick_and_seats/pallas_call | solution.py:550
  73.6 0.0 copy-start.2
  73.6 4.5 %all-to-all-start = ((f32[16,264,128]{2,1,0:T(8,128)}), f32[16,264,128]{2,1,0:T(8,128)}, u32[]{:S(2)}, u32[]{:S(2)}) async-start(f32[16,264,128]{2,1,0:T(8,128)} %get-tuple-element.24), calls=%async_computation | async-start | bytes 4325376 | tf_op jit(solution)/shard_map/all_to_all | solution.py:568
  78.1 0.0 copy-done.2
  78.1 3.4 %wavefields.1 = f32[2,2,512,256]{3,2,1,0:T(8,128)} custom-call(f32[2,64,8,256]{3,2,1,0:T(8,128)S(1)} %copy-done.2, f32[2,2,64,8,256]{4,3,2,1,0:T(8,128)S(1)} %receiver_ticks.1.receivers_ref), custom_call_target="tpu_custom_call" | custom-call | tf_op jit(solution)/shard_map/wavefields/pallas_call | solution.py:569
  81.5 45.1 %all-to-all-done.received_ref = f32[16,264,128]{2,1,0:T(8,128)} async-done(((f32[16,264,128]{2,1,0:T(8,128)}), f32[16,264,128]{2,1,0:T(8,128)}, u32[]{:S(2)}, u32[]{:S(2)}) %all-to-all-start) | async-done | bytes 2162720 | tf_op jit(solution)/shard_map/all_to_all | solution.py:568
  126.6 3.5 %image_volume.1 = f32[8,128,128]{2,1,0:T(8,128)} custom-call(f32[16,264,128]{2,1,0:T(8,128)} %all-to-all-done.received_ref), custom_call_target="tpu_custom_call" | custom-call | tf_op jit(solution)/shard_map/image_volume/pallas_call | solution.py:581
Async XLA Ops:
  0.6 17.4 %collective-permute-start.4 = (f32[2,128,128]{2,1,0:T(8,128)}, f32[2,128,128]{2,1,0:T(8,128)S(1)}, u32[]{:S(2)}, u32[]{:S(2)}) collective-permute-start(f32[2,128,128]{2,1,0:T(8,128)} %refs_0_.1), channel_id=1, source_target_pairs={{0,12},{1,13},{2,14},{3,15},{4,8},{5,9},{6,10},{7,11},{8,4},{9,5},... | collective-permute-start | bytes 393224 | tf_op jit(solution)/shard_map/ppermute | solution.py:446
  2.0 16.2 %collective-permute-start.3 = (f32[2,128,128]{2,1,0:T(8,128)}, f32[2,128,128]{2,1,0:T(8,128)S(1)}, u32[]{:S(2)}, u32[]{:S(2)}) collective-permute-start(f32[2,128,128]{2,1,0:T(8,128)} %refs_0_.1), channel_id=1, source_target_pairs={{0,8},{1,9},{2,10},{3,11},{4,12},{5,13},{6,14},{7,15},{8,0},{9,1},... | collective-permute-start | bytes 393224 | tf_op jit(solution)/shard_map/ppermute | solution.py:446
  3.1 16.5 %collective-permute-start.2 = (f32[2,128,128]{2,1,0:T(8,128)}, f32[2,128,128]{2,1,0:T(8,128)S(1)}, u32[]{:S(2)}, u32[]{:S(2)}) collective-permute-start(f32[2,128,128]{2,1,0:T(8,128)} %refs_0_.1), channel_id=1, source_target_pairs={{0,4},{1,5},{2,6},{3,7},{4,0},{5,1},{6,2},{7,3},{8,12},{9,13},{10,... | collective-permute-start | bytes 393224 | tf_op jit(solution)/shard_map/ppermute | solution.py:446
  4.2 22.5 %collective-permute-start.5 = (f32[2,128,128]{2,1,0:T(8,128)}, f32[2,128,128]{2,1,0:T(8,128)S(1)}, u32[]{:S(2)}, u32[]{:S(2)}) collective-permute-start(f32[2,128,128]{2,1,0:T(8,128)} %refs_0_.1), channel_id=1, source_target_pairs={{0,2},{1,3},{2,0},{3,1},{4,6},{5,7},{6,4},{7,5},{8,10},{9,11},{10,... | collective-permute-start | bytes 393224 | tf_op jit(solution)/shard_map/ppermute | solution.py:446
  4.4 8.5 %collective-permute-start.1 = (s32[1,2]{1,0:T(1,128)}, s32[1,2]{1,0:T(1,128)S(1)}, u32[]{:S(2)}, u32[]{:S(2)}) collective-permute-start(s32[1,2]{1,0:T(1,128)} %orders_ref.1), channel_id=1, source_target_pairs={{0,1},{1,2},{2,3},{3,4},{4,5},{5,6},{6,7},{7,8},{8,9},{9,10},{10,1... | collective-permute-start | bytes 32 | tf_op jit(solution)/shard_map/ppermute | solution.py:442
  12.9 6.8 %collective-permute-start = (s32[1,2,4,2]{3,2,1,0:T(4,128)S(1)}, s32[1,2,4,2]{3,2,1,0:T(4,128)S(1)}, u32[]{:S(2)}, u32[]{:S(2)}) collective-permute-start(s32[1,2,4,2]{3,2,1,0:T(4,128)S(1)} %copy.12.ids_ref), channel_id=1, source_target_pairs={{0,1},{1,2},{2,3},{3,4},{4,5},{5,6},{6,7},{7,8},{8,9},{9,10},{10,1... | collective-permute-start | bytes 200 | tf_op jit(solution)/shard_map/ppermute | solution.py:442
  18.1 8.6 %collective-permute-start.8 = (f32[2,128,128]{2,1,0:T(8,128)S(1)}, f32[2,128,128]{2,1,0:T(8,128)S(1)}, u32[]{:S(2)}, u32[]{:S(2)}) collective-permute-start(f32[2,128,128]{2,1,0:T(8,128)S(1)} %collective-permute-done.4.refs_3_), channel_id=1, source_target_pairs={{0,2},{1,3},{2,0},{3,1},{4,6},{5,7},{6,4},{7,5},{8,10},{9,11},{10,... | collective-permute-start | bytes 393224 | tf_op jit(solution)/shard_map/ppermute | solution.py:446
  18.2 8.5 %collective-permute-start.7 = (f32[2,128,128]{2,1,0:T(8,128)S(1)}, f32[2,128,128]{2,1,0:T(8,128)S(1)}, u32[]{:S(2)}, u32[]{:S(2)}) collective-permute-start(f32[2,128,128]{2,1,0:T(8,128)S(1)} %collective-permute-done.3.refs_2_), channel_id=1, source_target_pairs={{0,2},{1,3},{2,0},{3,1},{4,6},{5,7},{6,4},{7,5},{8,10},{9,11},{10,... | collective-permute-start | bytes 393224 | tf_op jit(solution)/shard_map/ppermute | solution.py:446
  19.6 7.1 %collective-permute-start.6 = (f32[2,128,128]{2,1,0:T(8,128)S(1)}, f32[2,128,128]{2,1,0:T(8,128)S(1)}, u32[]{:S(2)}, u32[]{:S(2)}) collective-permute-start(f32[2,128,128]{2,1,0:T(8,128)S(1)} %collective-permute-done.2.refs_1_), channel_id=1, source_target_pairs={{0,2},{1,3},{2,0},{3,1},{4,6},{5,7},{6,4},{7,5},{8,10},{9,11},{10,... | collective-permute-start | bytes 393224 | tf_op jit(solution)/shard_map/ppermute | solution.py:446
  19.7 1.1 copy-start
  20.8 1.6 %copy-start.9 = (f32[1,2,2,512,256]{4,3,2,1,0:T(8,128)S(1)}, f32[1,2,2,512,256]{4,3,2,1,0:T(8,128)}, u32[]{:S(2)}) copy-start(f32[1,2,2,512,256]{4,3,2,1,0:T(8,128)} %param.9) | copy-start | bytes 6291460
  22.4 4.3 %copy-start.3 = (f32[2,128,128]{2,1,0:T(8,128)S(1)}, f32[2,128,128]{2,1,0:T(8,128)}, u32[]{:S(2)}) copy-start(f32[2,128,128]{2,1,0:T(8,128)} %refs_0_.1) | copy-start | bytes 393220
  26.6 6.0 %copy-start.1 = (bf16[512,768]{1,0:T(8,128)(2,1)S(1)}, bf16[512,768]{1,0:T(8,128)(2,1)}, u32[]{:S(2)}) copy-start(bf16[512,768]{1,0:T(8,128)(2,1)} %constant.2.clone.sides_ref) | copy-start | bytes 2359300
  26.6 6.0 %copy-start.4 = (f32[3]{0:T(128)S(1)}, f32[3]{0:T(128)}, u32[]{:S(2)}) copy-start(f32[3]{0:T(128)} %weights_ref.3) | copy-start | bytes 40
  26.7 6.0 %copy-start.5 = (f32[4]{0:T(128)S(1)}, f32[4]{0:T(128)}, u32[]{:S(2)}) copy-start(f32[4]{0:T(128)} %rates_ref.3) | copy-start | bytes 52
  26.7 6.0 %copy-start.6 = (s32[1,2]{1,0:T(1,128)S(1)}, s32[1,2]{1,0:T(1,128)}, u32[]{:S(2)}) copy-start(s32[1,2]{1,0:T(1,128)} %orders_ref.1) | copy-start | bytes 28
  28.3 4.4 %collective-permute-start.9 = (f32[8,2,128,128]{3,2,1,0:T(8,128)S(1)}, f32[8,2,128,128]{3,2,1,0:T(8,128)S(1)}, u32[]{:S(2)}, u32[]{:S(2)}) collective-permute-start(f32[8,2,128,128]{3,2,1,0:T(8,128)S(1)} %get-tuple-element.16.rest_0_), channel_id=1, source_target_pairs={{0,1},{1,0},{2,3},{3,2},{4,5},{5,4},{6,7},{7,6},{8,9},{9,8},{10,11... | collective-permute-start | bytes 3145736 | tf_op jit(solution)/shard_map/ppermute | solution.py:446
  28.3 29.3 %collective-permute-start.11 = (f32[2,64,8,256]{3,2,1,0:T(8,128)S(1)}, f32[2,64,8,256]{3,2,1,0:T(8,128)S(1)}, u32[]{:S(2)}, u32[]{:S(2)}) collective-permute-start(f32[2,64,8,256]{3,2,1,0:T(8,128)S(1)} %get-tuple-element.19), channel_id=1, source_target_pairs={{0,1},{1,2},{2,3},{3,4},{4,5},{5,6},{6,7},{7,8},{8,9},{9,10},{10,1... | collective-permute-start | bytes 3145736 | tf_op jit(solution)/shard_map/ppermute | solution.py:442
  45.9 20.4 %collective-permute-start.10 = (f32[2,64,8,256]{3,2,1,0:T(8,128)}, f32[2,64,8,256]{3,2,1,0:T(8,128)S(1)}, u32[]{:S(2)}, u32[]{:S(2)}) collective-permute-start(f32[2,64,8,256]{3,2,1,0:T(8,128)} %get-tuple-element.17), channel_id=1, source_target_pairs={{0,1},{1,2},{2,3},{3,4},{4,5},{5,6},{6,7},{7,8},{8,9},{9,10},{10,1... | collective-permute-start | bytes 3145736 | tf_op jit(solution)/shard_map/ppermute | solution.py:442
  57.7 8.6 %copy-start.7 = (s32[1,16]{1,0:T(1,128)S(1)}, s32[1,16]{1,0:T(1,128)}, u32[]{:S(2)}) copy-start(s32[1,16]{1,0:T(1,128)} %owners_ref.1) | copy-start | bytes 196
  57.7 8.6 %copy-start.8 = (s32[1,16]{1,0:T(1,128)S(1)}, s32[1,16]{1,0:T(1,128)}, u32[]{:S(2)}) copy-start(s32[1,16]{1,0:T(1,128)} %slots_ref.1) | copy-start | bytes 196
  73.6 4.5 %copy-start.2 = (f32[2,64,8,256]{3,2,1,0:T(8,128)S(1)}, f32[2,64,8,256]{3,2,1,0:T(8,128)}, u32[]{:S(2)}) copy-start(f32[2,64,8,256]{3,2,1,0:T(8,128)} %get-tuple-element.25.source_ref) | copy-start | bytes 3145732
  73.6 53.0 %all-to-all-start = ((f32[16,264,128]{2,1,0:T(8,128)}), f32[16,264,128]{2,1,0:T(8,128)}, u32[]{:S(2)}, u32[]{:S(2)}) async-start(f32[16,264,128]{2,1,0:T(8,128)} %get-tuple-element.24), calls=%async_computation | async-start | bytes 4325376 | tf_op jit(solution)/shard_map/all_to_all | solution.py:568

commit v3 on v2

--- a/solution.py
+++ b/solution.py
@@ -16,11 +16,15 @@
 VMEM = pl.BlockSpec(memory_space=pltpu.VMEM)
 SMEM = pl.BlockSpec(memory_space=pltpu.SMEM)
 ANY = pl.BlockSpec(memory_space=pl.ANY)
-PARAMS = pltpu.CompilerParams(vmem_limit_bytes=18 * 2**20)
+PARAMS = pltpu.CompilerParams(vmem_limit_bytes=14 * 2**20)
 
 
 def in_vmem(x):
     return pltpu.with_memory_space_constraint(x, pltpu.VMEM)
+
+
+def in_hbm(x):
+    return pltpu.with_memory_space_constraint(x, pltpu.HBM)
 
 
 def in_powers(terms):
@@ -32,7 +36,8 @@
         polys.append(grown)
     for k in range(terms):
         rows[k, : len(polys[k])] = polys[k] / 8.0 ** np.arange(len(polys[k]))
-    return rows
+    lead = np.diag(rows).copy()
+    return rows / lead, lead
 
 
 def fitted():
@@ -48,6 +53,7 @@
 
 
 SINE, COSINE = fitted()
+ROUNDER = 1.5 * 2.0**23
 
 
 def horner(x, coefs):
@@ -58,7 +64,7 @@
 
 
 def cos_sin(turns):
-    r = turns - jnp.round(turns)
+    r = turns - ((turns + ROUNDER) - ROUNDER)
     r2 = r * r
     s = r * horner(r2, SINE)
     c = horner(r2, COSINE)
@@ -67,7 +73,8 @@
 
 def lane_sums(cells_y, terms):
     one = 2 * np.eye(cells_y) + np.eye(cells_y, k=1) + np.eye(cells_y, k=-1)
-    side = np.concatenate([np.linalg.matrix_power(one, k) for k in range(1, terms)], 1)
+    _, lead = in_powers(terms)
+    side = np.concatenate([lead[k] * np.linalg.matrix_power(one, k) for k in range(1, terms)], 1)
     return jnp.asarray(np.concatenate([side, side], 0), jnp.bfloat16)
 
 
@@ -177,41 +184,73 @@
 
 
 def stack_kernel(*refs):
-    parts, (ext, out, rows, sems) = refs[:-4], refs[-4:]
-    edge = (ext.shape[1] - rows.shape[1]) // 2
+    parts, (out, sems) = refs[:-2], refs[-2:]
     copies = [pltpu.make_async_copy(part, out.at[i], sems.at[i]) for i, part in enumerate(parts)]
-    copies.append(
-        pltpu.make_async_copy(
-            ext.at[pl.ds(2, 2), pl.ds(edge, rows.shape[1])], rows, sems.at[len(parts)]
-        )
-    )
     for copy in copies:
         copy.start()
     for copy in copies:
         copy.wait()
 
 
-def along_kernel(fields_ref, sides_ref, ids_ref, orders_ref, ext, sums, flat, flat_sem):
-    for copy in fetch(fields_ref, flat, flat_sem):
+def words_of(ids_ref, orders_ref):
+    _, steps, tiles_x, tiles_y = ids_ref.shape
+    for j in range(steps):
+        yield orders_ref[0, j]
+        for a in range(tiles_x):
+            for b in range(tiles_y):
+                yield ids_ref[0, j, a, b]
+
+
+def place_tiles(axis, tiles, tile_of, slow):
+    _, per, size, _ = tiles[0].shape
+    me = lax.axis_index(axis)
+    for a in range(slow.shape[1] // size):
+        for b in range(slow.shape[0]):
+            tile = tile_of(a, b)
+            apart = tile // per ^ me
+            for low, ref in enumerate(tiles):
+
+                @pl.when((apart & 3) == low)
+                def _(a=a, b=b, ref=ref, group=apart >> 2, tile=tile):
+                    slow[b, a * size : (a + 1) * size, :] = ref[group, tile % per]
+
+
+def rows_kernel(
+    ids_ref, orders_ref, fields_ref, sides_ref, ext, rows, source_sums, receiver_sums, flat, flat_sem, sem
+):
+    arriving = fetch(fields_ref, flat, flat_sem)
+    R = rows.shape[1] - 1
+    edge = (ext.shape[1] - R) // 2
+    lane = lax.broadcasted_iota(jnp.int32, rows.shape[2:], 1)
+    words = jnp.zeros(rows.shape[2:], jnp.int32)
+    for i, word in enumerate(words_of(ids_ref, orders_ref)):
+        words = jnp.where(lane == i, word, words)
+    for p in range(rows.shape[0]):
+        rows[p, R] = words.astype(jnp.float32)
+    for copy in arriving:
         copy.wait()
-    edge = sums.shape[1]
     load_rows(flat, Rows(ext, edge))
-    for pair in (0, 1):
-        along_y(Rows(ext, edge, 2 * pair, 2), sides_ref, sums.at[pair])
-
-
-def series(slow, orders_ref, weights_ref, rates_ref, coefs_ref, j):
+    copy = pltpu.make_async_copy(
+        ext.at[pl.ds(2, 2), pl.ds(edge, R)], rows.at[:, pl.ds(0, R)], sem
+    )
+    copy.start()
+    along_y(Rows(ext, edge, 0, 2), sides_ref, source_sums)
+    along_y(Rows(ext, edge, 2, 2), sides_ref, receiver_sums)
+    copy.wait()
+
+
+def series(slow, order, weights_ref, rates_ref, coefs_ref, j):
     terms = rates_ref.shape[0]
-    powers = in_powers(terms)
+    powers, _ = in_powers(terms)
     R = coefs_ref.shape[2]
     total = weights_ref[0]
     for k in range(1, terms - 1):
         total = total + weights_ref[k]
     base = [1.0 - total] + [weights_ref[k] for k in range(terms - 1)]
     turn = [rates_ref[k] * (0.5 / np.pi) for k in range(terms)]
-    scale = [jnp.where(k <= orders_ref[0, j], base[k], 0.0) for k in range(terms)]
-
-    def body(r, _):
+    scale = [jnp.where(k <= order, base[k], 0.0) for k in range(terms)]
+
+    def row(r, _):
         for b in range(slow.shape[0]):
             at = slice(b * LANES, (b + 1) * LANES)
             here = slow[b, pl.ds(r, SUBS, stride=R), :]
@@ -232,65 +271,42 @@
                     coefs_ref[j, 2 * m + i, r, :, at] = out
         return 0
 
-    lax.fori_loop(0, R, body, 0, unroll=4)
+    lax.fori_loop(0, R, row, 0, unroll=8)
 
 
 def first_source_kernel(
-    axis, pieces, ids_ref, orders_ref, ids_up_ref, weights_ref, rates_ref, sides_ref, ext_in, sums_in, *rest
+    axis, ids_ref, orders_ref, weights_ref, rates_ref, sides_ref, ext_in, sums_in, t0, t1, t2, t3,
+    coefs_ref, states_ref, sent_ref, slow, ext, sums
 ):
-    tiles, (coefs_ref, states_ref, out_ref, slow_up), (library, slow, sems, out_sem, ext, sums) = (
-        rest[: len(pieces)],
-        rest[len(pieces) : len(pieces) + 4],
-        rest[len(pieces) + 4 :],
-    )
-    per = library.shape[0] // sum(len(at) for at in pieces)
-    copies = []
-    for ref, at in zip(tiles, pieces):
-        for i, k in enumerate(at):
-            copies.append(
-                pltpu.make_async_copy(ref.at[i], library.at[pl.ds(k * per, per)], sems.at[len(copies)])
-            )
-            copies[-1].start()
-    for copy in copies:
-        copy.wait()
-    me = lax.axis_index(axis)
-    steps, tiles_x, tiles_y = ids_ref.shape[-3:]
-    size = library.shape[1]
+    steps = ids_ref.shape[1]
     for j in range(steps):
-        for a in range(tiles_x):
-            for b in range(tiles_y):
-                for ids, to in ((ids_ref, slow), (ids_up_ref, slow_up.at[j])):
-                    tile = ids[0, j, a, b]
-                    to[b, a * size : (a + 1) * size, :] = library[(tile // per ^ me) * per + tile % per]
-        series(slow, orders_ref, weights_ref, rates_ref, coefs_ref, j)
+        place_tiles(axis, (t0, t1, t2, t3), lambda a, b, j=j: ids_ref[0, j, a, b], slow)
         edge = sums.shape[0]
         state = Rows(ext_in if j == 0 else ext, edge, 0, 2)
         into = Rows(ext, edge)
         if j:
             state.halo()
             along_y(state, sides_ref, sums)
+        series(slow, orders_ref[0, j], weights_ref, rates_ref, coefs_ref, j)
 
         def emit(r, b, re, im, j=j, into=into):
             for p, value in enumerate((re, im)):
                 states_ref[j, p, r, :, b * LANES : (b + 1) * LANES] = value
                 if j + 1 < steps:
                     into.put(p, r, b, value)
-
-        depth_step(state, sums if j else sums_in.at[0], coefs_ref.at[j], 1, emit)
-    copy = pltpu.make_async_copy(states_ref.at[steps - 1], out_ref, out_sem)
-    copy.start()
-    copy.wait()
+                else:
+                    sent_ref[p, r, :, b * LANES : (b + 1) * LANES] = value
+
+        depth_step(state, sums if j else sums_in, coefs_ref.at[j], 1, emit)
 
 
 def first_image_kernel(
-    orders_up_ref, weights_ref, rates_ref, slow_up, sides_ref, ext_in, sums_in, coefs_ref, states_ref,
-    coefs_up_ref, image_ref, ext, sums
+    sides_ref, ext_in, sums_in, coefs_ref, states_ref, image_ref, ext, sums
 ):
     steps = coefs_ref.shape[0]
     edge = sums.shape[0]
     into = Rows(ext, edge)
     for j in range(steps):
-        series(slow_up.at[j], orders_up_ref, weights_ref, rates_ref, coefs_up_ref, j)
         state = into if j else Rows(ext_in, edge, 2, 2)
         if j:
             state.halo()
@@ -303,23 +319,44 @@
                 into.put(0, r, b, re)
                 into.put(1, r, b, im)
 
-        depth_step(state, sums if j else sums_in.at[1], coefs_ref.at[j], -1, emit)
-
-
-def take_rows(rows_ref, state, sem):
-    copy = pltpu.make_async_copy(rows_ref, state.ref.at[:, pl.ds(state.edge, state.R)], sem)
+        depth_step(state, sums if j else sums_in, coefs_ref.at[j], -1, emit)
+
+
+def take_rows(rows_ref, state):
+    def body(r, _):
+        for p in range(state.planes):
+            for b in range(state.blocks):
+                state.put(p, r, b, rows_ref[p, r, :, b * LANES : (b + 1) * LANES])
+        return 0
+
+    lax.fori_loop(0, state.R, body, 0, unroll=8)
+    state.halo()
+
+
+def receiver_kernel(
+    axis, weights_ref, rates_ref, rows_any, rows_ref, t0, t1, t2, t3, sides_ref, coefs_ref,
+    states_ref, words, words_sem, slow, coefs_up_ref, ext, sums
+):
+    copy = pltpu.make_async_copy(rows_any.at[0, rows_any.shape[1] - 1], words, words_sem)
     copy.start()
-    copy.wait()
-    state.halo()
-
-
-def receiver_kernel(rows_ref, coefs_up_ref, coefs_ref, sides_ref, states_ref, sem, ext, sums):
     steps = coefs_ref.shape[0]
     state = Rows(ext, sums.shape[0])
-    take_rows(rows_ref, state, sem)
+    take_rows(rows_ref, state)
+    copy.wait()
+    blocks = slow.shape[0]
+    tiles = blocks * slow.shape[1] // t0.shape[2]
     for which, coefs in enumerate((coefs_up_ref, coefs_ref)):
         for j in range(steps):
             final = which == 1 and j == steps - 1
+            if which == 0:
+                first = j * (1 + tiles)
+
+                def tile_of(a, b, first=first):
+                    return words[0, first + 1 + a * blocks + b].astype(jnp.int32)
+
+                place_tiles(axis, (t0, t1, t2, t3), tile_of, slow)
+                order = words[0, first].astype(jnp.int32)
+                series(slow, order, weights_ref, rates_ref, coefs, 0)
 
             def emit(r, b, re, im, j=j, which=which, final=final):
                 for p, value in enumerate((re, im)):
@@ -329,7 +366,7 @@
                         states_ref[j, p, r, :, b * LANES : (b + 1) * LANES] = value
 
             along_y(state, sides_ref, sums)
-            depth_step(state, sums, coefs.at[j], -1, emit)
+            depth_step(state, sums, coefs.at[j if which else 0], -1, emit)
             if not final:
                 state.halo()
 
@@ -341,36 +378,13 @@
     steps = coefs_ref.shape[0]
     state = Rows(ext, sums.shape[0])
     R = state.R
-    take_rows(rows_ref, state, slot_sem)
-    for j in range(steps):
-        final = j == steps - 1
-
-        def emit(r, b, re, im, j=j, final=final):
-            at = slice(b * LANES, (b + 1) * LANES)
-            for p, value in enumerate((re, im)):
-                if final:
-                    state_ref[p, r, :, at] = value
-                else:
-                    state.put(p, r, b, value)
-            images[j, b, pl.ds(r, SUBS, stride=R), :] = (
-                image_ref[j, r, :, at]
-                + re * receivers_ref[j, 0, r, :, at]
-                + im * receivers_ref[j, 1, r, :, at]
-            )
-
-        along_y(state, sides_ref, sums)
-        depth_step(state, sums, coefs_ref.at[j], 1, emit)
-        if not final:
-            state.halo()
-    size = buffer_ref.shape[2]
-    peers = buffer_ref.shape[0]
-    extra = slot_rows.shape[1]
-    tiles_x, tiles_y = images.shape[2] // size, images.shape[1]
-    rows = (buffer_ref.shape[1] - extra) // CAP
-    for o in range(peers * CAP):
-        held[o] = -1
+    take_rows(rows_ref, state)
+    peers, _, size = buffer_ref.shape
+    rows = (buffer_ref.shape[1] - slot_rows.shape[1]) // CAP
+    tiles_x, tiles_y = images.shape[2] // rows, images.shape[1]
     copies = []
-    for p in range(steps * tiles_x * tiles_y):
+
+    def seat(p):
         j, a, b = p // (tiles_x * tiles_y), p // tiles_y % tiles_x, p % tiles_y
         owner = owners_ref[0, p]
         rank = jnp.int32(0)
@@ -385,13 +399,40 @@
             )
         )
         copies[-1].start()
+
+    for o in range(peers * CAP):
+        held[o] = -1
+    for j in range(steps):
+        final = j == steps - 1
+
+        def emit(r, b, re, im, j=j, final=final):
+            at = slice(b * LANES, (b + 1) * LANES)
+            for p, value in enumerate((re, im)):
+                if final:
+                    state_ref[p, r, :, at] = value
+                else:
+                    state.put(p, r, b, value)
+            images[j, b, pl.ds(r, SUBS, stride=R), :] = (
+                image_ref[j, r, :, at]
+                + re * receivers_ref[j, 0, r, :, at]
+                + im * receivers_ref[j, 1, r, :, at]
+            )
+
+        along_y(state, sides_ref, sums)
+        depth_step(state, sums, coefs_ref.at[j], 1, emit)
+        for p in range(j * tiles_x * tiles_y, (j + 1) * tiles_x * tiles_y):
+            seat(p)
+        if not final:
+            state.halo()
     lane = lax.broadcasted_iota(jnp.int32, slot_rows.shape[1:], 1)
     for o in range(peers):
         out = jnp.full(slot_rows.shape[1:], -1, jnp.int32)
         for i in range(CAP):
             out = jnp.where(lane == i, held[o * CAP + i], out)
         slot_rows[o] = out.astype(jnp.float32)
-    last = pltpu.make_async_copy(slot_rows, buffer_ref.at[:, pl.ds(CAP * rows, extra)], slot_sem)
+    last = pltpu.make_async_copy(
+        slot_rows, buffer_ref.at[:, pl.ds(CAP * rows, slot_rows.shape[1])], slot_sem
+    )
     last.start()
     for copy in copies:
         copy.wait()
@@ -421,20 +462,26 @@
         copy.wait()
 
 
-def volume_kernel(received_ref, out_ref, slots, sem):
-    peers, rows, _ = received_ref.shape
-    size = out_ref.shape[1]
-    copy = pltpu.make_async_copy(received_ref.at[:, pl.ds(CAP * size, 1)], slots, sem)
-    copy.start()
+def volume_kernel(received_ref, out_ref, slots, slot_sem, seats, sems):
+    peers, rows, size = seats.shape
+    first = pltpu.make_async_copy(received_ref.at[:, pl.ds(rows, 1)], slots, slot_sem)
+    first.start()
+    copies = []
+    for s in range(peers):
+        copies.append(
+            pltpu.make_async_copy(received_ref.at[s, pl.ds(0, rows)], seats.at[s], sems.at[s])
+        )
+        copies[-1].start()
     out_ref[...] = jnp.zeros_like(out_ref)
-    copy.wait()
+    first.wait()
     for s in range(peers):
+        copies[s].wait()
         for i in range(CAP):
             slot = slots[s, 0, i].astype(jnp.int32)
 
             @pl.when(slot >= 0)
             def _(s=s, i=i, slot=slot):
-                out_ref[slot] += received_ref[s, i * size : (i + 1) * size, :]
+                out_ref[slot] += seats[s, i * size : (i + 1) * size, :]
 
 
 def shifted(shard, axis, by):
@@ -456,12 +503,6 @@
     R = cells_x // SUBS
     f32 = jnp.float32
 
-    ids_up = shifted(tile_ids, axis, 1)
-    orders_up = shifted(orders, axis, 1)
-    far = [(4 * i, swapped(vel_tiles, axis, 4 * i)) for i in range(1, peers // 4)]
-    beside = [(2, swapped(vel_tiles, axis, 2))]
-    beside += [(k + 2, swapped(v, axis, 2)) for k, v in far]
-    held = [(0, vel_tiles)] + far + beside
     blocks = cells_y // LANES
     assert size == LANES and cells_x % SUBS == 0 and cells_y % LANES == 0
 
@@ -480,71 +521,78 @@
     planes = (R, SUBS, cells_y)
     padded = (R + 2 * edge, SUBS, cells_y)
     call = partial(pl.pallas_call, compiler_params=PARAMS)
-    ext, sums = call(
-        along_kernel,
-        out_shape=(pltpu.VMEM((4,) + padded, f32), pltpu.VMEM((2, edge, 2) + padded, f32)),
-        in_specs=[ANY, VMEM, SMEM, SMEM],
-        out_specs=(VMEM, VMEM),
-        scratch_shapes=flat(4),
-        cost_estimate=pl.CostEstimate(flops=2**32, bytes_accessed=2**23, transcendentals=0),
-        name="along_y",
-    )(fields.reshape(4, cells_x, cells_y), sides, ids_up, orders_up)
-    ext, sums = in_vmem(ext), in_vmem(sums)
-    half, rows = call(
-        stack_kernel,
+    ext, rows, source_sums, receiver_sums = call(
+        rows_kernel,
         out_shape=(
-            pltpu.VMEM((len(held),) + vel_tiles.shape, f32),
-            pltpu.VMEM((2,) + planes, f32),
+            pltpu.VMEM((4,) + padded, f32),
+            pltpu.VMEM((2, R + 1) + planes[1:], f32),
+            pltpu.VMEM((edge, 2) + padded, f32),
+            pltpu.VMEM((edge, 2) + padded, f32),
         ),
-        in_specs=[ANY] * len(held) + [VMEM],
-        out_specs=(VMEM, VMEM),
-        scratch_shapes=[pltpu.SemaphoreType.DMA((len(held) + 1,))],
-        name="stack_tiles",
-    )(*[v for _, v in held], ext)
-    other = swapped(half, axis, 1)
-    pieces = [[k for k, _ in held], [k ^ 1 for k, _ in held]]
+        in_specs=[SMEM] * 2 + [ANY, VMEM],
+        out_specs=(VMEM,) * 4,
+        scratch_shapes=flat(4) + [pltpu.SemaphoreType.DMA],
+        name="rows",
+    )(tile_ids, orders, in_hbm(fields.reshape(4, cells_x, cells_y)), sides)
+
+    def stacked(parts):
+        return call(
+            stack_kernel,
+            out_shape=pltpu.VMEM((len(parts),) + vel_tiles.shape, f32),
+            in_specs=[ANY] * len(parts),
+            out_specs=VMEM,
+            scratch_shapes=[pltpu.SemaphoreType.DMA((len(parts),))],
+            name="stack_tiles",
+        )(*parts)
+
+    line = [vel_tiles] + [swapped(vel_tiles, axis, 4 * i) for i in range(1, peers // 4)]
+    across = [swapped(v, axis, 2) for v in line[:-1]]
+    ext, rows, line[-1] = lax.optimization_barrier((ext, rows, line[-1]))
+    across.append(swapped(line[-1], axis, 2))
+    tiles = {0: stacked(line)}
+    tiles[1] = swapped(tiles[0], axis, 1)
+    tiles[2] = stacked(across)
+    tiles[2], rows = lax.optimization_barrier((tiles[2], rows))
+    tiles[3] = swapped(tiles[2], axis, 1)
     receiver_up = shifted(rows, axis, 1)
-    coefs, states, sent, slow_up = call(
-        partial(first_source_kernel, axis, pieces),
+    ext, source_sums, receiver_sums = in_vmem(ext), in_vmem(source_sums), in_vmem(receiver_sums)
+    tiles = [in_vmem(tiles[i]) for i in range(4)]
+    slow = [pltpu.VMEM((blocks, cells_x, LANES), f32)]
+    coefs, states, sent = call(
+        partial(first_source_kernel, axis),
         out_shape=(
             pltpu.VMEM((steps, 2 * terms) + planes, f32),
             pltpu.VMEM((steps, 2) + planes, f32),
-            pltpu.HBM((2,) + planes, f32),
-            pltpu.VMEM((steps, blocks, cells_x, LANES), f32),
+            pltpu.VMEM((2,) + planes, f32),
         ),
-        in_specs=[SMEM] * 5 + [VMEM] * 3 + [ANY] * 2,
-        out_specs=(VMEM, VMEM, ANY, VMEM),
-        scratch_shapes=[
-            pltpu.VMEM((peers * vel_tiles.shape[0], size, size), f32),
-            pltpu.VMEM((blocks, cells_x, LANES), f32),
-            pltpu.SemaphoreType.DMA((peers,)),
-            pltpu.SemaphoreType.DMA,
-        ]
-        + work(2),
+        in_specs=[SMEM] * 4 + [VMEM] * 7,
+        out_specs=(VMEM, VMEM, VMEM),
+        scratch_shapes=slow + work(2),
         name="first_sources",
-    )(tile_ids, orders, ids_up, term_weights, phase_rates, sides, ext, sums, half, other)
+    )(tile_ids, orders, term_weights, phase_rates, sides, ext, source_sums, *tiles)
     source_up = shifted(sent, axis, 1)
-    coefs, states, slow_up = in_vmem(coefs), in_vmem(states), in_vmem(slow_up)
-    coefs_up, image = call(
+    coefs, states = in_vmem(coefs), in_vmem(states)
+    image = call(
         first_image_kernel,
-        out_shape=(
-            pltpu.VMEM((steps, 2 * terms) + planes, f32),
-            pltpu.VMEM((steps,) + planes, f32),
-        ),
-        in_specs=[SMEM] * 3 + [VMEM] * 6,
-        out_specs=(VMEM, VMEM),
+        out_shape=pltpu.VMEM((steps,) + planes, f32),
+        in_specs=[VMEM] * 5,
+        out_specs=VMEM,
         scratch_shapes=work(2),
         name="first_images",
-    )(orders_up, term_weights, phase_rates, slow_up, sides, ext, sums, coefs, states)
+    )(sides, ext, receiver_sums, coefs, states)
+    image, receiver_up = lax.optimization_barrier((image, receiver_up))
     receivers = in_vmem(
         call(
-            receiver_kernel,
+            partial(receiver_kernel, axis),
             out_shape=pltpu.VMEM((steps, 2) + planes, f32),
-            in_specs=[ANY] + [VMEM] * 3,
+            in_specs=[SMEM] * 2 + [ANY] + [VMEM] * 7,
             out_specs=VMEM,
-            scratch_shapes=[pltpu.SemaphoreType.DMA] + work(2),
+            scratch_shapes=[pltpu.SMEM((SUBS, cells_y), f32), pltpu.SemaphoreType.DMA]
+            + slow
+            + [pltpu.VMEM((1, 2 * terms) + planes, f32)]
+            + work(2),
             name="receiver_ticks",
-        )(receiver_up, in_vmem(coefs_up), coefs, sides)
+        )(term_weights, phase_rates, receiver_up, in_vmem(receiver_up), *tiles, sides, coefs)
     )
     extra = SUBS
     buffer, source = call(
@@ -553,7 +601,7 @@
             pltpu.HBM((peers, CAP * size + extra, size), f32),
             pltpu.HBM((2,) + planes, f32),
         ),
-        in_specs=[ANY] + [VMEM] * 4 + [SMEM] * 2,
+        in_specs=[VMEM] * 5 + [SMEM] * 2,
         out_specs=(ANY, VMEM),
         scratch_shapes=[
             pltpu.VMEM((steps, blocks, cells_x, LANES), f32),
@@ -564,7 +612,7 @@
         ]
         + work(2),
         name="source_tick_and_seats",
-    )(source_up, coefs, sides, receivers, in_vmem(image), owners, image_slots)
+    )(in_vmem(source_up), coefs, sides, receivers, in_vmem(image), owners, image_slots)
     received = lax.all_to_all(buffer, axis, split_axis=0, concat_axis=0, tiled=True)
     wavefields = pl.pallas_call(
         output_kernel,
@@ -578,15 +626,19 @@
         compiler_params=PARAMS,
         name="wavefields",
     )(source, receivers)
-    volume = pl.pallas_call(
+    volume = call(
         volume_kernel,
         out_shape=jax.ShapeDtypeStruct((IMG_SLOTS, size, size), f32),
-        in_specs=[VMEM],
+        in_specs=[ANY],
         out_specs=VMEM,
-        scratch_shapes=[pltpu.SMEM((peers, 1, size), f32), pltpu.SemaphoreType.DMA],
-        compiler_params=PARAMS,
+        scratch_shapes=[
+            pltpu.SMEM((peers, 1, size), f32),
+            pltpu.SemaphoreType.DMA,
+            pltpu.VMEM((peers, CAP * size, size), f32),
+            pltpu.SemaphoreType.DMA((peers,)),
+        ],
         name="image_volume",
-    )(in_vmem(received))
+    )(received)
     return volume, wavefields[None]
 
 

time: 131 us -> 124 us (0.947)
  starting transfers between devices: 27.6 us -> 23.3 us
  Pallas kernels: 50.6 us -> 48.1 us
  waiting for transfers between devices: 47.4 us -> 48.9 us
    ppermute x4 -> x2, starting transfers between devices: 17.7 us -> 6.3 us  [shifted(): return lax.ppermute(shard, axis, [(i, i + by) for i in range(peers - by)])]
    ppermute x8 -> x9, starting transfers between devices: 5.46 us -> 11.4 us  [swapped(): lax.ppermute(shard, axis, [(i, i ^ bits) for i in range(lax.axis_size(axi...]
    ppermute x8 -> x9, waiting for transfers between devices: 0.04 us -> 3.39 us  [swapped(): lax.ppermute(shard, axis, [(i, i ^ bits) for i in range(lax.axis_size(axi...]
    pallas_call x6 -> x7, Pallas kernels: 39.9 us -> 37.4 us  [the longest x1 15.2 us: local(): call(partial(receiver_kernel, axis), out_shape=pltpu.VMEM((steps, 2) + pl...]
    ppermute x4 -> x2, waiting for transfers between devices: 2.27 us -> 0.01 us  [shifted(): return lax.ppermute(shard, axis, [(i, i + by) for i in range(peers - by)])]
  transfers between devices with their start and end apart: 13 -> 12, of which waited for: 2 -> 4; matrix products, arithmetic and copies ran while one was open for 1% -> 1% of each run, Pallas kernels for 29% -> 31%
where the time goes in v3:
time: 124 us
  waiting for transfers between devices  48.9 us (39%)
  Pallas kernels  48.1 us (39%)
  starting transfers between devices  23.3 us (19%)
  local copies, waits for them, and re-layouts  2.6 us (2%)
    all_to_all x1, waiting for transfers between devices, local(): lax.all_to_all(buffer, axis, split_axis=0, concat_axis=0, tiled=True)  45.5 us
    pallas_call x1, Pallas kernels, local(): call(partial(receiver_kernel, axis), out_shape=pltpu.VMEM((steps, 2) + pl...  15.2 us
    ppermute x9, starting transfers between devices, swapped(): lax.ppermute(shard, axis, [(i, i ^ bits) for i in range(lax.axis_size(axi...  11.4 us
    pallas_call x1, Pallas kernels, local(): call(partial(first_source_kernel, axis), out_shape=(pltpu.VMEM((steps, 2...  9.19 us
    pallas_call x1, Pallas kernels, local(): call(source_kernel, out_shape=(pltpu.HBM((peers, CAP * size + extra, size...  7.24 us
    ppermute x2, starting transfers between devices, shifted(): return lax.ppermute(shard, axis, [(i, i + by) for i in range(peers - by)])  6.3 us
    pallas_call x1, Pallas kernels, local(): call(rows_kernel, out_shape=(pltpu.VMEM((4,) + padded, f32), pltpu.VMEM((...  5.76 us
    all_to_all x1, starting transfers between devices, local(): lax.all_to_all(buffer, axis, split_axis=0, concat_axis=0, tiled=True)  5.6 us
  transfers between devices with their start and end apart: 12, of which 4 were waited for; matrix products, arithmetic and copies ran while one was open for 1% of the time, Pallas kernels for 31%

profile of v3, /device:TPU:15, one launch (start us, length us, event | category | flops | bytes accessed | tf_op | source)
XLA Modules:
  0.0 123.9 jit_solution(5529330057459115764)
XLA Ops:
  0.6 1.4 %collective-permute-start = (f32[2,128,128]{2,1,0:T(8,128)}, f32[2,128,128]{2,1,0:T(8,128)S(1)}, u32[]{:S(2)}, u32[]{:S(2)}) collective-permute-start(f32[2,128,128]{2,1,0:T(8,128)} %refs_0_.1), channel_id=1, source_target_pairs={{0,12},{1,13},{2,14},{3,15},{4,8},{5,9},{6,10},{7,11},{8,4},{9,5},... | collective-permute-start | bytes 393224 | tf_op jit(solution)/shard_map/ppermute | solution.py:493
  2.0 1.1 collective-permute-start.2
  3.1 1.1 collective-permute-start.1
  4.2 0.2 collective-permute-start.4
  4.4 0.8 copy.12.ids_ref
  5.2 0.0 copy-start
  5.2 1.1 copy-done
  6.3 0.0 copy-start.4
  6.3 0.7 copy-done.4
  7.0 0.0 copy-start.3
  7.0 0.0 copy-start.1
  7.0 0.0 copy-start.5
  7.0 0.0 copy-start.6
  7.0 0.0 copy-start.7
  7.0 5.8 %rows.1 = (f32[4,70,8,256]{3,2,1,0:T(8,128)S(1)}, f32[2,65,8,256]{3,2,1,0:T(8,128)S(1)}, f32[3,2,70,8,256]{4,3,2,1,0:T(8,128)S(1)}, f32[3,2,70,8,256]{4,3,2,1,0:T(8,128)S(1)}) custom-call(s32[1,2,4,2]{3,2,1,0:T(4,128)S(1)} %copy.12.ids_ref, s32[1,2]{1,0:T(1,128)S(1)} %copy-done.4, f32[4,512,256]{2,1,0:T(8,128)} %bitcast.2, bf16[512,768]{1,0:T(8,128)(2,1)S(1)} %copy-done), custom_call_target="tpu_custom_call" | custom-call | tf_op jit(solution)/shard_map/rows/pallas_call | solution.py:524
  12.8 0.0 collective-permute-done.refs_3_
  12.8 0.1 collective-permute-done.2.refs_2_
  12.9 1.2 collective-permute-start.6
  14.1 0.0 collective-permute-done.1.refs_1_
  14.1 0.3 collective-permute-start.5
  14.4 1.2 collective-permute-start.7
  15.6 0.0 copy-done.3
  15.6 0.7 stack_tiles.2.t0
  16.3 2.4 %collective-permute-start.3 = (f32[4,2,128,128]{3,2,1,0:T(8,128)S(1)}, f32[4,2,128,128]{3,2,1,0:T(8,128)S(1)}, u32[]{:S(2)}, u32[]{:S(2)}) collective-permute-start(f32[4,2,128,128]{3,2,1,0:T(8,128)S(1)} %stack_tiles.2.t0), channel_id=1, source_target_pairs={{0,1},{1,0},{2,3},{3,2},{4,5},{5,4},{6,7},{7,6},{8,9},{9,8},{10,11... | collective-permute-start | bytes 1572872 | tf_op jit(solution)/shard_map/ppermute | solution.py:493
  18.7 0.0 collective-permute-done.4.refs_0_
  18.7 0.0 collective-permute-done.6.refs_2_
  18.7 0.5 collective-permute-done.5.refs_1_
  19.2 2.8 %collective-permute-done.7.refs_3_ = f32[2,128,128]{2,1,0:T(8,128)S(1)} collective-permute-done((f32[2,128,128]{2,1,0:T(8,128)S(1)}, f32[2,128,128]{2,1,0:T(8,128)S(1)}, u32[]{:S(2)}, u32[]{:S(2)}) %collective-permute-start.7) | collective-permute-done | bytes 131104 | tf_op jit(solution)/shard_map/ppermute | solution.py:493
  22.0 0.7 stack_tiles.3.t2
  22.7 2.5 %collective-permute-start.8 = (f32[4,2,128,128]{3,2,1,0:T(8,128)S(1)}, f32[4,2,128,128]{3,2,1,0:T(8,128)S(1)}, u32[]{:S(2)}, u32[]{:S(2)}) collective-permute-start(f32[4,2,128,128]{3,2,1,0:T(8,128)S(1)} %stack_tiles.3.t2), channel_id=1, source_target_pairs={{0,1},{1,0},{2,3},{3,2},{4,5},{5,4},{6,7},{7,6},{8,9},{9,8},{10,11... | collective-permute-start | bytes 1572872 | tf_op jit(solution)/shard_map/ppermute | solution.py:493
  25.2 3.9 %collective-permute-start.10 = (f32[2,65,8,256]{3,2,1,0:T(8,128)S(1)}, f32[2,65,8,256]{3,2,1,0:T(8,128)S(1)}, u32[]{:S(2)}, u32[]{:S(2)}) collective-permute-start(f32[2,65,8,256]{3,2,1,0:T(8,128)S(1)} %get-tuple-element.29), channel_id=1, source_target_pairs={{0,1},{1,2},{2,3},{3,4},{4,5},{5,6},{6,7},{7,8},{8,9},{9,10},{10,1... | collective-permute-start | bytes 3194888 | tf_op jit(solution)/shard_map/ppermute | solution.py:489
  29.1 0.0 collective-permute-done.3.t1
  29.1 0.0 collective-permute-done.8.t3
  29.1 0.0 copy-done.1
  29.1 0.0 copy-done.5
  29.1 0.0 copy-done.6
  29.2 0.0 copy-done.7
  29.2 9.2 %first_sources.1 = (f32[2,8,64,8,256]{4,3,2,1,0:T(8,128)S(1)}, f32[2,2,64,8,256]{4,3,2,1,0:T(8,128)S(1)}, f32[2,64,8,256]{3,2,1,0:T(8,128)S(1)}) custom-call(s32[1,2,4,2]{3,2,1,0:T(4,128)S(1)} %copy.12.ids_ref, s32[1,2]{1,0:T(1,128)S(1)} %copy-done.5, f32[3]{0:T(128)S(1)} %copy-done.6, f32[4]{0:T(128)S(1)} %copy-done.7, bf16[512,768]{1,0:T(8,128)(2,1)S(1)} %copy-done.1, ...), custom_call_target="tpu_custom_call" | custom-call | tf_op jit(solution)/shard_map/first_sources/pallas_call | solution.py:561
  38.4 2.4 %collective-permute-start.9 = (f32[2,64,8,256]{3,2,1,0:T(8,128)S(1)}, f32[2,64,8,256]{3,2,1,0:T(8,128)S(1)}, u32[]{:S(2)}, u32[]{:S(2)}) collective-permute-start(f32[2,64,8,256]{3,2,1,0:T(8,128)S(1)} %get-tuple-element.25), channel_id=1, source_target_pairs={{0,1},{1,2},{2,3},{3,4},{4,5},{5,6},{6,7},{7,8},{8,9},{9,10},{10,1... | collective-permute-start | bytes 3145736 | tf_op jit(solution)/shard_map/ppermute | solution.py:489
  40.8 3.4 %first_images.1.image_ref = f32[2,64,8,256]{3,2,1,0:T(8,128)S(1)} custom-call(bf16[512,768]{1,0:T(8,128)(2,1)S(1)} %copy-done.1, f32[4,70,8,256]{3,2,1,0:T(8,128)S(1)} %get-tuple-element.20.ext_in, f32[3,2,70,8,256]{4,3,2,1,0:T(8,128)S(1)} %get-tuple-element.27.sums_in, f32[2,8,64,8,256]{4,3,2,1,0:T(8,128)S(1)} %get-tuple-element.26.coefs_ref, ...), custom_call_target="tpu_custom_call" | custom-call | tf_op jit(solution)/shard_map/first_images/pallas_call | solution.py:575
  44.2 0.0 copy-start.8
  44.2 0.0 copy-start.9
  44.2 0.0 collective-permute-done.10.rows_any.rows_ref
  44.2 15.2 %receiver_ticks.1.receivers_ref = f32[2,2,64,8,256]{4,3,2,1,0:T(8,128)S(1)} custom-call(f32[3]{0:T(128)S(1)} %copy-done.6, f32[4]{0:T(128)S(1)} %copy-done.7, f32[2,65,8,256]{3,2,1,0:T(8,128)S(1)} %collective-permute-done.10.rows_any.rows_ref, f32[2,65,8,256]{3,2,1,0:T(8,128)S(1)} %collective-permute-done.10.rows_any.rows_ref, ...), custom_call_target="tpu_custom_call" | custom-call | tf_op jit(solution)/shard_map/receiver_ticks/pallas_call | solution.py:585
  59.4 0.0 collective-permute-done.9.rows_ref
  59.4 0.0 copy-done.8
  59.4 0.0 copy-done.9
  59.4 7.2 %source_tick_and_seats.1 = (f32[16,264,128]{2,1,0:T(8,128)}, f32[2,64,8,256]{3,2,1,0:T(8,128)}) custom-call(f32[2,64,8,256]{3,2,1,0:T(8,128)S(1)} %collective-permute-done.9.rows_ref, f32[2,8,64,8,256]{4,3,2,1,0:T(8,128)S(1)} %get-tuple-element.26.coefs_ref, bf16[512,768]{1,0:T(8,128)(2,1)S(1)} %copy-done.1, ...), custom_call_target="tpu_custom_call" | custom-call | tf_op jit(solution)/shard_map/source_tick_and_seats/pallas_call | solution.py:598
  66.7 0.0 copy-start.2
  66.7 5.6 %all-to-all-start = ((f32[16,264,128]{2,1,0:T(8,128)}), f32[16,264,128]{2,1,0:T(8,128)}, u32[]{:S(2)}, u32[]{:S(2)}) async-start(f32[16,264,128]{2,1,0:T(8,128)} %get-tuple-element.32), calls=%async_computation | async-start | bytes 4325376 | tf_op jit(solution)/shard_map/all_to_all | solution.py:616
  72.3 0.0 copy-done.2
  72.3 3.4 %wavefields.1 = f32[2,2,512,256]{3,2,1,0:T(8,128)} custom-call(f32[2,64,8,256]{3,2,1,0:T(8,128)S(1)} %copy-done.2, f32[2,2,64,8,256]{4,3,2,1,0:T(8,128)S(1)} %receiver_ticks.1.receivers_ref), custom_call_target="tpu_custom_call" | custom-call | tf_op jit(solution)/shard_map/wavefields/pallas_call | solution.py:617
  75.7 45.5 %all-to-all-done.received_ref = f32[16,264,128]{2,1,0:T(8,128)} async-done(((f32[16,264,128]{2,1,0:T(8,128)}), f32[16,264,128]{2,1,0:T(8,128)}, u32[]{:S(2)}, u32[]{:S(2)}) %all-to-all-start) | async-done | bytes 2162720 | tf_op jit(solution)/shard_map/all_to_all | solution.py:616
  121.2 2.5 %image_volume.1 = f32[8,128,128]{2,1,0:T(8,128)} custom-call(f32[16,264,128]{2,1,0:T(8,128)} %all-to-all-done.received_ref), custom_call_target="tpu_custom_call" | custom-call | tf_op jit(solution)/shard_map/image_volume/pallas_call | solution.py:629
Async XLA Ops:
  0.6 12.1 %collective-permute-start = (f32[2,128,128]{2,1,0:T(8,128)}, f32[2,128,128]{2,1,0:T(8,128)S(1)}, u32[]{:S(2)}, u32[]{:S(2)}) collective-permute-start(f32[2,128,128]{2,1,0:T(8,128)} %refs_0_.1), channel_id=1, source_target_pairs={{0,12},{1,13},{2,14},{3,15},{4,8},{5,9},{6,10},{7,11},{8,4},{9,5},... | collective-permute-start | bytes 393224 | tf_op jit(solution)/shard_map/ppermute | solution.py:493
  2.0 10.9 %collective-permute-start.2 = (f32[2,128,128]{2,1,0:T(8,128)}, f32[2,128,128]{2,1,0:T(8,128)S(1)}, u32[]{:S(2)}, u32[]{:S(2)}) collective-permute-start(f32[2,128,128]{2,1,0:T(8,128)} %refs_0_.1), channel_id=1, source_target_pairs={{0,8},{1,9},{2,10},{3,11},{4,12},{5,13},{6,14},{7,15},{8,0},{9,1},... | collective-permute-start | bytes 393224 | tf_op jit(solution)/shard_map/ppermute | solution.py:493
  3.1 11.0 %collective-permute-start.1 = (f32[2,128,128]{2,1,0:T(8,128)}, f32[2,128,128]{2,1,0:T(8,128)S(1)}, u32[]{:S(2)}, u32[]{:S(2)}) collective-permute-start(f32[2,128,128]{2,1,0:T(8,128)} %refs_0_.1), channel_id=1, source_target_pairs={{0,4},{1,5},{2,6},{3,7},{4,0},{5,1},{6,2},{7,3},{8,12},{9,13},{10,... | collective-permute-start | bytes 393224 | tf_op jit(solution)/shard_map/ppermute | solution.py:493
  4.2 14.5 %collective-permute-start.4 = (f32[2,128,128]{2,1,0:T(8,128)}, f32[2,128,128]{2,1,0:T(8,128)S(1)}, u32[]{:S(2)}, u32[]{:S(2)}) collective-permute-start(f32[2,128,128]{2,1,0:T(8,128)} %refs_0_.1), channel_id=1, source_target_pairs={{0,2},{1,3},{2,0},{3,1},{4,6},{5,7},{6,4},{7,5},{8,10},{9,11},{10,... | collective-permute-start | bytes 393224 | tf_op jit(solution)/shard_map/ppermute | solution.py:493
  5.2 1.1 copy-start
  6.3 0.7 copy-start.4
  7.0 8.6 %copy-start.3 = (f32[2,128,128]{2,1,0:T(8,128)S(1)}, f32[2,128,128]{2,1,0:T(8,128)}, u32[]{:S(2)}) copy-start(f32[2,128,128]{2,1,0:T(8,128)} %refs_0_.1) | copy-start | bytes 393220
  7.0 22.1 %copy-start.1 = (bf16[512,768]{1,0:T(8,128)(2,1)S(1)}, bf16[512,768]{1,0:T(8,128)(2,1)}, u32[]{:S(2)}) copy-start(bf16[512,768]{1,0:T(8,128)(2,1)} %constant.2.clone.sides_ref) | copy-start | bytes 2359300
  7.0 22.2 %copy-start.5 = (s32[1,2]{1,0:T(1,128)S(1)}, s32[1,2]{1,0:T(1,128)}, u32[]{:S(2)}) copy-start(s32[1,2]{1,0:T(1,128)} %orders_ref.3) | copy-start | bytes 28
  7.0 22.2 %copy-start.6 = (f32[3]{0:T(128)S(1)}, f32[3]{0:T(128)}, u32[]{:S(2)}) copy-start(f32[3]{0:T(128)} %weights_ref.3) | copy-start | bytes 40
  7.0 22.2 %copy-start.7 = (f32[4]{0:T(128)S(1)}, f32[4]{0:T(128)}, u32[]{:S(2)}) copy-start(f32[4]{0:T(128)} %rates_ref.3) | copy-start | bytes 52
  12.9 5.8 %collective-permute-start.6 = (f32[2,128,128]{2,1,0:T(8,128)S(1)}, f32[2,128,128]{2,1,0:T(8,128)S(1)}, u32[]{:S(2)}, u32[]{:S(2)}) collective-permute-start(f32[2,128,128]{2,1,0:T(8,128)S(1)} %collective-permute-done.2.refs_2_), channel_id=1, source_target_pairs={{0,2},{1,3},{2,0},{3,1},{4,6},{5,7},{6,4},{7,5},{8,10},{9,11},{10,... | collective-permute-start | bytes 393224 | tf_op jit(solution)/shard_map/ppermute | solution.py:493
  14.1 5.1 %collective-permute-start.5 = (f32[2,128,128]{2,1,0:T(8,128)S(1)}, f32[2,128,128]{2,1,0:T(8,128)S(1)}, u32[]{:S(2)}, u32[]{:S(2)}) collective-permute-start(f32[2,128,128]{2,1,0:T(8,128)S(1)} %collective-permute-done.1.refs_1_), channel_id=1, source_target_pairs={{0,2},{1,3},{2,0},{3,1},{4,6},{5,7},{6,4},{7,5},{8,10},{9,11},{10,... | collective-permute-start | bytes 393224 | tf_op jit(solution)/shard_map/ppermute | solution.py:493
  14.4 7.6 %collective-permute-start.7 = (f32[2,128,128]{2,1,0:T(8,128)S(1)}, f32[2,128,128]{2,1,0:T(8,128)S(1)}, u32[]{:S(2)}, u32[]{:S(2)}) collective-permute-start(f32[2,128,128]{2,1,0:T(8,128)S(1)} %collective-permute-done.refs_3_), channel_id=1, source_target_pairs={{0,2},{1,3},{2,0},{3,1},{4,6},{5,7},{6,4},{7,5},{8,10},{9,11},{10,... | collective-permute-start | bytes 393224 | tf_op jit(solution)/shard_map/ppermute | solution.py:493
  16.3 12.8 %collective-permute-start.3 = (f32[4,2,128,128]{3,2,1,0:T(8,128)S(1)}, f32[4,2,128,128]{3,2,1,0:T(8,128)S(1)}, u32[]{:S(2)}, u32[]{:S(2)}) collective-permute-start(f32[4,2,128,128]{3,2,1,0:T(8,128)S(1)} %stack_tiles.2.t0), channel_id=1, source_target_pairs={{0,1},{1,0},{2,3},{3,2},{4,5},{5,4},{6,7},{7,6},{8,9},{9,8},{10,11... | collective-permute-start | bytes 1572872 | tf_op jit(solution)/shard_map/ppermute | solution.py:493
  22.7 6.5 %collective-permute-start.8 = (f32[4,2,128,128]{3,2,1,0:T(8,128)S(1)}, f32[4,2,128,128]{3,2,1,0:T(8,128)S(1)}, u32[]{:S(2)}, u32[]{:S(2)}) collective-permute-start(f32[4,2,128,128]{3,2,1,0:T(8,128)S(1)} %stack_tiles.3.t2), channel_id=1, source_target_pairs={{0,1},{1,0},{2,3},{3,2},{4,5},{5,4},{6,7},{7,6},{8,9},{9,8},{10,11... | collective-permute-start | bytes 1572872 | tf_op jit(solution)/shard_map/ppermute | solution.py:493
  25.2 19.0 %collective-permute-start.10 = (f32[2,65,8,256]{3,2,1,0:T(8,128)S(1)}, f32[2,65,8,256]{3,2,1,0:T(8,128)S(1)}, u32[]{:S(2)}, u32[]{:S(2)}) collective-permute-start(f32[2,65,8,256]{3,2,1,0:T(8,128)S(1)} %get-tuple-element.29), channel_id=1, source_target_pairs={{0,1},{1,2},{2,3},{3,4},{4,5},{5,6},{6,7},{7,8},{8,9},{9,10},{10,1... | collective-permute-start | bytes 3194888 | tf_op jit(solution)/shard_map/ppermute | solution.py:489
  38.4 21.0 %collective-permute-start.9 = (f32[2,64,8,256]{3,2,1,0:T(8,128)S(1)}, f32[2,64,8,256]{3,2,1,0:T(8,128)S(1)}, u32[]{:S(2)}, u32[]{:S(2)}) collective-permute-start(f32[2,64,8,256]{3,2,1,0:T(8,128)S(1)} %get-tuple-element.25), channel_id=1, source_target_pairs={{0,1},{1,2},{2,3},{3,4},{4,5},{5,6},{6,7},{7,8},{8,9},{9,10},{10,1... | collective-permute-start | bytes 3145736 | tf_op jit(solution)/shard_map/ppermute | solution.py:489
  44.2 15.2 %copy-start.8 = (s32[1,16]{1,0:T(1,128)S(1)}, s32[1,16]{1,0:T(1,128)}, u32[]{:S(2)}) copy-start(s32[1,16]{1,0:T(1,128)} %owners_ref.1) | copy-start | bytes 196
  44.2 15.2 %copy-start.9 = (s32[1,16]{1,0:T(1,128)S(1)}, s32[1,16]{1,0:T(1,128)}, u32[]{:S(2)}) copy-start(s32[1,16]{1,0:T(1,128)} %slots_ref.1) | copy-start | bytes 196
  66.7 5.6 %copy-start.2 = (f32[2,64,8,256]{3,2,1,0:T(8,128)S(1)}, f32[2,64,8,256]{3,2,1,0:T(8,128)}, u32[]{:S(2)}) copy-start(f32[2,64,8,256]{3,2,1,0:T(8,128)} %get-tuple-element.33.source_ref) | copy-start | bytes 3145732
  66.7 54.5 %all-to-all-start = ((f32[16,264,128]{2,1,0:T(8,128)}), f32[16,264,128]{2,1,0:T(8,128)}, u32[]{:S(2)}, u32[]{:S(2)}) async-start(f32[16,264,128]{2,1,0:T(8,128)} %get-tuple-element.32), calls=%async_computation | async-start | bytes 4325376 | tf_op jit(solution)/shard_map/all_to_all | solution.py:616

commit v4 on v3

--- a/solution.py
+++ b/solution.py
@@ -126,7 +126,33 @@
     return kept, value
 
 
-def depth_step(state, sums, coefs, sign, emit, unroll=8):
+def warm(sums, p, k, edge, at):
+    chain = []
+    for r in range(-k, k):
+        chain, _ = chained(chain, sums[k - 1, p, r + edge, :, at], 2 * k)
+    return chain
+
+
+def along_x(sums, edge):
+    orders, planes, rows, _, cells_y = sums.shape
+    pairs = [(k, p) for k in range(1, orders + 1) for p in range(planes)]
+    for b in range(cells_y // LANES):
+        at = slice(b * LANES, (b + 1) * LANES)
+
+        def body(r, carry):
+            kept = []
+            for (k, p), chain in zip(pairs, carry):
+                new, value = chained(chain, sums[k - 1, p, r + edge + k, :, at], 2 * k)
+                sums[k - 1, p, r + edge, :, at] = value
+                kept.append(new)
+            return kept
+
+        lax.fori_loop(
+            0, rows - 2 * edge, body, [warm(sums, p, k, edge, at) for k, p in pairs], unroll=8
+        )
+
+
+def depth_step(state, sums, coefs, sign, emit, unroll=8, summed=False, done=None):
     terms, edge = sums.shape[0] + 1, state.edge
     for b in range(state.blocks):
         at = slice(b * LANES, (b + 1) * LANES)
@@ -139,6 +165,9 @@
                 else:
                     both = []
                     for p in (0, 1):
+                        if summed:
+                            both.append(sums[k - 1, p, r + edge, :, at])
+                            continue
                         new, value = chained(
                             carry[2 * (k - 1) + p], sums[k - 1, p, r + edge + k, :, at], 2 * k
                         )
@@ -152,14 +181,11 @@
             emit(r, b, *total)
             return kept
 
-        start = []
-        for k in range(1, terms):
-            for p in (0, 1):
-                chain = []
-                for r in range(-k, k):
-                    chain, _ = chained(chain, sums[k - 1, p, r + edge, :, at], 2 * k)
-                start.append(chain)
+        pairs = [] if summed else [(k, p) for k in range(1, terms) for p in (0, 1)]
+        start = [warm(sums, p, k, edge, at) for k, p in pairs]
         lax.fori_loop(0, state.R, body, start, unroll=unroll)
+        if done is not None:
+            done(b)
 
 
 def fetch(field_ref, flat, sem):
@@ -216,7 +242,7 @@
 
 
 def rows_kernel(
-    ids_ref, orders_ref, fields_ref, sides_ref, ext, rows, source_sums, receiver_sums, flat, flat_sem, sem
+    ids_ref, orders_ref, fields_ref, ext, rows, flat, flat_sem, sem
 ):
     arriving = fetch(fields_ref, flat, flat_sem)
     R = rows.shape[1] - 1
@@ -234,9 +260,14 @@
         ext.at[pl.ds(2, 2), pl.ds(edge, R)], rows.at[:, pl.ds(0, R)], sem
     )
     copy.start()
-    along_y(Rows(ext, edge, 0, 2), sides_ref, source_sums)
-    along_y(Rows(ext, edge, 2, 2), sides_ref, receiver_sums)
     copy.wait()
+
+
+def sums_kernel(ext, sides_ref, source_sums, receiver_sums):
+    edge = source_sums.shape[0]
+    for first, sums in ((0, source_sums), (2, receiver_sums)):
+        along_y(Rows(ext, edge, first, 2), sides_ref, sums)
+        along_x(sums, edge)
 
 
 def series(slow, order, weights_ref, rates_ref, coefs_ref, j):
@@ -297,7 +328,7 @@
                 else:
                     sent_ref[p, r, :, b * LANES : (b + 1) * LANES] = value
 
-        depth_step(state, sums if j else sums_in, coefs_ref.at[j], 1, emit)
+        depth_step(state, sums if j else sums_in, coefs_ref.at[j], 1, emit, summed=j == 0)
 
 
 def first_image_kernel(
@@ -319,7 +350,7 @@
                 into.put(0, r, b, re)
                 into.put(1, r, b, im)
 
-        depth_step(state, sums if j else sums_in, coefs_ref.at[j], -1, emit)
+        depth_step(state, sums if j else sums_in, coefs_ref.at[j], -1, emit, summed=j == 0)
 
 
 def take_rows(rows_ref, state):
@@ -373,35 +404,37 @@
 
 def source_kernel(
     rows_ref, coefs_ref, sides_ref, receivers_ref, image_ref, owners_ref, slots_ref,
-    buffer_ref, state_ref, images, slot_rows, held, sem, slot_sem, ext, sums
+    buffer_ref, state_out, images, slot_rows, held, sem, slot_sem, state_sem, last_state, ext, sums
 ):
     steps = coefs_ref.shape[0]
     state = Rows(ext, sums.shape[0])
     R = state.R
-    take_rows(rows_ref, state)
     peers, _, size = buffer_ref.shape
     rows = (buffer_ref.shape[1] - slot_rows.shape[1]) // CAP
     tiles_x, tiles_y = images.shape[2] // rows, images.shape[1]
-    copies = []
-
-    def seat(p):
-        j, a, b = p // (tiles_x * tiles_y), p // tiles_y % tiles_x, p % tiles_y
-        owner = owners_ref[0, p]
+    take_rows(rows_ref, state)
+    along_y(state, sides_ref, sums)
+    for o in range(peers * CAP):
+        held[o] = -1
+    ranks = []
+    for p in range(steps * tiles_x * tiles_y):
         rank = jnp.int32(0)
         for before in range(p):
-            rank = rank + (owners_ref[0, before] == owner).astype(jnp.int32)
-        held[owner * CAP + rank] = slots_ref[0, p]
-        copies.append(
-            pltpu.make_async_copy(
-                images.at[j, b, pl.ds(a * rows, rows)],
-                buffer_ref.at[owner, pl.ds(pl.multiple_of(rank * rows, rows), rows)],
-                sem.at[p],
-            )
+            rank = rank + (owners_ref[0, before] == owners_ref[0, p]).astype(jnp.int32)
+        held[owners_ref[0, p] * CAP + rank] = slots_ref[0, p]
+        ranks.append(rank)
+    lane = lax.broadcasted_iota(jnp.int32, slot_rows.shape[1:], 1)
+    for o in range(peers):
+        out = jnp.full(slot_rows.shape[1:], -1, jnp.int32)
+        for i in range(CAP):
+            out = jnp.where(lane == i, held[o * CAP + i], out)
+        slot_rows[o] = out.astype(jnp.float32)
+    copies = [
+        pltpu.make_async_copy(
+            slot_rows, buffer_ref.at[:, pl.ds(CAP * rows, slot_rows.shape[1])], slot_sem
         )
-        copies[-1].start()
-
-    for o in range(peers * CAP):
-        held[o] = -1
+    ]
+    copies[0].start()
     for j in range(steps):
         final = j == steps - 1
 
@@ -409,7 +442,7 @@
             at = slice(b * LANES, (b + 1) * LANES)
             for p, value in enumerate((re, im)):
                 if final:
-                    state_ref[p, r, :, at] = value
+                    last_state[p, r, :, at] = value
                 else:
                     state.put(p, r, b, value)
             images[j, b, pl.ds(r, SUBS, stride=R), :] = (
@@ -418,25 +451,34 @@
                 + im * receivers_ref[j, 1, r, :, at]
             )
 
-        along_y(state, sides_ref, sums)
-        depth_step(state, sums, coefs_ref.at[j], 1, emit)
-        for p in range(j * tiles_x * tiles_y, (j + 1) * tiles_x * tiles_y):
-            seat(p)
-        if not final:
+        def done(b, j=j, final=final):
+            for a in range(tiles_x):
+                p = (j * tiles_x + a) * tiles_y + b
+                copies.append(
+                    pltpu.make_async_copy(
+                        images.at[j, b, pl.ds(a * rows, rows)],
+                        buffer_ref.at[
+                            owners_ref[0, p], pl.ds(pl.multiple_of(ranks[p] * rows, rows), rows)
+                        ],
+                        sem.at[p],
+                    )
+                )
+                copies[-1].start()
+            if final:
+                at = pl.ds(b * LANES, LANES)
+                copies.append(
+                    pltpu.make_async_copy(
+                        last_state.at[:, :, :, at], state_out.at[:, :, :, at], state_sem.at[b]
+                    )
+                )
+                copies[-1].start()
+
+        if j:
             state.halo()
-    lane = lax.broadcasted_iota(jnp.int32, slot_rows.shape[1:], 1)
-    for o in range(peers):
-        out = jnp.full(slot_rows.shape[1:], -1, jnp.int32)
-        for i in range(CAP):
-            out = jnp.where(lane == i, held[o * CAP + i], out)
-        slot_rows[o] = out.astype(jnp.float32)
-    last = pltpu.make_async_copy(
-        slot_rows, buffer_ref.at[:, pl.ds(CAP * rows, slot_rows.shape[1])], slot_sem
-    )
-    last.start()
+            along_y(state, sides_ref, sums)
+        depth_step(state, sums, coefs_ref.at[j], 1, emit, done=done)
     for copy in copies:
         copy.wait()
-    last.wait()
 
 
 def output_kernel(source_ref, receivers_ref, out_ref, flat, sems):
@@ -521,19 +563,14 @@
     planes = (R, SUBS, cells_y)
     padded = (R + 2 * edge, SUBS, cells_y)
     call = partial(pl.pallas_call, compiler_params=PARAMS)
-    ext, rows, source_sums, receiver_sums = call(
+    ext, rows = call(
         rows_kernel,
-        out_shape=(
-            pltpu.VMEM((4,) + padded, f32),
-            pltpu.VMEM((2, R + 1) + planes[1:], f32),
-            pltpu.VMEM((edge, 2) + padded, f32),
-            pltpu.VMEM((edge, 2) + padded, f32),
-        ),
-        in_specs=[SMEM] * 2 + [ANY, VMEM],
-        out_specs=(VMEM,) * 4,
+        out_shape=(pltpu.VMEM((4,) + padded, f32), pltpu.VMEM((2, R + 1) + planes[1:], f32)),
+        in_specs=[SMEM] * 2 + [ANY],
+        out_specs=(VMEM, VMEM),
         scratch_shapes=flat(4) + [pltpu.SemaphoreType.DMA],
         name="rows",
-    )(tile_ids, orders, in_hbm(fields.reshape(4, cells_x, cells_y)), sides)
+    )(tile_ids, orders, in_hbm(fields.reshape(4, cells_x, cells_y)))
 
     def stacked(parts):
         return call(
@@ -545,9 +582,22 @@
             name="stack_tiles",
         )(*parts)
 
-    line = [vel_tiles] + [swapped(vel_tiles, axis, 4 * i) for i in range(1, peers // 4)]
-    across = [swapped(v, axis, 2) for v in line[:-1]]
-    ext, rows, line[-1] = lax.optimization_barrier((ext, rows, line[-1]))
+    line = [vel_tiles] + [swapped(vel_tiles, axis, 4 * i) for i in range(1, peers // 4 - 1)]
+    across = [swapped(vel_tiles, axis, 2)]
+    ext, rows, across[0], *line[1:] = lax.optimization_barrier((ext, rows, across[0], *line[1:]))
+    across += [swapped(v, axis, 2) for v in line[1:]]
+    line.append(swapped(line[-1], axis, 4))
+    ext = in_vmem(ext)
+    source_sums, receiver_sums = call(
+        sums_kernel,
+        out_shape=(pltpu.VMEM((edge, 2) + padded, f32),) * 2,
+        in_specs=[VMEM, VMEM],
+        out_specs=(VMEM, VMEM),
+        name="first_sums",
+    )(ext, sides)
+    line[-1], source_sums, receiver_sums = lax.optimization_barrier(
+        (line[-1], source_sums, receiver_sums)
+    )
     across.append(swapped(line[-1], axis, 2))
     tiles = {0: stacked(line)}
     tiles[1] = swapped(tiles[0], axis, 1)
@@ -555,7 +605,7 @@
     tiles[2], rows = lax.optimization_barrier((tiles[2], rows))
     tiles[3] = swapped(tiles[2], axis, 1)
     receiver_up = shifted(rows, axis, 1)
-    ext, source_sums, receiver_sums = in_vmem(ext), in_vmem(source_sums), in_vmem(receiver_sums)
+    source_sums, receiver_sums = in_vmem(source_sums), in_vmem(receiver_sums)
     tiles = [in_vmem(tiles[i]) for i in range(4)]
     slow = [pltpu.VMEM((blocks, cells_x, LANES), f32)]
     coefs, states, sent = call(
@@ -602,13 +652,15 @@
             pltpu.HBM((2,) + planes, f32),
         ),
         in_specs=[VMEM] * 5 + [SMEM] * 2,
-        out_specs=(ANY, VMEM),
+        out_specs=(ANY, ANY),
         scratch_shapes=[
             pltpu.VMEM((steps, blocks, cells_x, LANES), f32),
             pltpu.VMEM((peers, extra, size), f32),
             pltpu.SMEM((peers * CAP,), jnp.int32),
             pltpu.SemaphoreType.DMA((steps * tiles_x * tiles_y,)),
             pltpu.SemaphoreType.DMA,
+            pltpu.SemaphoreType.DMA((blocks,)),
+            pltpu.VMEM((2,) + planes, f32),
         ]
         + work(2),
         name="source_tick_and_seats",

time: 124 us -> 119 us (0.960)
  waiting for transfers between devices: 48.9 us -> 44.4 us
    pallas_call x0 -> x1, Pallas kernels: none -> 3.19 us  [local(): call(sums_kernel, out_shape=(pltpu.VMEM((edge, 2) + padded, f32),) * 2, i...]
    ppermute x9, waiting for transfers between devices: 3.39 us -> 0.46 us  [swapped(): lax.ppermute(shard, axis, [(i, i ^ bits) for i in range(lax.axis_size(axi...]
    pallas_call x1, Pallas kernels: 5.76 us -> 3.79 us  [local(): call(rows_kernel, out_shape=(pltpu.VMEM((4,) + padded, f32), pltpu.VMEM((...]
    all_to_all x1, waiting for transfers between devices: 45.5 us -> 43.9 us  [local(): lax.all_to_all(buffer, axis, split_axis=0, concat_axis=0, tiled=True)]
    all_to_all x1, starting transfers between devices: 5.6 us -> 4.34 us  [local(): lax.all_to_all(buffer, axis, split_axis=0, concat_axis=0, tiled=True)]
    unnamed x21 -> x19, local copies, waits for them, and re-layouts: 2.6 us -> 2.68 us
  transfers between devices with their start and end apart: 12 -> 12, of which waited for: 4 -> 2; matrix products, arithmetic and copies ran while one was open for 1% -> 1% of each run, Pallas kernels for 31% -> 32%
where the time goes in v4:
time: 119 us
  Pallas kernels  47.4 us (40%)
  waiting for transfers between devices  44.4 us (37%)
  starting transfers between devices  23.4 us (20%)
  local copies, waits for them, and re-layouts  2.68 us (2%)
    all_to_all x1, waiting for transfers between devices, local(): lax.all_to_all(buffer, axis, split_axis=0, concat_axis=0, tiled=True)  43.9 us
    pallas_call x1, Pallas kernels, local(): call(partial(receiver_kernel, axis), out_shape=pltpu.VMEM((steps, 2) + pl...  15.2 us
    ppermute x9, starting transfers between devices, swapped(): lax.ppermute(shard, axis, [(i, i ^ bits) for i in range(lax.axis_size(axi...  12.6 us
    pallas_call x1, Pallas kernels, local(): call(partial(first_source_kernel, axis), out_shape=(pltpu.VMEM((steps, 2...  8.72 us
    ppermute x2, starting transfers between devices, shifted(): return lax.ppermute(shard, axis, [(i, i + by) for i in range(peers - by)])  6.42 us
    pallas_call x1, Pallas kernels, local(): call(source_kernel, out_shape=(pltpu.HBM((peers, CAP * size + extra, size...  6.31 us
    all_to_all x1, starting transfers between devices, local(): lax.all_to_all(buffer, axis, split_axis=0, concat_axis=0, tiled=True)  4.34 us
    pallas_call x1, Pallas kernels, local(): call(rows_kernel, out_shape=(pltpu.VMEM((4,) + padded, f32), pltpu.VMEM((...  3.79 us
  transfers between devices with their start and end apart: 12, of which 2 were waited for; matrix products, arithmetic and copies ran while one was open for 1% of the time, Pallas kernels for 32%

profile of v4, /device:TPU:15, one launch (start us, length us, event | category | flops | bytes accessed | tf_op | source)
XLA Modules:
  0.0 118.9 jit_solution(11385774316622562323)
XLA Ops:
  0.6 0.0 copy-start
  0.6 0.2 collective-permute-start.1
  0.9 0.2 collective-permute-start
  1.1 2.3 %collective-permute-start.2 = (f32[2,128,128]{2,1,0:T(8,128)}, f32[2,128,128]{2,1,0:T(8,128)S(1)}, u32[]{:S(2)}, u32[]{:S(2)}) collective-permute-start(f32[2,128,128]{2,1,0:T(8,128)} %refs_0_.1), channel_id=1, source_target_pairs={{0,8},{1,9},{2,10},{3,11},{4,12},{5,13},{6,14},{7,15},{8,0},{9,1},... | collective-permute-start | bytes 393224 | tf_op jit(solution)/shard_map/ppermute | solution.py:535
  3.4 0.8 copy.12.ids_ref
  4.2 0.0 copy-start.3
  4.2 0.7 copy-done.3
  4.8 0.0 copy-start.2
  4.8 3.8 %rows.1 = (f32[4,70,8,256]{3,2,1,0:T(8,128)S(1)}, f32[2,65,8,256]{3,2,1,0:T(8,128)S(1)}) custom-call(s32[1,2,4,2]{3,2,1,0:T(4,128)S(1)} %copy.12.ids_ref, s32[1,2]{1,0:T(1,128)S(1)} %copy-done.3, f32[4,512,256]{2,1,0:T(8,128)} %bitcast.2), custom_call_target="tpu_custom_call" | custom-call | tf_op jit(solution)/shard_map/rows/pallas_call | solution.py:566
  8.6 0.0 collective-permute-done.1.refs_1_
  8.7 0.0 collective-permute-done.refs_0_
  8.7 0.4 collective-permute-done.2.refs_2_
  9.1 0.0 copy-start.4
  9.1 0.0 copy-start.5
  9.1 0.0 copy-start.6
  9.1 1.0 collective-permute-start.3
  10.1 2.0 %collective-permute-start.6 = (f32[2,128,128]{2,1,0:T(8,128)S(1)}, f32[2,128,128]{2,1,0:T(8,128)S(1)}, u32[]{:S(2)}, u32[]{:S(2)}) collective-permute-start(f32[2,128,128]{2,1,0:T(8,128)S(1)} %collective-permute-done.2.refs_2_), channel_id=1, source_target_pairs={{0,2},{1,3},{2,0},{3,1},{4,6},{5,7},{6,4},{7,5},{8,10},{9,11},{10,... | collective-permute-start | bytes 393224 | tf_op jit(solution)/shard_map/ppermute | solution.py:535
  12.1 0.0 collective-permute-start.5
  12.1 0.0 copy-done
  12.1 3.2 %first_sums.1 = (f32[3,2,70,8,256]{4,3,2,1,0:T(8,128)S(1)}, f32[3,2,70,8,256]{4,3,2,1,0:T(8,128)S(1)}) custom-call(f32[4,70,8,256]{3,2,1,0:T(8,128)S(1)} %get-tuple-element.25.ext.ext_in, bf16[512,768]{1,0:T(8,128)(2,1)S(1)} %copy-done), custom_call_target="tpu_custom_call" | custom-call | tf_op jit(solution)/shard_map/first_sums/pallas_call | solution.py:591
  15.3 0.0 collective-permute-done.3.refs_3_
  15.3 1.5 %collective-permute-start.7 = (f32[2,128,128]{2,1,0:T(8,128)S(1)}, f32[2,128,128]{2,1,0:T(8,128)S(1)}, u32[]{:S(2)}, u32[]{:S(2)}) collective-permute-start(f32[2,128,128]{2,1,0:T(8,128)S(1)} %collective-permute-done.3.refs_3_), channel_id=1, source_target_pairs={{0,2},{1,3},{2,0},{3,1},{4,6},{5,7},{6,4},{7,5},{8,10},{9,11},{10,... | collective-permute-start | bytes 393224 | tf_op jit(solution)/shard_map/ppermute | solution.py:535
  16.8 0.0 copy-done.2
  16.8 0.7 stack_tiles.2.t0
  17.5 2.6 %collective-permute-start.4 = (f32[4,2,128,128]{3,2,1,0:T(8,128)S(1)}, f32[4,2,128,128]{3,2,1,0:T(8,128)S(1)}, u32[]{:S(2)}, u32[]{:S(2)}) collective-permute-start(f32[4,2,128,128]{3,2,1,0:T(8,128)S(1)} %stack_tiles.2.t0), channel_id=1, source_target_pairs={{0,1},{1,0},{2,3},{3,2},{4,5},{5,4},{6,7},{7,6},{8,9},{9,8},{10,11... | collective-permute-start | bytes 1572872 | tf_op jit(solution)/shard_map/ppermute | solution.py:535
  20.1 0.0 collective-permute-done.5.refs_1_
  20.1 0.0 collective-permute-done.6.refs_2_
  20.1 0.0 collective-permute-done.7.refs_3_
  20.1 0.7 stack_tiles.3.t2
  20.9 2.8 %collective-permute-start.8 = (f32[4,2,128,128]{3,2,1,0:T(8,128)S(1)}, f32[4,2,128,128]{3,2,1,0:T(8,128)S(1)}, u32[]{:S(2)}, u32[]{:S(2)}) collective-permute-start(f32[4,2,128,128]{3,2,1,0:T(8,128)S(1)} %stack_tiles.3.t2), channel_id=1, source_target_pairs={{0,1},{1,0},{2,3},{3,2},{4,5},{5,4},{6,7},{7,6},{8,9},{9,8},{10,11... | collective-permute-start | bytes 1572872 | tf_op jit(solution)/shard_map/ppermute | solution.py:535
  23.6 4.0 %collective-permute-start.10 = (f32[2,65,8,256]{3,2,1,0:T(8,128)S(1)}, f32[2,65,8,256]{3,2,1,0:T(8,128)S(1)}, u32[]{:S(2)}, u32[]{:S(2)}) collective-permute-start(f32[2,65,8,256]{3,2,1,0:T(8,128)S(1)} %get-tuple-element.39), channel_id=1, source_target_pairs={{0,1},{1,2},{2,3},{3,4},{4,5},{5,6},{6,7},{7,8},{8,9},{9,10},{10,1... | collective-permute-start | bytes 3194888 | tf_op jit(solution)/shard_map/ppermute | solution.py:531
  27.7 0.0 collective-permute-done.4.t1
  27.7 0.0 collective-permute-done.8.t3
  27.7 0.0 copy-done.4
  27.7 0.0 copy-done.5
  27.7 0.0 copy-done.6
  27.7 8.7 %first_sources.1 = (f32[2,8,64,8,256]{4,3,2,1,0:T(8,128)S(1)}, f32[2,2,64,8,256]{4,3,2,1,0:T(8,128)S(1)}, f32[2,64,8,256]{3,2,1,0:T(8,128)S(1)}) custom-call(s32[1,2,4,2]{3,2,1,0:T(4,128)S(1)} %copy.12.ids_ref, s32[1,2]{1,0:T(1,128)S(1)} %copy-done.4, f32[3]{0:T(128)S(1)} %copy-done.5, f32[4]{0:T(128)S(1)} %copy-done.6, bf16[512,768]{1,0:T(8,128)(2,1)S(1)} %copy-done, ...), custom_call_target="tpu_custom_call" | custom-call | tf_op jit(solution)/shard_map/first_sources/pallas_call | solution.py:611
  36.5 2.4 %collective-permute-start.9 = (f32[2,64,8,256]{3,2,1,0:T(8,128)S(1)}, f32[2,64,8,256]{3,2,1,0:T(8,128)S(1)}, u32[]{:S(2)}, u32[]{:S(2)}) collective-permute-start(f32[2,64,8,256]{3,2,1,0:T(8,128)S(1)} %get-tuple-element.35), channel_id=1, source_target_pairs={{0,1},{1,2},{2,3},{3,4},{4,5},{5,6},{6,7},{7,8},{8,9},{9,10},{10,1... | collective-permute-start | bytes 3145736 | tf_op jit(solution)/shard_map/ppermute | solution.py:531
  38.9 2.9 %first_images.1.image_ref = f32[2,64,8,256]{3,2,1,0:T(8,128)S(1)} custom-call(bf16[512,768]{1,0:T(8,128)(2,1)S(1)} %copy-done, f32[4,70,8,256]{3,2,1,0:T(8,128)S(1)} %get-tuple-element.25.ext.ext_in, f32[3,2,70,8,256]{4,3,2,1,0:T(8,128)S(1)} %get-tuple-element.37.sums_in, f32[2,8,64,8,256]{4,3,2,1,0:T(8,128)S(1)} %get-tuple-element.36.coefs_ref, ...), custom_call_target="tpu_custom_call" | custom-call | tf_op jit(solution)/shard_map/first_images/pallas_call | solution.py:625
  41.7 0.0 copy-start.7
  41.7 0.0 copy-start.8
  41.8 0.0 collective-permute-done.10.rows_any.rows_ref
  41.8 15.2 %receiver_ticks.1.receivers_ref = f32[2,2,64,8,256]{4,3,2,1,0:T(8,128)S(1)} custom-call(f32[3]{0:T(128)S(1)} %copy-done.5, f32[4]{0:T(128)S(1)} %copy-done.6, f32[2,65,8,256]{3,2,1,0:T(8,128)S(1)} %collective-permute-done.10.rows_any.rows_ref, f32[2,65,8,256]{3,2,1,0:T(8,128)S(1)} %collective-permute-done.10.rows_any.rows_ref, ...), custom_call_target="tpu_custom_call" | custom-call | tf_op jit(solution)/shard_map/receiver_ticks/pallas_call | solution.py:635
  57.0 0.0 collective-permute-done.9.rows_ref
  57.0 0.0 copy-done.7
  57.0 0.0 copy-done.8
  57.0 6.3 %source_tick_and_seats.1 = (f32[16,264,128]{2,1,0:T(8,128)}, f32[2,64,8,256]{3,2,1,0:T(8,128)}) custom-call(f32[2,64,8,256]{3,2,1,0:T(8,128)S(1)} %collective-permute-done.9.rows_ref, f32[2,8,64,8,256]{4,3,2,1,0:T(8,128)S(1)} %get-tuple-element.36.coefs_ref, bf16[512,768]{1,0:T(8,128)(2,1)S(1)} %copy-done, ...), custom_call_target="tpu_custom_call" | custom-call | tf_op jit(solution)/shard_map/source_tick_and_seats/pallas_call | solution.py:648
  63.3 4.3 %all-to-all-start = ((f32[16,264,128]{2,1,0:T(8,128)}), f32[16,264,128]{2,1,0:T(8,128)}, u32[]{:S(2)}, u32[]{:S(2)}) async-start(f32[16,264,128]{2,1,0:T(8,128)} %get-tuple-element.42), calls=%async_computation | async-start | bytes 4325376 | tf_op jit(solution)/shard_map/all_to_all | solution.py:668
  67.7 0.0 copy-start.1
  67.7 1.2 %copy-done.1 = f32[2,64,8,256]{3,2,1,0:T(8,128)S(1)} copy-done((f32[2,64,8,256]{3,2,1,0:T(8,128)S(1)}, f32[2,64,8,256]{3,2,1,0:T(8,128)}, u32[]{:S(2)}) %copy-start.1) | copy-done | bytes 1048600
  68.9 3.4 %wavefields.1 = f32[2,2,512,256]{3,2,1,0:T(8,128)} custom-call(f32[2,64,8,256]{3,2,1,0:T(8,128)S(1)} %copy-done.1, f32[2,2,64,8,256]{4,3,2,1,0:T(8,128)S(1)} %receiver_ticks.1.receivers_ref), custom_call_target="tpu_custom_call" | custom-call | tf_op jit(solution)/shard_map/wavefields/pallas_call | solution.py:669
  72.3 43.9 %all-to-all-done.received_ref = f32[16,264,128]{2,1,0:T(8,128)} async-done(((f32[16,264,128]{2,1,0:T(8,128)}), f32[16,264,128]{2,1,0:T(8,128)}, u32[]{:S(2)}, u32[]{:S(2)}) %all-to-all-start) | async-done | bytes 2162720 | tf_op jit(solution)/shard_map/all_to_all | solution.py:668
  116.2 2.5 %image_volume.1 = f32[8,128,128]{2,1,0:T(8,128)} custom-call(f32[16,264,128]{2,1,0:T(8,128)} %all-to-all-done.received_ref), custom_call_target="tpu_custom_call" | custom-call | tf_op jit(solution)/shard_map/image_volume/pallas_call | solution.py:681
Async XLA Ops:
  0.6 11.5 %copy-start = (bf16[512,768]{1,0:T(8,128)(2,1)S(1)}, bf16[512,768]{1,0:T(8,128)(2,1)}, u32[]{:S(2)}) copy-start(bf16[512,768]{1,0:T(8,128)(2,1)} %constant.2.clone.sides_ref) | copy-start | bytes 2359300
  0.6 8.0 %collective-permute-start.1 = (f32[2,128,128]{2,1,0:T(8,128)}, f32[2,128,128]{2,1,0:T(8,128)S(1)}, u32[]{:S(2)}, u32[]{:S(2)}) collective-permute-start(f32[2,128,128]{2,1,0:T(8,128)} %refs_0_.1), channel_id=1, source_target_pairs={{0,4},{1,5},{2,6},{3,7},{4,0},{5,1},{6,2},{7,3},{8,12},{9,13},{10,... | collective-permute-start | bytes 393224 | tf_op jit(solution)/shard_map/ppermute | solution.py:535
  0.9 7.8 %collective-permute-start = (f32[2,128,128]{2,1,0:T(8,128)}, f32[2,128,128]{2,1,0:T(8,128)S(1)}, u32[]{:S(2)}, u32[]{:S(2)}) collective-permute-start(f32[2,128,128]{2,1,0:T(8,128)} %refs_0_.1), channel_id=1, source_target_pairs={{0,2},{1,3},{2,0},{3,1},{4,6},{5,7},{6,4},{7,5},{8,10},{9,11},{10,... | collective-permute-start | bytes 393224 | tf_op jit(solution)/shard_map/ppermute | solution.py:535
  1.1 8.0 %collective-permute-start.2 = (f32[2,128,128]{2,1,0:T(8,128)}, f32[2,128,128]{2,1,0:T(8,128)S(1)}, u32[]{:S(2)}, u32[]{:S(2)}) collective-permute-start(f32[2,128,128]{2,1,0:T(8,128)} %refs_0_.1), channel_id=1, source_target_pairs={{0,8},{1,9},{2,10},{3,11},{4,12},{5,13},{6,14},{7,15},{8,0},{9,1},... | collective-permute-start | bytes 393224 | tf_op jit(solution)/shard_map/ppermute | solution.py:535
  4.2 0.7 copy-start.3
  4.8 12.0 %copy-start.2 = (f32[2,128,128]{2,1,0:T(8,128)S(1)}, f32[2,128,128]{2,1,0:T(8,128)}, u32[]{:S(2)}) copy-start(f32[2,128,128]{2,1,0:T(8,128)} %refs_0_.1) | copy-start | bytes 393220
  9.1 18.6 %copy-start.4 = (s32[1,2]{1,0:T(1,128)S(1)}, s32[1,2]{1,0:T(1,128)}, u32[]{:S(2)}) copy-start(s32[1,2]{1,0:T(1,128)} %orders_ref.3) | copy-start | bytes 28
  9.1 18.6 %copy-start.5 = (f32[3]{0:T(128)S(1)}, f32[3]{0:T(128)}, u32[]{:S(2)}) copy-start(f32[3]{0:T(128)} %weights_ref.3) | copy-start | bytes 40
  9.1 18.6 %copy-start.6 = (f32[4]{0:T(128)S(1)}, f32[4]{0:T(128)}, u32[]{:S(2)}) copy-start(f32[4]{0:T(128)} %rates_ref.3) | copy-start | bytes 52
  9.1 6.2 %collective-permute-start.3 = (f32[2,128,128]{2,1,0:T(8,128)S(1)}, f32[2,128,128]{2,1,0:T(8,128)S(1)}, u32[]{:S(2)}, u32[]{:S(2)}) collective-permute-start(f32[2,128,128]{2,1,0:T(8,128)S(1)} %collective-permute-done.2.refs_2_), channel_id=1, source_target_pairs={{0,4},{1,5},{2,6},{3,7},{4,0},{5,1},{6,2},{7,3},{8,12},{9,13},{10,... | collective-permute-start | bytes 393224 | tf_op jit(solution)/shard_map/ppermute | solution.py:535
  10.1 10.1 %collective-permute-start.6 = (f32[2,128,128]{2,1,0:T(8,128)S(1)}, f32[2,128,128]{2,1,0:T(8,128)S(1)}, u32[]{:S(2)}, u32[]{:S(2)}) collective-permute-start(f32[2,128,128]{2,1,0:T(8,128)S(1)} %collective-permute-done.2.refs_2_), channel_id=1, source_target_pairs={{0,2},{1,3},{2,0},{3,1},{4,6},{5,7},{6,4},{7,5},{8,10},{9,11},{10,... | collective-permute-start | bytes 393224 | tf_op jit(solution)/shard_map/ppermute | solution.py:535
  12.1 8.1 %collective-permute-start.5 = (f32[2,128,128]{2,1,0:T(8,128)S(1)}, f32[2,128,128]{2,1,0:T(8,128)S(1)}, u32[]{:S(2)}, u32[]{:S(2)}) collective-permute-start(f32[2,128,128]{2,1,0:T(8,128)S(1)} %collective-permute-done.1.refs_1_), channel_id=1, source_target_pairs={{0,2},{1,3},{2,0},{3,1},{4,6},{5,7},{6,4},{7,5},{8,10},{9,11},{10,... | collective-permute-start | bytes 393224 | tf_op jit(solution)/shard_map/ppermute | solution.py:535
  15.3 4.8 %collective-permute-start.7 = (f32[2,128,128]{2,1,0:T(8,128)S(1)}, f32[2,128,128]{2,1,0:T(8,128)S(1)}, u32[]{:S(2)}, u32[]{:S(2)}) collective-permute-start(f32[2,128,128]{2,1,0:T(8,128)S(1)} %collective-permute-done.3.refs_3_), channel_id=1, source_target_pairs={{0,2},{1,3},{2,0},{3,1},{4,6},{5,7},{6,4},{7,5},{8,10},{9,11},{10,... | collective-permute-start | bytes 393224 | tf_op jit(solution)/shard_map/ppermute | solution.py:535
  17.5 10.1 %collective-permute-start.4 = (f32[4,2,128,128]{3,2,1,0:T(8,128)S(1)}, f32[4,2,128,128]{3,2,1,0:T(8,128)S(1)}, u32[]{:S(2)}, u32[]{:S(2)}) collective-permute-start(f32[4,2,128,128]{3,2,1,0:T(8,128)S(1)} %stack_tiles.2.t0), channel_id=1, source_target_pairs={{0,1},{1,0},{2,3},{3,2},{4,5},{5,4},{6,7},{7,6},{8,9},{9,8},{10,11... | collective-permute-start | bytes 1572872 | tf_op jit(solution)/shard_map/ppermute | solution.py:535
  20.9 6.8 %collective-permute-start.8 = (f32[4,2,128,128]{3,2,1,0:T(8,128)S(1)}, f32[4,2,128,128]{3,2,1,0:T(8,128)S(1)}, u32[]{:S(2)}, u32[]{:S(2)}) collective-permute-start(f32[4,2,128,128]{3,2,1,0:T(8,128)S(1)} %stack_tiles.3.t2), channel_id=1, source_target_pairs={{0,1},{1,0},{2,3},{3,2},{4,5},{5,4},{6,7},{7,6},{8,9},{9,8},{10,11... | collective-permute-start | bytes 1572872 | tf_op jit(solution)/shard_map/ppermute | solution.py:535
  23.6 18.1 %collective-permute-start.10 = (f32[2,65,8,256]{3,2,1,0:T(8,128)S(1)}, f32[2,65,8,256]{3,2,1,0:T(8,128)S(1)}, u32[]{:S(2)}, u32[]{:S(2)}) collective-permute-start(f32[2,65,8,256]{3,2,1,0:T(8,128)S(1)} %get-tuple-element.39), channel_id=1, source_target_pairs={{0,1},{1,2},{2,3},{3,4},{4,5},{5,6},{6,7},{7,8},{8,9},{9,10},{10,1... | collective-permute-start | bytes 3194888 | tf_op jit(solution)/shard_map/ppermute | solution.py:531
  36.5 20.5 %collective-permute-start.9 = (f32[2,64,8,256]{3,2,1,0:T(8,128)S(1)}, f32[2,64,8,256]{3,2,1,0:T(8,128)S(1)}, u32[]{:S(2)}, u32[]{:S(2)}) collective-permute-start(f32[2,64,8,256]{3,2,1,0:T(8,128)S(1)} %get-tuple-element.35), channel_id=1, source_target_pairs={{0,1},{1,2},{2,3},{3,4},{4,5},{5,6},{6,7},{7,8},{8,9},{9,10},{10,1... | collective-permute-start | bytes 3145736 | tf_op jit(solution)/shard_map/ppermute | solution.py:531
  41.7 15.2 %copy-start.7 = (s32[1,16]{1,0:T(1,128)S(1)}, s32[1,16]{1,0:T(1,128)}, u32[]{:S(2)}) copy-start(s32[1,16]{1,0:T(1,128)} %owners_ref.1) | copy-start | bytes 196
  41.7 15.2 %copy-start.8 = (s32[1,16]{1,0:T(1,128)S(1)}, s32[1,16]{1,0:T(1,128)}, u32[]{:S(2)}) copy-start(s32[1,16]{1,0:T(1,128)} %slots_ref.1) | copy-start | bytes 196
  63.3 52.9 %all-to-all-start = ((f32[16,264,128]{2,1,0:T(8,128)}), f32[16,264,128]{2,1,0:T(8,128)}, u32[]{:S(2)}, u32[]{:S(2)}) async-start(f32[16,264,128]{2,1,0:T(8,128)} %get-tuple-element.42), calls=%async_computation | async-start | bytes 4325376 | tf_op jit(solution)/shard_map/all_to_all | solution.py:668
  67.7 1.2 %copy-start.1 = (f32[2,64,8,256]{3,2,1,0:T(8,128)S(1)}, f32[2,64,8,256]{3,2,1,0:T(8,128)}, u32[]{:S(2)}) copy-start(f32[2,64,8,256]{3,2,1,0:T(8,128)} %get-tuple-element.43.source_ref) | copy-start | bytes 3145732

commit v5 on v4

--- a/solution.py
+++ b/solution.py
@@ -152,7 +152,7 @@
         )
 
 
-def depth_step(state, sums, coefs, sign, emit, unroll=8, summed=False, done=None):
+def depth_step(state, sums, coefs, sign, emit, unroll=16, summed=False, done=None):
     terms, edge = sums.shape[0] + 1, state.edge
     for b in range(state.blocks):
         at = slice(b * LANES, (b + 1) * LANES)
@@ -373,12 +373,14 @@
     steps = coefs_ref.shape[0]
     state = Rows(ext, sums.shape[0])
     take_rows(rows_ref, state)
-    copy.wait()
     blocks = slow.shape[0]
     tiles = blocks * slow.shape[1] // t0.shape[2]
     for which, coefs in enumerate((coefs_up_ref, coefs_ref)):
         for j in range(steps):
             final = which == 1 and j == steps - 1
+            along_y(state, sides_ref, sums)
+            if which == 0 and j == 0:
+                copy.wait()
             if which == 0:
                 first = j * (1 + tiles)
 
@@ -396,7 +398,6 @@
                     if which == 1:
                         states_ref[j, p, r, :, b * LANES : (b + 1) * LANES] = value
 
-            along_y(state, sides_ref, sums)
             depth_step(state, sums, coefs.at[j if which else 0], -1, emit)
             if not final:
                 state.halo()

time: 119 us -> 118 us (level)
  Pallas kernels: 47.4 us -> 46.2 us
where the time goes in v5:
time: 118 us
  Pallas kernels  46.2 us (39%)
  waiting for transfers between devices  44.6 us (38%)
  starting transfers between devices  23.4 us (20%)
  local copies, waits for them, and re-layouts  2.68 us (2%)
    all_to_all x1, waiting for transfers between devices, local(): lax.all_to_all(buffer, axis, split_axis=0, concat_axis=0, tiled=True)  44.1 us
    pallas_call x1, Pallas kernels, local(): call(partial(receiver_kernel, axis), out_shape=pltpu.VMEM((steps, 2) + pl...  14.3 us
    ppermute x9, starting transfers between devices, swapped(): lax.ppermute(shard, axis, [(i, i ^ bits) for i in range(lax.axis_size(axi...  12.6 us
    pallas_call x1, Pallas kernels, local(): call(partial(first_source_kernel, axis), out_shape=(pltpu.VMEM((steps, 2...  8.61 us
    ppermute x2, starting transfers between devices, shifted(): return lax.ppermute(shard, axis, [(i, i + by) for i in range(peers - by)])  6.42 us
    pallas_call x1, Pallas kernels, local(): call(source_kernel, out_shape=(pltpu.HBM((peers, CAP * size + extra, size...  6.17 us
    all_to_all x1, starting transfers between devices, local(): lax.all_to_all(buffer, axis, split_axis=0, concat_axis=0, tiled=True)  4.34 us
    pallas_call x1, Pallas kernels, local(): call(rows_kernel, out_shape=(pltpu.VMEM((4,) + padded, f32), pltpu.VMEM((...  3.79 us
  transfers between devices with their start and end apart: 12, of which 2 were waited for; matrix products, arithmetic and copies ran while one was open for 1% of the time, Pallas kernels for 32%

profile of v5, /device:TPU:15, one launch (start us, length us, event | category | flops | bytes accessed | tf_op | source)
XLA Modules:
  0.0 117.9 jit_solution(10545687847093672037)
XLA Ops:
  0.6 0.0 copy-start
  0.6 0.2 collective-permute-start.1
  0.9 0.2 collective-permute-start
  1.1 2.3 %collective-permute-start.2 = (f32[2,128,128]{2,1,0:T(8,128)}, f32[2,128,128]{2,1,0:T(8,128)S(1)}, u32[]{:S(2)}, u32[]{:S(2)}) collective-permute-start(f32[2,128,128]{2,1,0:T(8,128)} %refs_0_.1), channel_id=1, source_target_pairs={{0,8},{1,9},{2,10},{3,11},{4,12},{5,13},{6,14},{7,15},{8,0},{9,1},... | collective-permute-start | bytes 393224 | tf_op jit(solution)/shard_map/ppermute | solution.py:536
  3.4 0.8 copy.12.ids_ref
  4.2 0.0 copy-start.3
  4.2 0.7 copy-done.3
  4.8 0.0 copy-start.2
  4.8 3.8 %rows.1 = (f32[4,70,8,256]{3,2,1,0:T(8,128)S(1)}, f32[2,65,8,256]{3,2,1,0:T(8,128)S(1)}) custom-call(s32[1,2,4,2]{3,2,1,0:T(4,128)S(1)} %copy.12.ids_ref, s32[1,2]{1,0:T(1,128)S(1)} %copy-done.3, f32[4,512,256]{2,1,0:T(8,128)} %bitcast.2), custom_call_target="tpu_custom_call" | custom-call | tf_op jit(solution)/shard_map/rows/pallas_call | solution.py:567
  8.6 0.0 collective-permute-done.1.refs_1_
  8.7 0.0 collective-permute-done.refs_0_
  8.7 0.4 collective-permute-done.2.refs_2_
  9.1 0.0 copy-start.4
  9.1 0.0 copy-start.5
  9.1 0.0 copy-start.6
  9.1 1.0 collective-permute-start.3
  10.1 2.0 %collective-permute-start.6 = (f32[2,128,128]{2,1,0:T(8,128)S(1)}, f32[2,128,128]{2,1,0:T(8,128)S(1)}, u32[]{:S(2)}, u32[]{:S(2)}) collective-permute-start(f32[2,128,128]{2,1,0:T(8,128)S(1)} %collective-permute-done.2.refs_2_), channel_id=1, source_target_pairs={{0,2},{1,3},{2,0},{3,1},{4,6},{5,7},{6,4},{7,5},{8,10},{9,11},{10,... | collective-permute-start | bytes 393224 | tf_op jit(solution)/shard_map/ppermute | solution.py:536
  12.1 0.0 collective-permute-start.5
  12.1 0.0 copy-done
  12.1 3.2 %first_sums.1 = (f32[3,2,70,8,256]{4,3,2,1,0:T(8,128)S(1)}, f32[3,2,70,8,256]{4,3,2,1,0:T(8,128)S(1)}) custom-call(f32[4,70,8,256]{3,2,1,0:T(8,128)S(1)} %get-tuple-element.25.ext.ext_in, bf16[512,768]{1,0:T(8,128)(2,1)S(1)} %copy-done), custom_call_target="tpu_custom_call" | custom-call | tf_op jit(solution)/shard_map/first_sums/pallas_call | solution.py:592
  15.3 0.0 collective-permute-done.3.refs_3_
  15.3 1.5 %collective-permute-start.7 = (f32[2,128,128]{2,1,0:T(8,128)S(1)}, f32[2,128,128]{2,1,0:T(8,128)S(1)}, u32[]{:S(2)}, u32[]{:S(2)}) collective-permute-start(f32[2,128,128]{2,1,0:T(8,128)S(1)} %collective-permute-done.3.refs_3_), channel_id=1, source_target_pairs={{0,2},{1,3},{2,0},{3,1},{4,6},{5,7},{6,4},{7,5},{8,10},{9,11},{10,... | collective-permute-start | bytes 393224 | tf_op jit(solution)/shard_map/ppermute | solution.py:536
  16.8 0.0 copy-done.2
  16.8 0.7 stack_tiles.2.t0
  17.5 2.6 %collective-permute-start.4 = (f32[4,2,128,128]{3,2,1,0:T(8,128)S(1)}, f32[4,2,128,128]{3,2,1,0:T(8,128)S(1)}, u32[]{:S(2)}, u32[]{:S(2)}) collective-permute-start(f32[4,2,128,128]{3,2,1,0:T(8,128)S(1)} %stack_tiles.2.t0), channel_id=1, source_target_pairs={{0,1},{1,0},{2,3},{3,2},{4,5},{5,4},{6,7},{7,6},{8,9},{9,8},{10,11... | collective-permute-start | bytes 1572872 | tf_op jit(solution)/shard_map/ppermute | solution.py:536
  20.1 0.0 collective-permute-done.5.refs_1_
  20.1 0.0 collective-permute-done.6.refs_2_
  20.1 0.0 collective-permute-done.7.refs_3_
  20.1 0.7 stack_tiles.3.t2
  20.9 2.8 %collective-permute-start.8 = (f32[4,2,128,128]{3,2,1,0:T(8,128)S(1)}, f32[4,2,128,128]{3,2,1,0:T(8,128)S(1)}, u32[]{:S(2)}, u32[]{:S(2)}) collective-permute-start(f32[4,2,128,128]{3,2,1,0:T(8,128)S(1)} %stack_tiles.3.t2), channel_id=1, source_target_pairs={{0,1},{1,0},{2,3},{3,2},{4,5},{5,4},{6,7},{7,6},{8,9},{9,8},{10,11... | collective-permute-start | bytes 1572872 | tf_op jit(solution)/shard_map/ppermute | solution.py:536
  23.6 4.0 %collective-permute-start.10 = (f32[2,65,8,256]{3,2,1,0:T(8,128)S(1)}, f32[2,65,8,256]{3,2,1,0:T(8,128)S(1)}, u32[]{:S(2)}, u32[]{:S(2)}) collective-permute-start(f32[2,65,8,256]{3,2,1,0:T(8,128)S(1)} %get-tuple-element.39), channel_id=1, source_target_pairs={{0,1},{1,2},{2,3},{3,4},{4,5},{5,6},{6,7},{7,8},{8,9},{9,10},{10,1... | collective-permute-start | bytes 3194888 | tf_op jit(solution)/shard_map/ppermute | solution.py:532
  27.7 0.0 collective-permute-done.4.t1
  27.7 0.0 collective-permute-done.8.t3
  27.7 0.0 copy-done.4
  27.7 0.0 copy-done.5
  27.7 0.0 copy-done.6
  27.7 8.6 %first_sources.1 = (f32[2,8,64,8,256]{4,3,2,1,0:T(8,128)S(1)}, f32[2,2,64,8,256]{4,3,2,1,0:T(8,128)S(1)}, f32[2,64,8,256]{3,2,1,0:T(8,128)S(1)}) custom-call(s32[1,2,4,2]{3,2,1,0:T(4,128)S(1)} %copy.12.ids_ref, s32[1,2]{1,0:T(1,128)S(1)} %copy-done.4, f32[3]{0:T(128)S(1)} %copy-done.5, f32[4]{0:T(128)S(1)} %copy-done.6, bf16[512,768]{1,0:T(8,128)(2,1)S(1)} %copy-done, ...), custom_call_target="tpu_custom_call" | custom-call | tf_op jit(solution)/shard_map/first_sources/pallas_call | solution.py:612
  36.3 2.4 %collective-permute-start.9 = (f32[2,64,8,256]{3,2,1,0:T(8,128)S(1)}, f32[2,64,8,256]{3,2,1,0:T(8,128)S(1)}, u32[]{:S(2)}, u32[]{:S(2)}) collective-permute-start(f32[2,64,8,256]{3,2,1,0:T(8,128)S(1)} %get-tuple-element.35), channel_id=1, source_target_pairs={{0,1},{1,2},{2,3},{3,4},{4,5},{5,6},{6,7},{7,8},{8,9},{9,10},{10,1... | collective-permute-start | bytes 3145736 | tf_op jit(solution)/shard_map/ppermute | solution.py:532
  38.7 2.8 %first_images.1.image_ref = f32[2,64,8,256]{3,2,1,0:T(8,128)S(1)} custom-call(bf16[512,768]{1,0:T(8,128)(2,1)S(1)} %copy-done, f32[4,70,8,256]{3,2,1,0:T(8,128)S(1)} %get-tuple-element.25.ext.ext_in, f32[3,2,70,8,256]{4,3,2,1,0:T(8,128)S(1)} %get-tuple-element.37.sums_in, f32[2,8,64,8,256]{4,3,2,1,0:T(8,128)S(1)} %get-tuple-element.36.coefs_ref, ...), custom_call_target="tpu_custom_call" | custom-call | tf_op jit(solution)/shard_map/first_images/pallas_call | solution.py:626
  41.5 0.0 copy-start.7
  41.5 0.0 copy-start.8
  41.5 0.0 collective-permute-done.10.rows_any.rows_ref
  41.5 14.3 %receiver_ticks.1.receivers_ref = f32[2,2,64,8,256]{4,3,2,1,0:T(8,128)S(1)} custom-call(f32[3]{0:T(128)S(1)} %copy-done.5, f32[4]{0:T(128)S(1)} %copy-done.6, f32[2,65,8,256]{3,2,1,0:T(8,128)S(1)} %collective-permute-done.10.rows_any.rows_ref, f32[2,65,8,256]{3,2,1,0:T(8,128)S(1)} %collective-permute-done.10.rows_any.rows_ref, ...), custom_call_target="tpu_custom_call" | custom-call | tf_op jit(solution)/shard_map/receiver_ticks/pallas_call | solution.py:636
  55.9 0.0 collective-permute-done.9.rows_ref
  55.9 0.0 copy-done.7
  55.9 0.0 copy-done.8
  55.9 6.2 %source_tick_and_seats.1 = (f32[16,264,128]{2,1,0:T(8,128)}, f32[2,64,8,256]{3,2,1,0:T(8,128)}) custom-call(f32[2,64,8,256]{3,2,1,0:T(8,128)S(1)} %collective-permute-done.9.rows_ref, f32[2,8,64,8,256]{4,3,2,1,0:T(8,128)S(1)} %get-tuple-element.36.coefs_ref, bf16[512,768]{1,0:T(8,128)(2,1)S(1)} %copy-done, ...), custom_call_target="tpu_custom_call" | custom-call | tf_op jit(solution)/shard_map/source_tick_and_seats/pallas_call | solution.py:649
  62.1 4.3 %all-to-all-start = ((f32[16,264,128]{2,1,0:T(8,128)}), f32[16,264,128]{2,1,0:T(8,128)}, u32[]{:S(2)}, u32[]{:S(2)}) async-start(f32[16,264,128]{2,1,0:T(8,128)} %get-tuple-element.42), calls=%async_computation | async-start | bytes 4325376 | tf_op jit(solution)/shard_map/all_to_all | solution.py:669
  66.4 0.0 copy-start.1
  66.5 1.2 %copy-done.1 = f32[2,64,8,256]{3,2,1,0:T(8,128)S(1)} copy-done((f32[2,64,8,256]{3,2,1,0:T(8,128)S(1)}, f32[2,64,8,256]{3,2,1,0:T(8,128)}, u32[]{:S(2)}) %copy-start.1) | copy-done | bytes 1048600
  67.7 3.4 %wavefields.1 = f32[2,2,512,256]{3,2,1,0:T(8,128)} custom-call(f32[2,64,8,256]{3,2,1,0:T(8,128)S(1)} %copy-done.1, f32[2,2,64,8,256]{4,3,2,1,0:T(8,128)S(1)} %receiver_ticks.1.receivers_ref), custom_call_target="tpu_custom_call" | custom-call | tf_op jit(solution)/shard_map/wavefields/pallas_call | solution.py:670
  71.1 44.1 %all-to-all-done.received_ref = f32[16,264,128]{2,1,0:T(8,128)} async-done(((f32[16,264,128]{2,1,0:T(8,128)}), f32[16,264,128]{2,1,0:T(8,128)}, u32[]{:S(2)}, u32[]{:S(2)}) %all-to-all-start) | async-done | bytes 2162720 | tf_op jit(solution)/shard_map/all_to_all | solution.py:669
  115.2 2.5 %image_volume.1 = f32[8,128,128]{2,1,0:T(8,128)} custom-call(f32[16,264,128]{2,1,0:T(8,128)} %all-to-all-done.received_ref), custom_call_target="tpu_custom_call" | custom-call | tf_op jit(solution)/shard_map/image_volume/pallas_call | solution.py:682
Async XLA Ops:
  0.6 11.5 %copy-start = (bf16[512,768]{1,0:T(8,128)(2,1)S(1)}, bf16[512,768]{1,0:T(8,128)(2,1)}, u32[]{:S(2)}) copy-start(bf16[512,768]{1,0:T(8,128)(2,1)} %constant.2.clone.sides_ref) | copy-start | bytes 2359300
  0.6 8.0 %collective-permute-start.1 = (f32[2,128,128]{2,1,0:T(8,128)}, f32[2,128,128]{2,1,0:T(8,128)S(1)}, u32[]{:S(2)}, u32[]{:S(2)}) collective-permute-start(f32[2,128,128]{2,1,0:T(8,128)} %refs_0_.1), channel_id=1, source_target_pairs={{0,4},{1,5},{2,6},{3,7},{4,0},{5,1},{6,2},{7,3},{8,12},{9,13},{10,... | collective-permute-start | bytes 393224 | tf_op jit(solution)/shard_map/ppermute | solution.py:536
  0.9 7.8 %collective-permute-start = (f32[2,128,128]{2,1,0:T(8,128)}, f32[2,128,128]{2,1,0:T(8,128)S(1)}, u32[]{:S(2)}, u32[]{:S(2)}) collective-permute-start(f32[2,128,128]{2,1,0:T(8,128)} %refs_0_.1), channel_id=1, source_target_pairs={{0,2},{1,3},{2,0},{3,1},{4,6},{5,7},{6,4},{7,5},{8,10},{9,11},{10,... | collective-permute-start | bytes 393224 | tf_op jit(solution)/shard_map/ppermute | solution.py:536
  1.1 8.0 %collective-permute-start.2 = (f32[2,128,128]{2,1,0:T(8,128)}, f32[2,128,128]{2,1,0:T(8,128)S(1)}, u32[]{:S(2)}, u32[]{:S(2)}) collective-permute-start(f32[2,128,128]{2,1,0:T(8,128)} %refs_0_.1), channel_id=1, source_target_pairs={{0,8},{1,9},{2,10},{3,11},{4,12},{5,13},{6,14},{7,15},{8,0},{9,1},... | collective-permute-start | bytes 393224 | tf_op jit(solution)/shard_map/ppermute | solution.py:536
  4.2 0.7 copy-start.3
  4.8 12.0 %copy-start.2 = (f32[2,128,128]{2,1,0:T(8,128)S(1)}, f32[2,128,128]{2,1,0:T(8,128)}, u32[]{:S(2)}) copy-start(f32[2,128,128]{2,1,0:T(8,128)} %refs_0_.1) | copy-start | bytes 393220
  9.1 18.6 %copy-start.4 = (s32[1,2]{1,0:T(1,128)S(1)}, s32[1,2]{1,0:T(1,128)}, u32[]{:S(2)}) copy-start(s32[1,2]{1,0:T(1,128)} %orders_ref.3) | copy-start | bytes 28
  9.1 18.6 %copy-start.5 = (f32[3]{0:T(128)S(1)}, f32[3]{0:T(128)}, u32[]{:S(2)}) copy-start(f32[3]{0:T(128)} %weights_ref.3) | copy-start | bytes 40
  9.1 18.6 %copy-start.6 = (f32[4]{0:T(128)S(1)}, f32[4]{0:T(128)}, u32[]{:S(2)}) copy-start(f32[4]{0:T(128)} %rates_ref.3) | copy-start | bytes 52
  9.1 6.2 %collective-permute-start.3 = (f32[2,128,128]{2,1,0:T(8,128)S(1)}, f32[2,128,128]{2,1,0:T(8,128)S(1)}, u32[]{:S(2)}, u32[]{:S(2)}) collective-permute-start(f32[2,128,128]{2,1,0:T(8,128)S(1)} %collective-permute-done.2.refs_2_), channel_id=1, source_target_pairs={{0,4},{1,5},{2,6},{3,7},{4,0},{5,1},{6,2},{7,3},{8,12},{9,13},{10,... | collective-permute-start | bytes 393224 | tf_op jit(solution)/shard_map/ppermute | solution.py:536
  10.1 10.1 %collective-permute-start.6 = (f32[2,128,128]{2,1,0:T(8,128)S(1)}, f32[2,128,128]{2,1,0:T(8,128)S(1)}, u32[]{:S(2)}, u32[]{:S(2)}) collective-permute-start(f32[2,128,128]{2,1,0:T(8,128)S(1)} %collective-permute-done.2.refs_2_), channel_id=1, source_target_pairs={{0,2},{1,3},{2,0},{3,1},{4,6},{5,7},{6,4},{7,5},{8,10},{9,11},{10,... | collective-permute-start | bytes 393224 | tf_op jit(solution)/shard_map/ppermute | solution.py:536
  12.1 8.1 %collective-permute-start.5 = (f32[2,128,128]{2,1,0:T(8,128)S(1)}, f32[2,128,128]{2,1,0:T(8,128)S(1)}, u32[]{:S(2)}, u32[]{:S(2)}) collective-permute-start(f32[2,128,128]{2,1,0:T(8,128)S(1)} %collective-permute-done.1.refs_1_), channel_id=1, source_target_pairs={{0,2},{1,3},{2,0},{3,1},{4,6},{5,7},{6,4},{7,5},{8,10},{9,11},{10,... | collective-permute-start | bytes 393224 | tf_op jit(solution)/shard_map/ppermute | solution.py:536
  15.3 4.8 %collective-permute-start.7 = (f32[2,128,128]{2,1,0:T(8,128)S(1)}, f32[2,128,128]{2,1,0:T(8,128)S(1)}, u32[]{:S(2)}, u32[]{:S(2)}) collective-permute-start(f32[2,128,128]{2,1,0:T(8,128)S(1)} %collective-permute-done.3.refs_3_), channel_id=1, source_target_pairs={{0,2},{1,3},{2,0},{3,1},{4,6},{5,7},{6,4},{7,5},{8,10},{9,11},{10,... | collective-permute-start | bytes 393224 | tf_op jit(solution)/shard_map/ppermute | solution.py:536
  17.5 10.1 %collective-permute-start.4 = (f32[4,2,128,128]{3,2,1,0:T(8,128)S(1)}, f32[4,2,128,128]{3,2,1,0:T(8,128)S(1)}, u32[]{:S(2)}, u32[]{:S(2)}) collective-permute-start(f32[4,2,128,128]{3,2,1,0:T(8,128)S(1)} %stack_tiles.2.t0), channel_id=1, source_target_pairs={{0,1},{1,0},{2,3},{3,2},{4,5},{5,4},{6,7},{7,6},{8,9},{9,8},{10,11... | collective-permute-start | bytes 1572872 | tf_op jit(solution)/shard_map/ppermute | solution.py:536
  20.9 6.8 %collective-permute-start.8 = (f32[4,2,128,128]{3,2,1,0:T(8,128)S(1)}, f32[4,2,128,128]{3,2,1,0:T(8,128)S(1)}, u32[]{:S(2)}, u32[]{:S(2)}) collective-permute-start(f32[4,2,128,128]{3,2,1,0:T(8,128)S(1)} %stack_tiles.3.t2), channel_id=1, source_target_pairs={{0,1},{1,0},{2,3},{3,2},{4,5},{5,4},{6,7},{7,6},{8,9},{9,8},{10,11... | collective-permute-start | bytes 1572872 | tf_op jit(solution)/shard_map/ppermute | solution.py:536
  23.6 17.9 %collective-permute-start.10 = (f32[2,65,8,256]{3,2,1,0:T(8,128)S(1)}, f32[2,65,8,256]{3,2,1,0:T(8,128)S(1)}, u32[]{:S(2)}, u32[]{:S(2)}) collective-permute-start(f32[2,65,8,256]{3,2,1,0:T(8,128)S(1)} %get-tuple-element.39), channel_id=1, source_target_pairs={{0,1},{1,2},{2,3},{3,4},{4,5},{5,6},{6,7},{7,8},{8,9},{9,10},{10,1... | collective-permute-start | bytes 3194888 | tf_op jit(solution)/shard_map/ppermute | solution.py:532
  36.3 19.5 %collective-permute-start.9 = (f32[2,64,8,256]{3,2,1,0:T(8,128)S(1)}, f32[2,64,8,256]{3,2,1,0:T(8,128)S(1)}, u32[]{:S(2)}, u32[]{:S(2)}) collective-permute-start(f32[2,64,8,256]{3,2,1,0:T(8,128)S(1)} %get-tuple-element.35), channel_id=1, source_target_pairs={{0,1},{1,2},{2,3},{3,4},{4,5},{5,6},{6,7},{7,8},{8,9},{9,10},{10,1... | collective-permute-start | bytes 3145736 | tf_op jit(solution)/shard_map/ppermute | solution.py:532
  41.5 14.4 %copy-start.7 = (s32[1,16]{1,0:T(1,128)S(1)}, s32[1,16]{1,0:T(1,128)}, u32[]{:S(2)}) copy-start(s32[1,16]{1,0:T(1,128)} %owners_ref.1) | copy-start | bytes 196
  41.5 14.4 %copy-start.8 = (s32[1,16]{1,0:T(1,128)S(1)}, s32[1,16]{1,0:T(1,128)}, u32[]{:S(2)}) copy-start(s32[1,16]{1,0:T(1,128)} %slots_ref.1) | copy-start | bytes 196
  62.1 53.1 %all-to-all-start = ((f32[16,264,128]{2,1,0:T(8,128)}), f32[16,264,128]{2,1,0:T(8,128)}, u32[]{:S(2)}, u32[]{:S(2)}) async-start(f32[16,264,128]{2,1,0:T(8,128)} %get-tuple-element.42), calls=%async_computation | async-start | bytes 4325376 | tf_op jit(solution)/shard_map/all_to_all | solution.py:669
  66.4 1.2 %copy-start.1 = (f32[2,64,8,256]{3,2,1,0:T(8,128)S(1)}, f32[2,64,8,256]{3,2,1,0:T(8,128)}, u32[]{:S(2)}) copy-start(f32[2,64,8,256]{3,2,1,0:T(8,128)} %get-tuple-element.43.source_ref) | copy-start | bytes 3145732

commit v6 on v5

--- a/solution.py
+++ b/solution.py
@@ -263,11 +263,10 @@
     copy.wait()
 
 
-def sums_kernel(ext, sides_ref, source_sums, receiver_sums):
-    edge = source_sums.shape[0]
-    for first, sums in ((0, source_sums), (2, receiver_sums)):
-        along_y(Rows(ext, edge, first, 2), sides_ref, sums)
-        along_x(sums, edge)
+def sums_kernel(first, ext, sides_ref, sums):
+    edge = sums.shape[0]
+    along_y(Rows(ext, edge, first, 2), sides_ref, sums)
+    along_x(sums, edge)
 
 
 def series(slow, order, weights_ref, rates_ref, coefs_ref, j):
@@ -589,17 +588,19 @@
     across += [swapped(v, axis, 2) for v in line[1:]]
     line.append(swapped(line[-1], axis, 4))
     ext = in_vmem(ext)
-    source_sums, receiver_sums = call(
-        sums_kernel,
-        out_shape=(pltpu.VMEM((edge, 2) + padded, f32),) * 2,
-        in_specs=[VMEM, VMEM],
-        out_specs=(VMEM, VMEM),
-        name="first_sums",
-    )(ext, sides)
-    line[-1], source_sums, receiver_sums = lax.optimization_barrier(
-        (line[-1], source_sums, receiver_sums)
-    )
+
+    def summed(first):
+        return call(
+            partial(sums_kernel, first),
+            out_shape=pltpu.VMEM((edge, 2) + padded, f32),
+            in_specs=[VMEM, VMEM],
+            out_specs=VMEM,
+            name="first_sums",
+        )(ext, sides)
+
+    line[-1], source_sums = lax.optimization_barrier((line[-1], summed(0)))
     across.append(swapped(line[-1], axis, 2))
+    across[0], receiver_sums = lax.optimization_barrier((across[0], summed(2)))
     tiles = {0: stacked(line)}
     tiles[1] = swapped(tiles[0], axis, 1)
     tiles[2] = stacked(across)

time: 118 us -> 118 us (level)
    pallas_call x1 -> x2, Pallas kernels: 3.19 us -> 3.2 us  [summed(): call(partial(sums_kernel, first), out_shape=pltpu.VMEM((edge, 2) + padded...]
where the time goes in v6:
time: 118 us; the launch traced here: 117 us
  Pallas kernels  46.2 us (39%)
  waiting for transfers between devices  44.6 us (38%)
  starting transfers between devices  22.8 us (19%)
  local copies, waits for them, and re-layouts  2.69 us (2%)
    all_to_all x1, waiting for transfers between devices, local(): lax.all_to_all(buffer, axis, split_axis=0, concat_axis=0, tiled=True)  44.1 us
    pallas_call x1, Pallas kernels, local(): call(partial(receiver_kernel, axis), out_shape=pltpu.VMEM((steps, 2) + pl...  14.3 us
    ppermute x9, starting transfers between devices, swapped(): lax.ppermute(shard, axis, [(i, i ^ bits) for i in range(lax.axis_size(axi...  11.9 us
    pallas_call x1, Pallas kernels, local(): call(partial(first_source_kernel, axis), out_shape=(pltpu.VMEM((steps, 2...  8.61 us
    ppermute x2, starting transfers between devices, shifted(): return lax.ppermute(shard, axis, [(i, i + by) for i in range(peers - by)])  6.52 us
    pallas_call x1, Pallas kernels, local(): call(source_kernel, out_shape=(pltpu.HBM((peers, CAP * size + extra, size...  6.08 us
    all_to_all x1, starting transfers between devices, local(): lax.all_to_all(buffer, axis, split_axis=0, concat_axis=0, tiled=True)  4.36 us
    pallas_call x1, Pallas kernels, local(): call(rows_kernel, out_shape=(pltpu.VMEM((4,) + padded, f32), pltpu.VMEM((...  3.79 us
  transfers between devices with their start and end apart: 12, of which 2 were waited for; matrix products, arithmetic and copies ran while one was open for 1% of the time, Pallas kernels for 32%

profile of v6, /device:TPU:15, one launch (start us, length us, event | category | flops | bytes accessed | tf_op | source)
XLA Modules:
  0.0 117.3 jit_solution(11687005357560627238)
XLA Ops:
  0.6 0.0 copy-start
  0.6 0.2 collective-permute-start.1
  0.9 0.2 collective-permute-start
  1.1 2.3 %collective-permute-start.2 = (f32[2,128,128]{2,1,0:T(8,128)}, f32[2,128,128]{2,1,0:T(8,128)S(1)}, u32[]{:S(2)}, u32[]{:S(2)}) collective-permute-start(f32[2,128,128]{2,1,0:T(8,128)} %refs_0_.1), channel_id=1, source_target_pairs={{0,8},{1,9},{2,10},{3,11},{4,12},{5,13},{6,14},{7,15},{8,0},{9,1},... | collective-permute-start | bytes 393224 | tf_op jit(solution)/shard_map/ppermute | solution.py:535
  3.4 0.8 copy.12.ids_ref
  4.2 0.0 copy-start.3
  4.2 0.7 copy-done.3
  4.8 3.8 %rows.1 = (f32[4,70,8,256]{3,2,1,0:T(8,128)S(1)}, f32[2,65,8,256]{3,2,1,0:T(8,128)S(1)}) custom-call(s32[1,2,4,2]{3,2,1,0:T(4,128)S(1)} %copy.12.ids_ref, s32[1,2]{1,0:T(1,128)S(1)} %copy-done.3, f32[4,512,256]{2,1,0:T(8,128)} %bitcast.2), custom_call_target="tpu_custom_call" | custom-call | tf_op jit(solution)/shard_map/rows/pallas_call | solution.py:566
  8.6 0.0 collective-permute-done.1.refs_1_
  8.7 0.0 collective-permute-done.refs_0_
  8.7 0.4 collective-permute-done.2.refs_2_
  9.1 0.9 collective-permute-start.3
  10.0 2.0 %collective-permute-start.6 = (f32[2,128,128]{2,1,0:T(8,128)S(1)}, f32[2,128,128]{2,1,0:T(8,128)S(1)}, u32[]{:S(2)}, u32[]{:S(2)}) collective-permute-start(f32[2,128,128]{2,1,0:T(8,128)S(1)} %collective-permute-done.2.refs_2_), channel_id=1, source_target_pairs={{0,2},{1,3},{2,0},{3,1},{4,6},{5,7},{6,4},{7,5},{8,10},{9,11},{10,... | collective-permute-start | bytes 393224 | tf_op jit(solution)/shard_map/ppermute | solution.py:535
  12.1 0.0 collective-permute-start.5
  12.1 0.0 copy-done
  12.1 1.6 %first_sums.2.sums_in = f32[3,2,70,8,256]{4,3,2,1,0:T(8,128)S(1)} custom-call(f32[4,70,8,256]{3,2,1,0:T(8,128)S(1)} %get-tuple-element.24.ext.ext_in, bf16[512,768]{1,0:T(8,128)(2,1)S(1)} %copy-done), custom_call_target="tpu_custom_call" | custom-call | tf_op jit(solution)/shard_map/first_sums/pallas_call | solution.py:593
  13.7 0.0 copy-start.2
  13.7 0.0 copy-start.4
  13.7 0.0 copy-start.5
  13.8 0.0 copy-start.6
  13.8 0.0 collective-permute-done.3.refs_3_
  13.8 1.5 %collective-permute-start.7 = (f32[2,128,128]{2,1,0:T(8,128)S(1)}, f32[2,128,128]{2,1,0:T(8,128)S(1)}, u32[]{:S(2)}, u32[]{:S(2)}) collective-permute-start(f32[2,128,128]{2,1,0:T(8,128)S(1)} %collective-permute-done.3.refs_3_), channel_id=1, source_target_pairs={{0,2},{1,3},{2,0},{3,1},{4,6},{5,7},{6,4},{7,5},{8,10},{9,11},{10,... | collective-permute-start | bytes 393224 | tf_op jit(solution)/shard_map/ppermute | solution.py:535
  15.3 1.6 %first_sums.3.sums_in = f32[3,2,70,8,256]{4,3,2,1,0:T(8,128)S(1)} custom-call(f32[4,70,8,256]{3,2,1,0:T(8,128)S(1)} %get-tuple-element.24.ext.ext_in, bf16[512,768]{1,0:T(8,128)(2,1)S(1)} %copy-done), custom_call_target="tpu_custom_call" | custom-call | tf_op jit(solution)/shard_map/first_sums/pallas_call | solution.py:593
  16.9 0.0 copy-done.2
  16.9 0.7 stack_tiles.2.t0
  17.6 2.6 %collective-permute-start.4 = (f32[4,2,128,128]{3,2,1,0:T(8,128)S(1)}, f32[4,2,128,128]{3,2,1,0:T(8,128)S(1)}, u32[]{:S(2)}, u32[]{:S(2)}) collective-permute-start(f32[4,2,128,128]{3,2,1,0:T(8,128)S(1)} %stack_tiles.2.t0), channel_id=1, source_target_pairs={{0,1},{1,0},{2,3},{3,2},{4,5},{5,4},{6,7},{7,6},{8,9},{9,8},{10,11... | collective-permute-start | bytes 1572872 | tf_op jit(solution)/shard_map/ppermute | solution.py:535
  20.2 0.0 collective-permute-done.5.refs_1_
  20.2 0.0 collective-permute-done.6.refs_2_
  20.2 0.0 collective-permute-done.7.refs_3_
  20.2 0.7 stack_tiles.3.t2
  21.0 2.0 %collective-permute-start.8 = (f32[4,2,128,128]{3,2,1,0:T(8,128)S(1)}, f32[4,2,128,128]{3,2,1,0:T(8,128)S(1)}, u32[]{:S(2)}, u32[]{:S(2)}) collective-permute-start(f32[4,2,128,128]{3,2,1,0:T(8,128)S(1)} %stack_tiles.3.t2), channel_id=1, source_target_pairs={{0,1},{1,0},{2,3},{3,2},{4,5},{5,4},{6,7},{7,6},{8,9},{9,8},{10,11... | collective-permute-start | bytes 1572872 | tf_op jit(solution)/shard_map/ppermute | solution.py:535
  23.0 4.1 %collective-permute-start.10 = (f32[2,65,8,256]{3,2,1,0:T(8,128)S(1)}, f32[2,65,8,256]{3,2,1,0:T(8,128)S(1)}, u32[]{:S(2)}, u32[]{:S(2)}) collective-permute-start(f32[2,65,8,256]{3,2,1,0:T(8,128)S(1)} %get-tuple-element.37), channel_id=1, source_target_pairs={{0,1},{1,2},{2,3},{3,4},{4,5},{5,6},{6,7},{7,8},{8,9},{9,10},{10,1... | collective-permute-start | bytes 3194888 | tf_op jit(solution)/shard_map/ppermute | solution.py:531
  27.1 0.0 collective-permute-done.4.t1
  27.1 0.0 collective-permute-done.8.t3
  27.1 0.0 copy-done.4
  27.1 0.0 copy-done.5
  27.1 0.0 copy-done.6
  27.2 8.6 %first_sources.1 = (f32[2,8,64,8,256]{4,3,2,1,0:T(8,128)S(1)}, f32[2,2,64,8,256]{4,3,2,1,0:T(8,128)S(1)}, f32[2,64,8,256]{3,2,1,0:T(8,128)S(1)}) custom-call(s32[1,2,4,2]{3,2,1,0:T(4,128)S(1)} %copy.12.ids_ref, s32[1,2]{1,0:T(1,128)S(1)} %copy-done.4, f32[3]{0:T(128)S(1)} %copy-done.5, f32[4]{0:T(128)S(1)} %copy-done.6, bf16[512,768]{1,0:T(8,128)(2,1)S(1)} %copy-done, ...), custom_call_target="tpu_custom_call" | custom-call | tf_op jit(solution)/shard_map/first_sources/pallas_call | solution.py:613
  35.8 2.4 %collective-permute-start.9 = (f32[2,64,8,256]{3,2,1,0:T(8,128)S(1)}, f32[2,64,8,256]{3,2,1,0:T(8,128)S(1)}, u32[]{:S(2)}, u32[]{:S(2)}) collective-permute-start(f32[2,64,8,256]{3,2,1,0:T(8,128)S(1)} %get-tuple-element.33), channel_id=1, source_target_pairs={{0,1},{1,2},{2,3},{3,4},{4,5},{5,6},{6,7},{7,8},{8,9},{9,10},{10,1... | collective-permute-start | bytes 3145736 | tf_op jit(solution)/shard_map/ppermute | solution.py:531
  38.2 2.8 %first_images.1.image_ref = f32[2,64,8,256]{3,2,1,0:T(8,128)S(1)} custom-call(bf16[512,768]{1,0:T(8,128)(2,1)S(1)} %copy-done, f32[4,70,8,256]{3,2,1,0:T(8,128)S(1)} %get-tuple-element.24.ext.ext_in, f32[3,2,70,8,256]{4,3,2,1,0:T(8,128)S(1)} %first_sums.3.sums_in, f32[2,8,64,8,256]{4,3,2,1,0:T(8,128)S(1)} %get-tuple-element.34.coefs_ref, ...), custom_call_target="tpu_custom_call" | custom-call | tf_op jit(solution)/shard_map/first_images/pallas_call | solution.py:627
  40.9 0.0 copy-start.7
  41.0 0.0 copy-start.8
  41.0 0.0 collective-permute-done.10.rows_any.rows_ref
  41.0 14.3 %receiver_ticks.1.receivers_ref = f32[2,2,64,8,256]{4,3,2,1,0:T(8,128)S(1)} custom-call(f32[3]{0:T(128)S(1)} %copy-done.5, f32[4]{0:T(128)S(1)} %copy-done.6, f32[2,65,8,256]{3,2,1,0:T(8,128)S(1)} %collective-permute-done.10.rows_any.rows_ref, f32[2,65,8,256]{3,2,1,0:T(8,128)S(1)} %collective-permute-done.10.rows_any.rows_ref, ...), custom_call_target="tpu_custom_call" | custom-call | tf_op jit(solution)/shard_map/receiver_ticks/pallas_call | solution.py:637
  55.3 0.0 collective-permute-done.9.rows_ref
  55.3 0.0 copy-done.7
  55.3 0.0 copy-done.8
  55.4 6.1 %source_tick_and_seats.1 = (f32[16,264,128]{2,1,0:T(8,128)}, f32[2,64,8,256]{3,2,1,0:T(8,128)}) custom-call(f32[2,64,8,256]{3,2,1,0:T(8,128)S(1)} %collective-permute-done.9.rows_ref, f32[2,8,64,8,256]{4,3,2,1,0:T(8,128)S(1)} %get-tuple-element.34.coefs_ref, bf16[512,768]{1,0:T(8,128)(2,1)S(1)} %copy-done, ...), custom_call_target="tpu_custom_call" | custom-call | tf_op jit(solution)/shard_map/source_tick_and_seats/pallas_call | solution.py:650
  61.4 4.4 %all-to-all-start = ((f32[16,264,128]{2,1,0:T(8,128)}), f32[16,264,128]{2,1,0:T(8,128)}, u32[]{:S(2)}, u32[]{:S(2)}) async-start(f32[16,264,128]{2,1,0:T(8,128)} %get-tuple-element.40), calls=%async_computation | async-start | bytes 4325376 | tf_op jit(solution)/shard_map/all_to_all | solution.py:670
  65.8 0.0 copy-start.1
  65.8 1.2 %copy-done.1 = f32[2,64,8,256]{3,2,1,0:T(8,128)S(1)} copy-done((f32[2,64,8,256]{3,2,1,0:T(8,128)S(1)}, f32[2,64,8,256]{3,2,1,0:T(8,128)}, u32[]{:S(2)}) %copy-start.1) | copy-done | bytes 1048600
  67.0 3.4 %wavefields.1 = f32[2,2,512,256]{3,2,1,0:T(8,128)} custom-call(f32[2,64,8,256]{3,2,1,0:T(8,128)S(1)} %copy-done.1, f32[2,2,64,8,256]{4,3,2,1,0:T(8,128)S(1)} %receiver_ticks.1.receivers_ref), custom_call_target="tpu_custom_call" | custom-call | tf_op jit(solution)/shard_map/wavefields/pallas_call | solution.py:671
  70.4 44.1 %all-to-all-done.received_ref = f32[16,264,128]{2,1,0:T(8,128)} async-done(((f32[16,264,128]{2,1,0:T(8,128)}), f32[16,264,128]{2,1,0:T(8,128)}, u32[]{:S(2)}, u32[]{:S(2)}) %all-to-all-start) | async-done | bytes 2162720 | tf_op jit(solution)/shard_map/all_to_all | solution.py:670
  114.6 2.5 %image_volume.1 = f32[8,128,128]{2,1,0:T(8,128)} custom-call(f32[16,264,128]{2,1,0:T(8,128)} %all-to-all-done.received_ref), custom_call_target="tpu_custom_call" | custom-call | tf_op jit(solution)/shard_map/image_volume/pallas_call | solution.py:683
Async XLA Ops:
  0.6 11.5 %copy-start = (bf16[512,768]{1,0:T(8,128)(2,1)S(1)}, bf16[512,768]{1,0:T(8,128)(2,1)}, u32[]{:S(2)}) copy-start(bf16[512,768]{1,0:T(8,128)(2,1)} %constant.2.clone.sides_ref) | copy-start | bytes 2359300
  0.6 8.0 %collective-permute-start.1 = (f32[2,128,128]{2,1,0:T(8,128)}, f32[2,128,128]{2,1,0:T(8,128)S(1)}, u32[]{:S(2)}, u32[]{:S(2)}) collective-permute-start(f32[2,128,128]{2,1,0:T(8,128)} %refs_0_.1), channel_id=1, source_target_pairs={{0,4},{1,5},{2,6},{3,7},{4,0},{5,1},{6,2},{7,3},{8,12},{9,13},{10,... | collective-permute-start | bytes 393224 | tf_op jit(solution)/shard_map/ppermute | solution.py:535
  0.9 7.8 %collective-permute-start = (f32[2,128,128]{2,1,0:T(8,128)}, f32[2,128,128]{2,1,0:T(8,128)S(1)}, u32[]{:S(2)}, u32[]{:S(2)}) collective-permute-start(f32[2,128,128]{2,1,0:T(8,128)} %refs_0_.1), channel_id=1, source_target_pairs={{0,2},{1,3},{2,0},{3,1},{4,6},{5,7},{6,4},{7,5},{8,10},{9,11},{10,... | collective-permute-start | bytes 393224 | tf_op jit(solution)/shard_map/ppermute | solution.py:535
  1.1 8.0 %collective-permute-start.2 = (f32[2,128,128]{2,1,0:T(8,128)}, f32[2,128,128]{2,1,0:T(8,128)S(1)}, u32[]{:S(2)}, u32[]{:S(2)}) collective-permute-start(f32[2,128,128]{2,1,0:T(8,128)} %refs_0_.1), channel_id=1, source_target_pairs={{0,8},{1,9},{2,10},{3,11},{4,12},{5,13},{6,14},{7,15},{8,0},{9,1},... | collective-permute-start | bytes 393224 | tf_op jit(solution)/shard_map/ppermute | solution.py:535
  4.2 0.7 copy-start.3
  9.1 4.7 %collective-permute-start.3 = (f32[2,128,128]{2,1,0:T(8,128)S(1)}, f32[2,128,128]{2,1,0:T(8,128)S(1)}, u32[]{:S(2)}, u32[]{:S(2)}) collective-permute-start(f32[2,128,128]{2,1,0:T(8,128)S(1)} %collective-permute-done.2.refs_2_), channel_id=1, source_target_pairs={{0,4},{1,5},{2,6},{3,7},{4,0},{5,1},{6,2},{7,3},{8,12},{9,13},{10,... | collective-permute-start | bytes 393224 | tf_op jit(solution)/shard_map/ppermute | solution.py:535
  10.0 10.2 %collective-permute-start.6 = (f32[2,128,128]{2,1,0:T(8,128)S(1)}, f32[2,128,128]{2,1,0:T(8,128)S(1)}, u32[]{:S(2)}, u32[]{:S(2)}) collective-permute-start(f32[2,128,128]{2,1,0:T(8,128)S(1)} %collective-permute-done.2.refs_2_), channel_id=1, source_target_pairs={{0,2},{1,3},{2,0},{3,1},{4,6},{5,7},{6,4},{7,5},{8,10},{9,11},{10,... | collective-permute-start | bytes 393224 | tf_op jit(solution)/shard_map/ppermute | solution.py:535
  12.1 8.2 %collective-permute-start.5 = (f32[2,128,128]{2,1,0:T(8,128)S(1)}, f32[2,128,128]{2,1,0:T(8,128)S(1)}, u32[]{:S(2)}, u32[]{:S(2)}) collective-permute-start(f32[2,128,128]{2,1,0:T(8,128)S(1)} %collective-permute-done.1.refs_1_), channel_id=1, source_target_pairs={{0,2},{1,3},{2,0},{3,1},{4,6},{5,7},{6,4},{7,5},{8,10},{9,11},{10,... | collective-permute-start | bytes 393224 | tf_op jit(solution)/shard_map/ppermute | solution.py:535
  13.7 3.2 %copy-start.2 = (f32[2,128,128]{2,1,0:T(8,128)S(1)}, f32[2,128,128]{2,1,0:T(8,128)}, u32[]{:S(2)}) copy-start(f32[2,128,128]{2,1,0:T(8,128)} %refs_0_.1) | copy-start | bytes 393220
  13.7 13.4 %copy-start.4 = (s32[1,2]{1,0:T(1,128)S(1)}, s32[1,2]{1,0:T(1,128)}, u32[]{:S(2)}) copy-start(s32[1,2]{1,0:T(1,128)} %orders_ref.3) | copy-start | bytes 28
  13.7 13.4 %copy-start.5 = (f32[3]{0:T(128)S(1)}, f32[3]{0:T(128)}, u32[]{:S(2)}) copy-start(f32[3]{0:T(128)} %weights_ref.3) | copy-start | bytes 40
  13.8 13.4 %copy-start.6 = (f32[4]{0:T(128)S(1)}, f32[4]{0:T(128)}, u32[]{:S(2)}) copy-start(f32[4]{0:T(128)} %rates_ref.3) | copy-start | bytes 52
  13.8 6.5 %collective-permute-start.7 = (f32[2,128,128]{2,1,0:T(8,128)S(1)}, f32[2,128,128]{2,1,0:T(8,128)S(1)}, u32[]{:S(2)}, u32[]{:S(2)}) collective-permute-start(f32[2,128,128]{2,1,0:T(8,128)S(1)} %collective-permute-done.3.refs_3_), channel_id=1, source_target_pairs={{0,2},{1,3},{2,0},{3,1},{4,6},{5,7},{6,4},{7,5},{8,10},{9,11},{10,... | collective-permute-start | bytes 393224 | tf_op jit(solution)/shard_map/ppermute | solution.py:535
  17.6 9.5 %collective-permute-start.4 = (f32[4,2,128,128]{3,2,1,0:T(8,128)S(1)}, f32[4,2,128,128]{3,2,1,0:T(8,128)S(1)}, u32[]{:S(2)}, u32[]{:S(2)}) collective-permute-start(f32[4,2,128,128]{3,2,1,0:T(8,128)S(1)} %stack_tiles.2.t0), channel_id=1, source_target_pairs={{0,1},{1,0},{2,3},{3,2},{4,5},{5,4},{6,7},{7,6},{8,9},{9,8},{10,11... | collective-permute-start | bytes 1572872 | tf_op jit(solution)/shard_map/ppermute | solution.py:535
  21.0 6.2 %collective-permute-start.8 = (f32[4,2,128,128]{3,2,1,0:T(8,128)S(1)}, f32[4,2,128,128]{3,2,1,0:T(8,128)S(1)}, u32[]{:S(2)}, u32[]{:S(2)}) collective-permute-start(f32[4,2,128,128]{3,2,1,0:T(8,128)S(1)} %stack_tiles.3.t2), channel_id=1, source_target_pairs={{0,1},{1,0},{2,3},{3,2},{4,5},{5,4},{6,7},{7,6},{8,9},{9,8},{10,11... | collective-permute-start | bytes 1572872 | tf_op jit(solution)/shard_map/ppermute | solution.py:535
  23.0 18.0 %collective-permute-start.10 = (f32[2,65,8,256]{3,2,1,0:T(8,128)S(1)}, f32[2,65,8,256]{3,2,1,0:T(8,128)S(1)}, u32[]{:S(2)}, u32[]{:S(2)}) collective-permute-start(f32[2,65,8,256]{3,2,1,0:T(8,128)S(1)} %get-tuple-element.37), channel_id=1, source_target_pairs={{0,1},{1,2},{2,3},{3,4},{4,5},{5,6},{6,7},{7,8},{8,9},{9,10},{10,1... | collective-permute-start | bytes 3194888 | tf_op jit(solution)/shard_map/ppermute | solution.py:531
  35.8 19.6 %collective-permute-start.9 = (f32[2,64,8,256]{3,2,1,0:T(8,128)S(1)}, f32[2,64,8,256]{3,2,1,0:T(8,128)S(1)}, u32[]{:S(2)}, u32[]{:S(2)}) collective-permute-start(f32[2,64,8,256]{3,2,1,0:T(8,128)S(1)} %get-tuple-element.33), channel_id=1, source_target_pairs={{0,1},{1,2},{2,3},{3,4},{4,5},{5,6},{6,7},{7,8},{8,9},{9,10},{10,1... | collective-permute-start | bytes 3145736 | tf_op jit(solution)/shard_map/ppermute | solution.py:531
  40.9 14.4 %copy-start.7 = (s32[1,16]{1,0:T(1,128)S(1)}, s32[1,16]{1,0:T(1,128)}, u32[]{:S(2)}) copy-start(s32[1,16]{1,0:T(1,128)} %owners_ref.1) | copy-start | bytes 196
  41.0 14.4 %copy-start.8 = (s32[1,16]{1,0:T(1,128)S(1)}, s32[1,16]{1,0:T(1,128)}, u32[]{:S(2)}) copy-start(s32[1,16]{1,0:T(1,128)} %slots_ref.1) | copy-start | bytes 196
  61.4 53.1 %all-to-all-start = ((f32[16,264,128]{2,1,0:T(8,128)}), f32[16,264,128]{2,1,0:T(8,128)}, u32[]{:S(2)}, u32[]{:S(2)}) async-start(f32[16,264,128]{2,1,0:T(8,128)} %get-tuple-element.40), calls=%async_computation | async-start | bytes 4325376 | tf_op jit(solution)/shard_map/all_to_all | solution.py:670
  65.8 1.2 %copy-start.1 = (f32[2,64,8,256]{3,2,1,0:T(8,128)S(1)}, f32[2,64,8,256]{3,2,1,0:T(8,128)}, u32[]{:S(2)}) copy-start(f32[2,64,8,256]{3,2,1,0:T(8,128)} %get-tuple-element.41.source_ref) | copy-start | bytes 3145732
